TPU v7x, 128 devices: a whole 4x4x4 slice. The times are simulated.
128 devices in a mesh: seq: 16 (over x, z), head: 8 (over y, core).
Axes of the slice: x: 4, y: 4, z: 4, core: 2. Of those that a mesh axis runs over, the one named last changes fastest.
Arguments:
- query: bfloat16 [4096, 73728], P('seq', 'head'), may hold values from -390 to 390
- latent_blocks: bfloat16 [2048, 36864], P('seq'), may hold values from -6 to 6
- index_keys: bfloat16 [2048, 8192], P('seq'), may hold values from -6 to 6
- index_query: bfloat16 [4096, 8192], P(('seq', 'head')), may hold values from -14 to 14
- index_weight: float32 [4096, 64], P(('seq', 'head')), may hold values from 0.1 to 1
- block_list: int32 [32, 32], P('seq'), may hold values from 0 to 2047, as said below
- list_len: int32 [32], P('seq'), may hold values from 8 to 32
- group_start: int32 [32], P('seq'), may hold values from 384 to 130944, as said below
Outputs:
- context: bfloat16 [4096, 65536], P('seq', 'head')
- row_loss: float32 [4096], P(('seq', 'head'))
- index_grad: float32 [4096, 8192], P(('seq', 'head'))
Inputs may be any that keep to these rules, and one draw needn't show every extreme that they name: Group c belongs to the queries of seq index c // 2: its rows lie in blocks of that index's range of 128 blocks. group_start is a multiple of 64. `block_list`: the first list_len[c] entries of row c are distinct blocks that end no later than the group; entries past list_len[c] are padding. Exactly 8 used entries lie in the group's own seq index's range, the group's last block among them; at most 8 used entries of one row lie in any one index's range, so the lists of one index's 2 groups name at most 16 blocks (repeats counted) of any one index's range.
All inputs are finite; a program needn't handle non-finite values.
Results may differ from a plain program's by a relative error of at most 0.0046.
Values may be sent and summed in bfloat16 or wider, within the bound.
No kernel may reach another device: no remote copies, remote signals or barrier semaphores. Data moves between devices by JAX's collectives and lax.ppermute only.
A program may use at most 256 MiB of HBM per device.

v0:
```python
import jax
import jax.numpy as jnp
from jax import lax
from jax.sharding import PartitionSpec as P

H = 128
LAT = 512
IH = 64
ID = 128
BLK = 64
NSEL = 32
GROUP = 128
CAPC = 8
QK = 576


SOFTMAX_SCALE = 192.0 ** (-0.5)
INDEX_SCALE = 128.0 ** (-0.5)


def group_mask(blocks, length, start, first_row, rows):
    slot = jnp.arange(NSEL * BLK, dtype=jnp.int32) // BLK
    offset = jnp.arange(NSEL * BLK, dtype=jnp.int32) % BLK
    key_pos = jnp.take(blocks, slot) * BLK + offset
    query_pos = start + first_row + jnp.arange(rows, dtype=jnp.int32)
    return (slot < length)[None, :] & (key_pos[None, :] <= query_pos[:, None])


def attend(q_rows, keys, visible):
    rows = q_rows.shape[0]
    heads = q_rows.shape[1] // QK
    q_heads = q_rows.reshape(rows, heads, QK)
    scores = (
        jnp.einsum("rhd,kd->hrk", q_heads, keys, preferred_element_type=jnp.float32) * SOFTMAX_SCALE
    )
    scores = jnp.where(visible[None], scores, -jnp.inf)
    top = jnp.max(scores, -1, keepdims=True)
    weights = jnp.exp(scores - top)
    probs = weights / jnp.sum(weights, -1, keepdims=True)
    context = jnp.einsum(
        "hrk,kd->rhd", probs.astype(jnp.bfloat16), keys[:, :LAT], preferred_element_type=jnp.float32
    )
    return (context.astype(jnp.bfloat16).reshape(rows, heads * LAT), jnp.sum(probs, 0))


def indexer_rows(index_rows, weight_rows, key_sel, target, visible):
    rows = index_rows.shape[0]
    index_heads = index_rows.reshape(rows, IH, ID)
    activity = jnp.einsum("rjd,kd->rjk", index_heads, key_sel, preferred_element_type=jnp.float32)
    logits = jnp.sum(jnp.maximum(activity, 0.0) * weight_rows[:, :, None], 1) * INDEX_SCALE
    logits = jnp.where(visible, logits, -jnp.inf)
    top = jnp.max(logits, -1, keepdims=True)
    shifted = logits - top
    log_q = shifted - jnp.log(jnp.sum(jnp.exp(shifted), -1, keepdims=True))
    prob_q = jnp.where(visible, jnp.exp(log_q), 0.0)
    live = visible & (target > 0)
    safe = jnp.where(live, target, 1.0)
    loss = jnp.sum(jnp.where(live, target * (jnp.log(safe) - log_q), 0.0), -1)
    diff = prob_q - target
    coef = jnp.where(
        activity > 0, diff[:, None, :] * weight_rows[:, :, None] * INDEX_SCALE, 0.0
    ).astype(jnp.bfloat16)
    grad = jnp.einsum("rjk,kd->rjd", coef, key_sel, preferred_element_type=jnp.float32)
    return (loss, grad.reshape(rows, IH * ID))


def body(
    query, latent_blocks, index_keys, index_query, index_weight, block_list, list_len, group_start
):
    seq_count = lax.axis_size("seq")
    head_count = lax.axis_size("head")
    head_pos = lax.axis_index("head")
    blk_local = latent_blocks.shape[0]
    groups = block_list.shape[0]
    capacity = groups * CAPC
    flat = block_list.reshape(-1)
    wanted = (jnp.arange(NSEL, dtype=jnp.int32)[None, :] < list_len[:, None]).reshape(-1)
    owner = flat // blk_local
    onehot = (
        (owner[:, None] == jnp.arange(seq_count, dtype=jnp.int32)[None, :]) & wanted[:, None]
    ).astype(jnp.int32)
    before = jnp.cumsum(onehot, 0) - onehot
    rank = jnp.sum(before * onehot, 1)
    place = jnp.where(wanted, owner * capacity + rank, seq_count * capacity)
    request = (
        jnp.zeros((seq_count * capacity + 1,), jnp.int32).at[place].set(flat - owner * blk_local)
    )
    request = request[:-1].reshape(seq_count, capacity)
    asked = lax.all_to_all(request, "seq", split_axis=0, concat_axis=0, tiled=True)
    tiles = jnp.take(latent_blocks, asked, axis=0)
    key_tiles = jnp.take(index_keys, asked, axis=0)
    got_latent = lax.all_to_all(tiles, "seq", split_axis=0, concat_axis=0, tiled=True)
    got_keys = lax.all_to_all(key_tiles, "seq", split_axis=0, concat_axis=0, tiled=True)
    slot_index = jnp.where(wanted, owner * capacity + rank, 0)
    sel_latent = jnp.take(got_latent.reshape(seq_count * capacity, BLK * QK), slot_index, axis=0)
    sel_latent = sel_latent.reshape(groups, NSEL * BLK, QK)
    sel_keys = jnp.take(got_keys.reshape(seq_count * capacity, BLK * ID), slot_index, axis=0)
    sel_keys = sel_keys.reshape(groups, NSEL * BLK, ID)
    contexts = []
    partials = []
    for group in range(groups):
        rows = query[group * GROUP : (group + 1) * GROUP]
        visible = group_mask(block_list[group], list_len[group], group_start[group], 0, GROUP)
        context, partial_value = attend(rows, sel_latent[group], visible)
        contexts.append(context)
        partials.append(partial_value)
    context_all = jnp.concatenate(contexts, 0)
    partial_all = jnp.concatenate(partials, 0)
    share = query.shape[0] // head_count
    summed = lax.psum(partial_all, "head")
    target = lax.dynamic_slice_in_dim(summed, head_pos * share, share, 0)
    target = target / H
    piece = min(share, GROUP)
    first = head_pos * share + 0
    group_id = first // GROUP
    blocks = lax.dynamic_index_in_dim(block_list, group_id, 0, keepdims=False)
    length = lax.dynamic_index_in_dim(list_len, group_id, 0, keepdims=False)
    start = lax.dynamic_index_in_dim(group_start, group_id, 0, keepdims=False)
    key_sel = lax.dynamic_index_in_dim(sel_keys, group_id, 0, keepdims=False)
    visible = group_mask(blocks, length, start, first - group_id * GROUP, piece)
    loss, grad = indexer_rows(index_query, index_weight, key_sel, target, visible)
    return (context_all, loss, grad)


def solution(mesh):
    placed = (
        P("seq", "head"),
        P("seq", None),
        P("seq", None),
        P(("seq", "head"), None),
        P(("seq", "head"), None),
        P("seq", None),
        P("seq"),
        P("seq"),
    )
    return jax.shard_map(
        body,
        mesh=mesh,
        in_specs=placed,
        out_specs=(P("seq", "head"), P(("seq", "head")), P(("seq", "head"), None)),
        check_vma=False,
    )
```

profile of v0, /device:TPU:1, one launch (start us, length us, event | category | flops | bytes accessed | tf_op | source)
XLA Modules:
  0.0 671.0 jit_solution(5674985047775579988)
XLA Ops:
  7.2 0.9 iota_compare_fusion.1
  8.2 0.8 reshape.400
  9.0 0.8 reshape.401
  9.9 0.2 select_reduce_fusion.1
  10.2 0.8 scatter_custom_fusion
  11.0 14.6 %all_to_all.25 = s32[16,1,16]{2,1,0:T(1,128)S(1)} all-to-all(s32[16,1,16]{2,1,0:T(1,128)S(1)} %all_to_all.16), channel_id=1, replica_groups=mesh['seq'=16,'head'=8] {'seq'}, dimensions={0} | all-to-all | bytes 2048 | tf_op jit(solution)/shard_map/all_to_all | solution.py:89
  25.8 40.5 %gather_fusion = bf16[256,36864]{1,0:T(8,128)(2,1)} fusion(bf16[128,36864]{1,0:T(8,128)(2,1)} %param.11, s32[1024]{0:T(1024)S(1)} %pad_clamp_fusion.1), kind=kCustom, calls=%fused_computation | custom fusion | bytes 37749760 | tf_op jit(solution)/shard_map/jit(_take)/gather | solution.py:90
  66.3 5.2 gather_fusion.2
  71.5 4.7 broadcast_select_fusion.2
  76.2 9.1 %all-to-all-start.2 = ((bf16[16,16,8192]{2,1,0:T(8,128)(2,1)}), bf16[16,16,8192]{2,1,0:T(8,128)(2,1)}, u32[]{:S(2)}, u32[]{:S(2)}) async-start(bf16[16,16,8192]{2,1,0:T(8,128)(2,1)} %broadcast_select_fusion.2), calls=%async_computation.2 | async-start | bytes 8388608 | tf_op jit(solution)/shard_map/all_to_all | solution.py:93
  85.3 17.0 %broadcast_select_fusion = bf16[16,16,36864]{2,1,0:T(8,128)(2,1)} fusion(bf16[16,16,36864]{2,1,0:T(8,128)(2,1)} %bitcast.200, pred[16,16]{1,0:T(8,128)(4,1)S(1)} %compare_and_fusion.3), kind=kLoop, calls=%fused_computation.7 | loop fusion | flops 9437184 | bytes 37748992 | tf_op jit(solution)/shard_map/jit(_take)/select_n | solution.py:90
  102.3 34.3 %all-to-all-done.2 = bf16[16,16,8192]{2,1,0:T(8,128)(2,1)} async-done(((bf16[16,16,8192]{2,1,0:T(8,128)(2,1)}), bf16[16,16,8192]{2,1,0:T(8,128)(2,1)}, u32[]{:S(2)}, u32[]{:S(2)}) %all-to-all-start.2) | async-done | bytes 4194336 | tf_op jit(solution)/shard_map/all_to_all | solution.py:93
  136.6 5.5 all-to-all-start.1
  142.2 5.0 fusion.99
  147.2 4.3 copy.55
  151.5 4.3 copy.51
  155.8 0.1 copy.70
  156.1 0.1 broadcast_in_dim.120
  156.2 0.7 fusion.100
  157.5 0.6 iota_add_fusion.1
  158.0 0.7 iota_add_fusion.2
  158.7 0.7 fusion.46
  159.4 0.7 fusion.47
  160.1 0.7 fusion.45
  160.8 0.7 fusion.107
  161.5 0.7 fusion.106
  162.2 20.1 %fusion.42 = s32[2048]{0:T(1024)S(1)} fusion(s32[]{:T(128)} %bitcast.82, s32[]{:T(128)} %bitcast.81, s32[]{:T(128)} %bitcast.80, s32[]{:T(128)} %bitcast.79, s32[]{:T(128)} %bitcast.78, s32[]{:T(128)} %bitcast.77, s32[]{:T(128)} %bitcast.76, s32[]{:T(128)} %bitcast.75, s32[]{:T(128)} %bitcast.74, s32[]{:T(128)} %bitcast.73, s32[]{:T(128)} %bitcast.72, ...), kind=kLoop, calls=%fused_computation.75 | loop fusion | flops 169984 | bytes 8320 | tf_op jit(solution)/shard_map/add | solution.py:24
  182.3 0.7 fusion.105
  183.1 0.7 fusion.104
  183.8 20.1 %fusion.43 = s32[2048]{0:T(1024)S(1)} fusion(s32[]{:T(128)} %bitcast.41, s32[]{:T(128)} %bitcast.40, s32[]{:T(128)} %bitcast.39, s32[]{:T(128)} %bitcast.38, s32[]{:T(128)} %bitcast.37, s32[]{:T(128)} %bitcast.36, s32[]{:T(128)} %bitcast.35, s32[]{:T(128)} %bitcast.34, s32[]{:T(128)} %bitcast.33, s32[]{:T(128)} %bitcast.32, s32[]{:T(128)} %bitcast.31, ...), kind=kLoop, calls=%fused_computation.76 | loop fusion | flops 169984 | bytes 8320 | tf_op jit(solution)/shard_map/add | solution.py:24
  203.9 0.7 fusion.102
  204.6 0.7 fusion.101
  205.4 20.1 %fusion.41 = s32[2048]{0:T(1024)S(1)} fusion(s32[]{:T(128)} %bitcast.122, s32[]{:T(128)} %bitcast.121, s32[]{:T(128)} %bitcast.120, s32[]{:T(128)} %bitcast.119, s32[]{:T(128)} %bitcast.118, s32[]{:T(128)} %bitcast.117, s32[]{:T(128)} %bitcast.116, s32[]{:T(128)} %bitcast.115, s32[]{:T(128)} %bitcast.114, s32[]{:T(128)} %bitcast.113, s32[]{:T(128)} %bitcast.112, ...), kind=kLoop, calls=%fused_computation.74 | loop fusion | flops 169984 | bytes 8320 | tf_op jit(solution)/shard_map/add | solution.py:24
  225.6 1.5 compare_and_fusion
  227.1 2.2 compare_and_fusion.1
  229.3 4.9 gather_fusion.3
  234.2 0.5 gather.25
  234.7 7.6 %multiply_reduce_fusion = (f32[2048,32]{0,1:T(8,128)S(1)}, f32[2048,32,64]{0,2,1:T(8,128)}) fusion(f32[32,64]{1,0:T(8,128)S(1)} %copy-done.6, bf16[32,64,128]{2,1,0:T(8,128)(2,1)S(1)} %bitcast.202, bf16[2,2048,128]{2,1,0:T(8,128)(2,1)S(1)} %gather.25, s32[]{:T(128)S(6)} %select_n.224, pred[1,2048]{1,0:T(4,128)(4,1)S(1)} %constant_dynamic-slice_fusion), kind=kOutput, calls=%fused_computation.11 | convolution fusion | flops 1086521344 | bytes 18112516 | tf_op jit(solution)/shard_map/rjd,kd->rjk/dot_general | solution.py:49
  242.4 0.2 fusion.97
  242.6 0.3 exponential_reduce_fusion
  242.9 202.6 %all-to-all-done.1 = bf16[16,16,36864]{2,1,0:T(8,128)(2,1)} async-done(((bf16[16,16,36864]{2,1,0:T(8,128)(2,1)}), bf16[16,16,36864]{2,1,0:T(8,128)(2,1)}, u32[]{:S(2)}, u32[]{:S(2)}) %all-to-all-start.1) | async-done | bytes 18874400 | tf_op jit(solution)/shard_map/all_to_all | solution.py:92
  445.5 18.5 %gather_fusion.1 = bf16[64,36864]{1,0:T(8,128)(2,1)} fusion(bf16[256,36864]{1,0:T(8,128)(2,1)} %bitcast.5, s32[1024]{0:T(1024)S(1)} %pad_clamp_fusion), kind=kCustom, calls=%fused_computation.1 | custom fusion | bytes 9437440 | tf_op jit(solution)/shard_map/jit(_take)/gather | solution.py:95
  464.0 2.9 broadcast_select_fusion.1
  466.8 2.5 fusion.98
  469.3 5.6 squeeze.43
  474.9 12.3 %fusion.17 = f32[2048,128,16]{1,0,2:T(8,128)} fusion(bf16[128,16,576]{0,2,1:T(8,128)(2,1)} %bitcast.203, bf16[2048,576]{1,0:T(8,128)(2,1)} %squeeze.43), kind=kOutput, calls=%fused_computation.34 | convolution fusion | flops 4831838208 | bytes 21495808 | tf_op jit(solution)/shard_map/rhd,kd->hrk/dot_general | solution.py:34
  487.2 20.8 %fusion.108 = (f32[16,128]{1,0:T(8,128)S(1)}, f32[16,128,2048]{1,2,0:T(8,128)}) fusion(f32[2048,128,16]{1,0,2:T(8,128)} %fusion.17, pred[128,2048]{0,1:T(8,128)(4,1)S(1)} %compare_and_fusion), kind=kOutput, calls=%fused_computation.175 | output fusion | flops 25167872 | bytes 33824768 | tf_op jit(solution)/shard_map/sub | solution.py:38
  508.0 12.4 %fusion.24 = bf16[512,16,128]{2,0,1:T(8,128)(2,1)} fusion(f32[16,128,2048]{1,2,0:T(8,128)} %get-tuple-element.120, f32[16,128]{1,0:T(8,128)S(1)} %get-tuple-element.119, bf16[2048,576]{1,0:T(8,128)(2,1)} %squeeze.43), kind=kOutput, calls=%fused_computation.42 | convolution fusion | flops 4304404480 | bytes 20979712 | tf_op jit(solution)/shard_map/hrk,kd->rhd/dot_general | solution.py:40
  520.3 7.1 %fusion.16 = f32[128,2048]{0,1:T(8,128)S(1)} fusion(f32[16,128,2048]{1,2,0:T(8,128)} %get-tuple-element.120, f32[16,128]{1,0:T(8,128)S(1)} %get-tuple-element.119), kind=kLoop, calls=%fused_computation.30 | loop fusion | flops 8126464 | bytes 17833984 | tf_op jit(solution)/shard_map/reduce_sum | solution.py:43
  527.4 5.8 squeeze.39
  533.2 0.3 copy.61
  533.6 12.2 %fusion.19 = f32[2048,128,16]{1,0,2:T(8,128)} fusion(bf16[128,16,576]{0,2,1:T(8,128)(2,1)} %bitcast.204, bf16[2048,576]{1,0:T(8,128)(2,1)} %squeeze.39), kind=kOutput, calls=%fused_computation.36 | convolution fusion | flops 4831838208 | bytes 21495808 | tf_op jit(solution)/shard_map/rhd,kd->hrk/dot_general | solution.py:34
  545.7 21.0 %fusion.109 = (f32[16,128]{1,0:T(8,128)S(1)}, f32[16,128,2048]{1,2,0:T(8,128)}) fusion(f32[2048,128,16]{1,0,2:T(8,128)} %fusion.19, pred[128,2048]{0,1:T(8,128)(4,1)S(1)} %copy-done.5), kind=kOutput, calls=%fused_computation.176 | output fusion | flops 25167872 | bytes 33824768 | tf_op jit(solution)/shard_map/sub | solution.py:38
  566.8 7.1 %fusion.15 = f32[128,2048]{0,1:T(8,128)S(1)} fusion(f32[16,128,2048]{1,2,0:T(8,128)} %get-tuple-element.122, f32[16,128]{1,0:T(8,128)S(1)} %get-tuple-element.121), kind=kLoop, calls=%fused_computation.29 | loop fusion | flops 8126464 | bytes 17833984 | tf_op jit(solution)/shard_map/reduce_sum | solution.py:43
  573.8 0.3 copy.60
  574.2 1.5 pad_maximum_fusion.1
  575.7 12.3 %fusion.21 = bf16[512,16,128]{2,0,1:T(8,128)(2,1)} fusion(f32[16,128,2048]{1,2,0:T(8,128)} %get-tuple-element.122, f32[16,128]{1,0:T(8,128)S(1)} %get-tuple-element.121, bf16[2048,576]{1,0:T(8,128)(2,1)} %squeeze.39), kind=kOutput, calls=%fused_computation.41 | convolution fusion | flops 4304404480 | bytes 20979712 | tf_op jit(solution)/shard_map/hrk,kd->rhd/dot_general | solution.py:40
  588.0 3.0 copy.59
  591.0 4.1 copy.58
  595.2 4.0 pad_maximum_fusion
  599.2 53.8 %all-reduce.2.cloned.1.call-done = f32[256,2048]{1,0:T(8,128)} async-done(((f32[256,2048]{1,0:T(8,128)}), f32[256,2048]{1,0:T(8,128)}) %all-reduce.2.cloned.1.call-update) | async-done | bytes 2097168 | tf_op jit(solution)/shard_map/psum | solution.py:110
  652.9 1.9 select_subtract_fusion
  654.8 7.3 %fusion.12 = f32[32,64,128]{2,1,0:T(8,128)S(1)} fusion(f32[2048,32,64]{0,2,1:T(8,128)} %get-tuple-element.124, f32[32,64]{1,0:T(8,128)S(1)} %copy-done.6, f32[32,2048]{1,0:T(8,128)S(1)} %get-tuple-element.12, bf16[2,2048,128]{2,1,0:T(8,128)(2,1)S(1)} %copy-done.3, s32[]{:T(128)S(6)} %select_n.224, pred[1,2048]{1,0:T(4,128)(4,1)S(1)} %constant_dynamic-slice_fusion), kind=kOutput, calls=%fused_computation.26 | convolution fusion | flops 1094975488 | bytes 18636804 | tf_op jit(solution)/shard_map/rjk,kd->rjd/dot_general | solution.py:63
  662.1 1.6 copy.73
  (44 shorter events, 1.0 us)
Async XLA Ops:
  7.2 59.2 %copy-start = (bf16[128,8192]{1,0:T(8,128)(2,1)S(1)}, bf16[128,8192]{1,0:T(8,128)(2,1)}, u32[]{:S(2)}) copy-start(bf16[128,8192]{1,0:T(8,128)(2,1)} %param.12) | copy-start | bytes 6291460
  76.2 60.4 %all-to-all-start.2 = ((bf16[16,16,8192]{2,1,0:T(8,128)(2,1)}), bf16[16,16,8192]{2,1,0:T(8,128)(2,1)}, u32[]{:S(2)}, u32[]{:S(2)}) async-start(bf16[16,16,8192]{2,1,0:T(8,128)(2,1)} %broadcast_select_fusion.2), calls=%async_computation.2 | async-start | bytes 8388608 | tf_op jit(solution)/shard_map/all_to_all | solution.py:93
  136.6 308.9 %all-to-all-start.1 = ((bf16[16,16,36864]{2,1,0:T(8,128)(2,1)}), bf16[16,16,36864]{2,1,0:T(8,128)(2,1)}, u32[]{:S(2)}, u32[]{:S(2)}) async-start(bf16[16,16,36864]{2,1,0:T(8,128)(2,1)} %broadcast_select_fusion), calls=%async_computation.1 | async-start | bytes 37748736 | tf_op jit(solution)/shard_map/all_to_all | solution.py:92
  142.1 510.9 %all-reduce.2.cloned.1.call-start = ((), (), s32[]{:S(2)}) async-start(), calls=%async_computation.3 | async-start | bytes 4194304 | tf_op jit(solution)/shard_map/psum | solution.py:110
  142.2 13.6 %copy-start.4 = (bf16[32,8192]{1,0:T(8,128)(2,1)S(1)}, bf16[32,8192]{1,0:T(8,128)(2,1)}, u32[]{:S(2)}) copy-start(bf16[32,8192]{1,0:T(8,128)(2,1)} %param.13) | copy-start | bytes 1572868
  142.2 13.7 %copy-start.7 = (s32[2]{0:T(128)S(1)}, s32[2]{0:T(128)}, u32[]{:S(2)}) copy-start(s32[2]{0:T(128)} %param.16) | copy-start | bytes 28
  142.2 13.7 %copy-start.8 = (s32[2,32]{1,0:T(2,128)S(1)}, s32[2,32]{1,0:T(2,128)}, u32[]{:S(2)}) copy-start(s32[2,32]{1,0:T(2,128)} %param.15) | copy-start | bytes 772
  142.2 14.0 %copy-start.9 = (s32[2]{0:T(128)S(1)}, s32[2]{0:T(128)}, u32[]{:S(2)}) copy-start(s32[2]{0:T(128)} %param.17) | copy-start | bytes 28
  151.5 83.2 %copy-start.6 = (f32[32,64]{1,0:T(8,128)S(1)}, f32[32,64]{1,0:T(8,128)}, u32[]{:S(2)}) copy-start(f32[32,64]{1,0:T(8,128)} %param.14) | copy-start | bytes 24580
  234.7 7.7 %copy-start.2 = (bf16[2,2048,128]{2,1,0:T(8,128)(2,1)}, bf16[2,2048,128]{2,1,0:T(8,128)(2,1)S(1)}, u32[]{:S(2)}) copy-start(bf16[2,2048,128]{2,1,0:T(8,128)(2,1)S(1)} %gather.25) | copy-start | bytes 3145732
  533.6 12.2 %copy-start.5 = (pred[128,2048]{0,1:T(8,128)(4,1)S(1)}, pred[128,2048]{0,1:T(8,128)(4,1)}, u32[]{:S(2)}) copy-start(pred[128,2048]{0,1:T(8,128)(4,1)} %compare_and_fusion.1) | copy-start | bytes 786436
  588.0 66.8 %copy-start.3 = (bf16[2,2048,128]{2,1,0:T(8,128)(2,1)S(1)}, bf16[2,2048,128]{2,1,0:T(8,128)(2,1)}, u32[]{:S(2)}) copy-start(bf16[2,2048,128]{2,1,0:T(8,128)(2,1)} %copy-done.2) | copy-start | bytes 3145732
  654.8 8.9 %copy-start.1 = (bf16[128,8192]{1,0:T(8,128)(2,1)S(1)}, bf16[128,8192]{1,0:T(8,128)(2,1)}, u32[]{:S(2)}) copy-start(bf16[128,8192]{1,0:T(8,128)(2,1)} %param.12) | copy-start | bytes 6291460
Sparse Core Ops, SparseCore 0:
  575.9 77.0 all-reduce.1
where the time goes:
time: 683 us; the launch traced here: 671 us
  waiting for transfers between devices  291 us (43%)
  other arithmetic  157 us (23%)
  local copies, waits for them, and re-layouts  115 us (17%)
  matrix products  64.1 us (9%)
  between operations  15.5 us (2%)
  blocking collectives  14.6 us (2%)
  starting transfers between devices  14.6 us (2%)
    all_to_all x1, waiting for transfers between devices, body(): lax.all_to_all(tiles, 'seq', split_axis=0, concat_axis=0, tiled=True)  203 us
    add x3, other arithmetic, group_mask(): key_pos = jnp.take(blocks, slot) * BLK + offset  60.4 us
    psum x1, waiting for transfers between devices, body(): summed = lax.psum(partial_all, 'head')  53.8 us
    sub x2, other arithmetic, attend(): weights = jnp.exp(scores - top)  41.8 us
    gather x1, local copies, waits for them, and re-layouts, body(): tiles = jnp.take(latent_blocks, asked, axis=0)  40.5 us
    all_to_all x1, waiting for transfers between devices, body(): lax.all_to_all(key_tiles, 'seq', split_axis=0, concat_axis=0, tiled=True)  34.3 us
    dot_general x2, matrix products, attend(): jnp.einsum('hrk,kd->rhd', probs.astype(jnp.bfloat16), keys[:, :LAT], pref...  24.7 us
    dot_general x2, matrix products, attend(): jnp.einsum('rhd,kd->hrk', q_heads, keys, preferred_element_type=jnp.float32)  24.5 us
  transfers between devices with their start and end apart: 3, of which 3 were waited for; matrix products, arithmetic and copies ran while one was open for 21% of the time, Pallas kernels for 0%

commit v1 on v0

v1 whole, which is shorter than its diff:
```python
import functools
import math

import jax
import jax.numpy as jnp
from jax import lax
from jax.experimental import pallas as pl
from jax.experimental.pallas import tpu as pltpu
from jax.sharding import PartitionSpec as P

H = 128
LAT = 512
IH = 64
ID = 128
BLK = 64
NSEL = 32
GROUP = 128
CAPC = 8
QK = 576

PAIR = 2 * QK
KW = 640
SCALE = 192.0 ** -0.5
INDEX_SCALE = 128.0 ** -0.5
LOG2E = math.log2(math.e)
NEG = -1e30
OWN = CAPC * BLK
REM = NSEL - CAPC
VMEM_LIMIT = 56 * 1024 * 1024

f32 = jnp.float32
bf16 = jnp.bfloat16
i32 = jnp.int32


def params(n=1):
    return pltpu.CompilerParams(
        vmem_limit_bytes=VMEM_LIMIT, dimension_semantics=("arbitrary",) * n
    )


def smem():
    return pl.BlockSpec(memory_space=pltpu.SMEM)


def vmem():
    return pl.BlockSpec(memory_space=pltpu.VMEM)


def nt(a, b):
    return lax.dot_general(a, b, (((1,), (1,)), ((), ())), preferred_element_type=f32)


def nn(a, b):
    return jnp.dot(a, b, preferred_element_type=f32)


def plan_kernel(seqs, blk_dev, me_ref, list_ref, len_ref, req_ref, place_ref, own_ref, count):
    cap = 2 * CAPC
    me = me_ref[0]

    def clear_row(o, carry):
        count[o] = 0

        def clear(r, c):
            req_ref[o, r] = -1
            return c

        return lax.fori_loop(0, cap, clear, carry)

    lax.fori_loop(0, seqs, clear_row, 0)
    for g in range(2):

        def clear_place(r, c):
            place_ref[g * REM + r] = -1
            return c

        lax.fori_loop(0, REM, clear_place, 0)
        for r in range(CAPC):
            own_ref[g * CAPC + r] = -1

        def entry(k, carry):
            own_n, rem_n = carry
            block = list_ref[g, k]
            owner = block // blk_dev
            local = block - owner * blk_dev
            mine = owner == me

            @pl.when(mine)
            def _():
                own_ref[g * CAPC + jnp.minimum(own_n, CAPC - 1)] = local

            @pl.when(jnp.logical_not(mine))
            def _():
                rank = jnp.minimum(count[owner], cap - 1)
                count[owner] = rank + 1
                req_ref[owner, rank] = local
                place_ref[g * REM + jnp.minimum(rem_n, REM - 1)] = owner * cap + rank

            step = mine.astype(i32)
            return own_n + step, rem_n + 1 - step

        lax.fori_loop(0, len_ref[g], entry, (jnp.int32(0), jnp.int32(0)))


def plan(me, lists, lens, seqs, blk_dev):
    return pl.pallas_call(
        functools.partial(plan_kernel, seqs, blk_dev),
        out_shape=(
            jax.ShapeDtypeStruct((seqs, 2 * CAPC), i32),
            jax.ShapeDtypeStruct((2 * REM,), i32),
            jax.ShapeDtypeStruct((2 * CAPC,), i32),
        ),
        in_specs=[smem()] * 3,
        out_specs=(smem(),) * 3,
        scratch_shapes=[pltpu.SMEM((seqs,), i32)],
    )(me, lists, lens)


def send_kernel(h_ref, asked_ref, lat_ref, key_ref, lat_out, key_out):
    rows, blocks = asked_ref.shape[0], lat_ref.shape[0]
    lane = lax.broadcasted_iota(i32, (rows, blocks), 1)
    pick = (asked_ref[...] == lane).astype(f32).astype(bf16)
    lat_out[...] = nn(pick, lat_ref[...]).astype(bf16)
    key_out[...] = nn(pick, key_ref[...]).astype(bf16)


def send(h, asked, latent, keys, heads):
    rows = asked.shape[0]
    blocks = latent.shape[0]
    steps = 4
    lw = latent.shape[1] // heads // steps
    kw = keys.shape[1] // heads // steps
    return pl.pallas_call(
        send_kernel,
        out_shape=(
            jax.ShapeDtypeStruct((rows, lw * steps), bf16),
            jax.ShapeDtypeStruct((rows, kw * steps), bf16),
        ),
        grid_spec=pltpu.PrefetchScalarGridSpec(
            num_scalar_prefetch=1,
            grid=(steps,),
            in_specs=[
                pl.BlockSpec((rows, 1), lambda c, h: (0, 0)),
                pl.BlockSpec((blocks, lw), lambda c, h: (0, h[0] * steps + c)),
                pl.BlockSpec((blocks, kw), lambda c, h: (0, h[0] * steps + c)),
            ],
            out_specs=(
                pl.BlockSpec((rows, lw), lambda c, h: (0, c)),
                pl.BlockSpec((rows, kw), lambda c, h: (0, c)),
            ),
        ),
        compiler_params=params(),
    )(h, asked, latent, keys)


def picker(idx_ref, rows, width):
    row = lax.broadcasted_iota(i32, (rows, width), 0)
    lane = lax.broadcasted_iota(i32, (rows, width), 1)
    want = jnp.full((rows, width), -1, i32)
    for r in range(rows):
        want = jnp.where(row == r, idx_ref[r], want)
    return (want == lane).astype(f32).astype(bf16)


def own_kernel(idx_ref, lat_ref, key_ref, lat_out, key_out):
    pick = picker(idx_ref, 2 * CAPC, lat_ref.shape[0])
    pairs = lat_ref.shape[1] // PAIR
    got = [nn(pick, lat_ref[:, i * PAIR : (i + 1) * PAIR]) for i in range(pairs)]
    for g in range(2):
        part = [x[g * CAPC : (g + 1) * CAPC] for x in got]
        lat_out[g] = jnp.concatenate(part, 0).astype(bf16)
    got = [nn(pick, key_ref[:, t * ID : (t + 1) * ID]) for t in range(2 * pairs)]
    for g in range(2):
        for par in range(2):
            part = [x[g * CAPC : (g + 1) * CAPC] for x in got[par::2]]
            key_out[g, par] = jnp.concatenate(part, 0).astype(bf16)


def own_rows(idx, latent, keys):
    blocks = latent.shape[0]
    steps = 8
    pairs = BLK // 2 // steps
    rows = pairs * CAPC
    return pl.pallas_call(
        own_kernel,
        out_shape=(
            jax.ShapeDtypeStruct((2, OWN // 2, PAIR), bf16),
            jax.ShapeDtypeStruct((2, 2, OWN // 2, ID), bf16),
        ),
        grid=(steps,),
        in_specs=[
            smem(),
            pl.BlockSpec((blocks, pairs * PAIR), lambda c: (0, c)),
            pl.BlockSpec((blocks, 2 * pairs * ID), lambda c: (0, c)),
        ],
        out_specs=(
            pl.BlockSpec((2, rows, PAIR), lambda c: (0, c, 0)),
            pl.BlockSpec((2, 2, rows, ID), lambda c: (0, 0, c, 0)),
        ),
        compiler_params=params(),
    )(idx, latent, keys)


def pack_lat_kernel(idx_ref, lat_ref, lat_out):
    pick = picker(idx_ref, 2 * REM, lat_ref.shape[0])
    pairs = lat_ref.shape[1] // PAIR
    got = [nn(pick, lat_ref[:, i * PAIR : (i + 1) * PAIR]) for i in range(pairs)]
    for g in range(2):
        part = [x[g * REM : (g + 1) * REM] for x in got]
        lat_out[g] = jnp.concatenate(part, 0).astype(bf16)


def pack_lat(idx, lat):
    pairs = lat.shape[1] // PAIR
    return pl.pallas_call(
        pack_lat_kernel,
        out_shape=jax.ShapeDtypeStruct((2, pairs * REM, PAIR), bf16),
        in_specs=[smem(), vmem()],
        out_specs=vmem(),
        compiler_params=params(0),
    )(idx, lat)


def pack_key_kernel(idx_ref, key_ref, key_out):
    pick = picker(idx_ref, 2 * REM, key_ref.shape[0])
    heads = key_out.shape[0]
    tokens = key_ref.shape[1] // ID
    got = [nn(pick, key_ref[:, t * ID : (t + 1) * ID]) for t in range(tokens)]
    for g in range(2):
        part = [x[g * REM : (g + 1) * REM] for x in got[0::2] + got[1::2]]
        rows = jnp.concatenate(part, 0).astype(bf16)
        for d in range(heads // 2):
            key_out[g * (heads // 2) + d] = rows


def pack_key(idx, keys, heads):
    tokens = keys.shape[1] // ID
    return pl.pallas_call(
        pack_key_kernel,
        out_shape=jax.ShapeDtypeStruct((heads, tokens * REM, ID), bf16),
        in_specs=[smem(), vmem()],
        out_specs=vmem(),
        compiler_params=params(0),
    )(idx, keys)


def place_keys(x, ka, kb, at, rows):
    xf = x.astype(f32)
    lane = lax.broadcasted_iota(i32, (rows, KW), 1)
    gap = KW - QK
    even = jnp.where(lane < QK, xf[:, :KW], 0.0)
    odd = jnp.where(lane >= gap, xf[:, PAIR - KW :], 0.0)
    ka[pl.ds(at, rows), :] = even.astype(bf16)
    kb[pl.ds(at, rows), :] = pltpu.roll(even, gap, 1).astype(bf16)
    kb[pl.ds(at + rows, rows), :] = odd.astype(bf16)
    ka[pl.ds(at + rows, rows), :] = pltpu.roll(odd, QK, 1).astype(bf16)


def attend_kernel(src_ref, q_ref, own_ref, *refs):
    pieces, (bias_own, bias_rem, ctx_ref, t_ref, ka, kb, total) = refs[:8], refs[8:]
    step = pl.program_id(1)

    @pl.when(step == 0)
    def _():
        place_keys(own_ref[...], ka, kb, 0, own_ref.shape[0])
        for n, piece in enumerate(pieces):
            rows = piece.shape[0]
            at = pl.multiple_of(OWN + src_ref[n] * (2 * rows), 2 * rows)
            place_keys(piece[...], ka, kb, at, rows)
        total[...] = jnp.zeros_like(total)

    q = q_ref[...]
    pairs = q.shape[1] // PAIR
    own_b = jnp.concatenate([bias_own[...]] * pairs, 0)
    rem_b = bias_rem[...]
    for par, keys in ((0, ka), (1, kb)):
        first = [n * PAIR + par * (PAIR - KW) for n in range(pairs)]
        rows = jnp.concatenate([q[:, c : c + KW] for c in first], 0)
        s = nt(rows, keys[...])
        s_own = s[:, :OWN] + own_b
        s_rem = s[:, OWN:] + rem_b
        top = jnp.maximum(
            jnp.max(s_own, -1, keepdims=True), jnp.max(s_rem, -1, keepdims=True)
        )
        s = jnp.concatenate([s_own, s_rem], 1)
        w = jnp.exp2((s - top) * (SCALE * LOG2E))
        probs = w * (1.0 / jnp.sum(w, -1, keepdims=True))
        add = probs[:GROUP]
        for n in range(1, pairs):
            add = add + probs[n * GROUP : (n + 1) * GROUP]
        total[...] += add
        out = nn(probs.astype(bf16), ka[:, :LAT]).astype(bf16)
        for n in range(pairs):
            c = (2 * n + par) * LAT
            ctx_ref[:, c : c + LAT] = out[n * GROUP : (n + 1) * GROUP]

    @pl.when(step == pl.num_programs(1) - 1)
    def _():
        t_ref[...] = total[...].astype(bf16)


def attend(src, q, own, pieces, bias_own, bias_rem):
    rows, width = q.shape
    step_heads = 4
    steps = width // (step_heads * QK)
    keys = NSEL * BLK
    piece_rows = pieces[0].shape[1]
    whole = lambda g, j: (g, 0, 0)
    return pl.pallas_call(
        attend_kernel,
        out_shape=(
            jax.ShapeDtypeStruct((rows, width // QK * LAT), bf16),
            jax.ShapeDtypeStruct((rows, keys), bf16),
        ),
        grid=(2, steps),
        in_specs=[
            smem(),
            pl.BlockSpec((GROUP, step_heads * QK), lambda g, j: (g, j)),
            pl.BlockSpec((None, OWN // 2, PAIR), whole),
        ]
        + [pl.BlockSpec((None, piece_rows, PAIR), whole)] * 8
        + [
            pl.BlockSpec((None, GROUP, OWN), whole),
            pl.BlockSpec((None, 1, keys - OWN), whole),
        ],
        out_specs=(
            pl.BlockSpec((GROUP, step_heads * LAT), lambda g, j: (g, j)),
            pl.BlockSpec((GROUP, keys), lambda g, j: (g, 0)),
        ),
        scratch_shapes=[
            pltpu.VMEM((keys, KW), bf16),
            pltpu.VMEM((keys, KW), bf16),
            pltpu.VMEM((GROUP, keys), f32),
        ],
        compiler_params=params(2),
    )(src, q, own, *pieces, bias_own, bias_rem)


JB = 8


def index_part(iq, keys, b):
    cols = [iq[:, (b * JB + n) * ID : (b * JB + n + 1) * ID] for n in range(JB)]
    return nt(jnp.concatenate(cols, 0), keys)


def logits_kernel(iq_ref, w_ref, own_ref, rem_ref, bias_own, bias_rem, out_ref, keys):
    keys[:OWN] = own_ref[...]
    keys[OWN:] = rem_ref[...]
    rows = iq_ref.shape[0]
    sum_ = jnp.zeros(out_ref.shape, f32)
    for b in range(IH // JB):
        act = index_part(iq_ref, keys[...], b)
        for n in range(JB):
            j = b * JB + n
            sum_ = sum_ + jnp.maximum(act[n * rows : (n + 1) * rows], 0.0) * w_ref[:, j : j + 1]
    logits = sum_ * INDEX_SCALE
    logits = jnp.concatenate(
        [logits[:, :OWN] + bias_own[...], logits[:, OWN:] + bias_rem[...]], 1
    )
    top = jnp.max(logits, -1, keepdims=True)
    shifted = logits - top
    out_ref[...] = shifted - jnp.log(jnp.sum(jnp.exp(shifted), -1, keepdims=True))


def index_specs(rows, heads):
    group = lambda c, h: (h[0] // (heads // 2), 0, 0)
    return group, [
        pl.BlockSpec((rows, IH * ID), lambda c, h: (0, 0)),
        pl.BlockSpec((rows, IH), lambda c, h: (0, 0)),
        pl.BlockSpec((None, OWN, ID), group),
        pl.BlockSpec((NSEL * BLK - OWN, ID), lambda c, h: (0, 0)),
    ]


def index_logits(h, iq, w, own, rem, bias_own, bias_rem, heads):
    rows = iq.shape[0]
    group, specs = index_specs(rows, heads)
    keys = NSEL * BLK

    def kernel(h_ref, *refs):
        logits_kernel(*refs)

    return pl.pallas_call(
        kernel,
        out_shape=jax.ShapeDtypeStruct((rows, keys), f32),
        grid_spec=pltpu.PrefetchScalarGridSpec(
            num_scalar_prefetch=1,
            grid=(1,),
            in_specs=specs
            + [
                pl.BlockSpec((None, rows, OWN), lambda c, h: (h[0], 0, 0)),
                pl.BlockSpec((None, 1, keys - OWN), group),
            ],
            out_specs=pl.BlockSpec((rows, keys), lambda c, h: (0, 0)),
            scratch_shapes=[pltpu.VMEM((keys, ID), bf16)],
        ),
        compiler_params=params(),
    )(h, iq, w, own, rem, bias_own, bias_rem)


def grad_kernel(iq_ref, w_ref, own_ref, rem_ref, logq_ref, part_ref, loss_ref, grad_ref, keys):
    keys[:OWN] = own_ref[...]
    keys[OWN:] = rem_ref[...]
    rows = iq_ref.shape[0]
    target = part_ref[0].astype(f32)
    for n in range(1, part_ref.shape[0]):
        target = target + part_ref[n].astype(f32)
    target = target / H
    log_q = logq_ref[...]
    shown = log_q > 0.5 * NEG
    prob_q = jnp.where(shown, jnp.exp(log_q), 0.0)
    live = shown & (target > 0)
    safe = jnp.where(live, target, 1.0)
    terms = jnp.where(live, target * (jnp.log(safe) - log_q), 0.0)
    loss_ref[...] = jnp.sum(terms, -1, keepdims=True)
    diff = prob_q - target
    for b in range(IH // JB):
        act = index_part(iq_ref, keys[...], b)
        coef = []
        for n in range(JB):
            j = b * JB + n
            value = diff * (w_ref[:, j : j + 1] * INDEX_SCALE)
            coef.append(jnp.where(act[n * rows : (n + 1) * rows] > 0, value, 0.0))
        got = nn(jnp.concatenate(coef, 0).astype(bf16), keys[...])
        for n in range(JB):
            j = b * JB + n
            grad_ref[:, j * ID : (j + 1) * ID] = got[n * rows : (n + 1) * rows]


def index_grads(h, iq, w, own, rem, log_q, parts, heads):
    rows = iq.shape[0]
    group, specs = index_specs(rows, heads)
    keys = NSEL * BLK

    def kernel(h_ref, *refs):
        grad_kernel(*refs)

    return pl.pallas_call(
        kernel,
        out_shape=(
            jax.ShapeDtypeStruct((rows, 1), f32),
            jax.ShapeDtypeStruct((rows, IH * ID), f32),
        ),
        grid_spec=pltpu.PrefetchScalarGridSpec(
            num_scalar_prefetch=1,
            grid=(1,),
            in_specs=specs
            + [
                pl.BlockSpec((rows, keys), lambda c, h: (0, 0)),
                pl.BlockSpec((heads, rows, keys), lambda c, h: (0, 0, 0)),
            ],
            out_specs=(
                pl.BlockSpec((rows, 1), lambda c, h: (0, 0)),
                pl.BlockSpec((rows, IH * ID), lambda c, h: (0, 0)),
            ),
            scratch_shapes=[pltpu.VMEM((keys, ID), bf16)],
        ),
        compiler_params=params(),
    )(h, iq, w, own, rem, log_q, parts)


def gather_head(x, heads):
    ring = [x]
    for d in (2, heads - 2, 4):
        ring.append(lax.ppermute(x, "head", [(i, (i + d) % heads) for i in range(heads)]))
    other = [lax.ppermute(r, "head", [(i, i ^ 1) for i in range(heads)]) for r in ring]
    h = lax.axis_index("head")
    back = jnp.array([0, 2, heads - 2, 4], i32)
    at = jnp.concatenate([h - back + heads, (h ^ 1) - back + heads]) % heads
    return ring + other, at


def body(query, latent, index_keys, index_query, index_weight, block_list, list_len, start):
    seqs = lax.axis_size("seq")
    heads = lax.axis_size("head")
    me = lax.axis_index("seq")
    h = lax.axis_index("head")
    h1 = h.astype(i32).reshape(1)
    blk_dev = latent.shape[0]
    request, place, own_idx = plan(
        me.astype(i32).reshape(1), block_list, list_len, seqs, blk_dev
    )
    asked = lax.all_to_all(request, "seq", split_axis=0, concat_axis=0, tiled=True)
    lat_out, key_out = send(h1, asked.reshape(-1, 1), latent, index_keys, heads)
    lat_in = lax.all_to_all(lat_out, "seq", split_axis=0, concat_axis=0, tiled=True)
    key_in = lax.all_to_all(key_out, "seq", split_axis=0, concat_axis=0, tiled=True)

    own_lat, own_key = own_rows(own_idx, latent, index_keys)
    own_key = own_key.reshape(2, OWN, ID)

    col = jnp.arange(OWN, dtype=i32)
    token = (col % (OWN // 2)) // CAPC * 2 + col // (OWN // 2)
    blocks = jnp.tile(own_idx.reshape(2, CAPC), (1, OWN // CAPC)) + me * blk_dev
    key_pos = blocks * BLK + token[None, :]
    row_pos = start[:, None] + jnp.arange(GROUP, dtype=i32)[None, :]
    bias_own = jnp.where(key_pos[:, None, :] <= row_pos[:, :, None], 0.0, NEG).astype(f32)
    used = jnp.where(place.reshape(2, REM) >= 0, 0.0, NEG).astype(f32)
    bias_rem = jnp.tile(used, (1, BLK))[:, None, :]

    pieces, src = gather_head(pack_lat(place, lat_in), heads)
    rem_key = lax.all_to_all(
        pack_key(place, key_in, heads), "head", split_axis=0, concat_axis=0, tiled=True
    ).reshape(-1, ID)

    context, partial = attend(src, query, own_lat, pieces, bias_own, bias_rem)
    share = index_query.shape[0]
    parts = lax.all_to_all(
        partial.reshape(heads, share, -1), "head", split_axis=0, concat_axis=0, tiled=True
    )
    log_q = index_logits(
        h1, index_query, index_weight, own_key, rem_key,
        bias_own.reshape(heads, share, OWN), bias_rem, heads,
    )
    loss, grad = index_grads(
        h1, index_query, index_weight, own_key, rem_key, log_q, parts, heads
    )
    return context, loss.reshape(-1), grad


def solution(mesh):
    placed = (
        P("seq", "head"),
        P("seq", None),
        P("seq", None),
        P(("seq", "head"), None),
        P(("seq", "head"), None),
        P("seq", None),
        P("seq"),
        P("seq"),
    )
    return jax.shard_map(
        body,
        mesh=mesh,
        in_specs=placed,
        out_specs=(P("seq", "head"), P(("seq", "head")), P(("seq", "head"), None)),
        check_vma=False,
    )
```

time: 683 us -> 175 us (0.26); the launches traced: 671 us -> 174 us
  waiting for transfers between devices: 291 us -> 43.8 us
  other arithmetic: 157 us -> 4.6 us
  local copies, waits for them, and re-layouts: 115 us -> 6.69 us
  Pallas kernels: 0 us -> 72.2 us
  matrix products: 64.1 us -> 0 us
  starting transfers between devices: 14.6 us -> 46 us
  between operations: 15.5 us -> 0.82 us
  blocking collectives: 14.6 us -> 0 us
    all_to_all x2 -> x5, waiting for transfers between devices: 237 us -> 43.8 us  [the longest x1 28.1 us: body(): lax.all_to_all(lat_out, 'seq', split_axis=0, concat_axis=0, tiled=True)]
    gather x11 -> x0, local copies, waits for them, and re-layouts: 74 us -> none  [the longest x1 40.5 us: body(): tiles = jnp.take(latent_blocks, asked, axis=0)]
    pallas_call x0 -> x8, Pallas kernels: none -> 72.2 us  [the longest x1 38.6 us: attend(): pl.pallas_call(attend_kernel, out_shape=(jax.ShapeDtypeStruct((rows, widt...]
    dot_general x6 -> x0, matrix products: 64.1 us -> none  [the longest x2 24.7 us: attend(): jnp.einsum('hrk,kd->rhd', probs.astype(jnp.bfloat16), keys[:, :LAT], pref...]
    add x6, other arithmetic: 61.6 us -> 0.17 us  [the longest x3 0.15 us: body(): row_pos = start[:, None] + jnp.arange(GROUP, dtype=i32)[None, :]]
    psum x1 -> x0, waiting for transfers between devices: 53.8 us -> none  [body(): summed = lax.psum(partial_all, 'head')]
    sub x4 -> x0, other arithmetic: 43.6 us -> none  [the longest x2 41.8 us: attend(): weights = jnp.exp(scores - top)]
    select_n x6 -> x4, other arithmetic: 24.5 us -> 2.42 us  [the longest x2 1.81 us: body(): jnp.where(key_pos[:, None, :] <= row_pos[:, :, None], 0.0, NEG).astype(f32)]
  transfers between devices with their start and end apart: 3 -> 12, of which waited for: 3 -> 3; matrix products, arithmetic and copies ran while one was open for 21% -> 2% of each run, Pallas kernels for 0% -> 31%
where the time goes in v1:
time: 175 us; the launch traced here: 174 us
  Pallas kernels  72.2 us (41%)
  starting transfers between devices  46 us (26%)
  waiting for transfers between devices  43.8 us (25%)
  local copies, waits for them, and re-layouts  6.69 us (4%)
  other arithmetic  4.6 us (3%)
    pallas_call x1, Pallas kernels, attend(): pl.pallas_call(attend_kernel, out_shape=(jax.ShapeDtypeStruct((rows, widt...  38.6 us
    all_to_all x1, waiting for transfers between devices, body(): lax.all_to_all(lat_out, 'seq', split_axis=0, concat_axis=0, tiled=True)  28.1 us
    ppermute x4, starting transfers between devices, gather_head(): lax.ppermute(r, 'head', [(i, i ^ 1) for i in range(heads)])  14.4 us
    all_to_all x1, waiting for transfers between devices, body(): lax.all_to_all(partial.reshape(heads, share, -1), 'head', split_axis=0, c...  9.43 us
    all_to_all x1, starting transfers between devices, body(): lax.all_to_all(request, 'seq', split_axis=0, concat_axis=0, tiled=True)  9.23 us
    pallas_call x1, Pallas kernels, own_rows(): pl.pallas_call(own_kernel, out_shape=(jax.ShapeDtypeStruct((2, OWN // 2,...  8.54 us
    pallas_call x1, Pallas kernels, index_grads(): pl.pallas_call(kernel, out_shape=(jax.ShapeDtypeStruct((rows, 1), f32), j...  7.37 us
    all_to_all x1, waiting for transfers between devices, body(): lax.all_to_all(request, 'seq', split_axis=0, concat_axis=0, tiled=True)  6.33 us
  transfers between devices with their start and end apart: 12, of which 3 were waited for; matrix products, arithmetic and copies ran while one was open for 2% of the time, Pallas kernels for 31%

profile of v1, /device:TPU:1, one launch (start us, length us, event | category | flops | bytes accessed | tf_op | source)
XLA Modules:
  0.0 174.2 jit_solution(297363398592931928)
XLA Ops:
  0.6 3.8 %shard_map.112 = (s32[16,16]{1,0:T(8,128)}, s32[48]{0:T(128)}, s32[16]{0:T(128)}) custom-call(s32[1]{0:T(128)} %bitcast.me_ref, s32[2,32]{1,0:T(2,128)} %list_ref.1, s32[2]{0:T(128)} %len_ref.1), custom_call_target="tpu_custom_call" | custom-call | tf_op jit(solution)/shard_map/pallas_call | solution.py:107
  4.4 9.2 %all-to-all-start = ((s32[16,1,16]{2,1,0:T(1,128)}), s32[16,1,16]{2,1,0:T(1,128)S(1)}, u32[]{:S(2)}, u32[]{:S(2)}) async-start(s32[16,1,16]{2,1,0:T(1,128)} %bitcast.22), calls=%async_computation | async-start | bytes 16384 | tf_op jit(solution)/shard_map/all_to_all | solution.py:485
  13.7 6.3 %all-to-all-done = s32[16,1,16]{2,1,0:T(1,128)S(1)} async-done(((s32[16,1,16]{2,1,0:T(1,128)}), s32[16,1,16]{2,1,0:T(1,128)S(1)}, u32[]{:S(2)}, u32[]{:S(2)}) %all-to-all-start) | async-done | bytes 1056 | tf_op jit(solution)/shard_map/all_to_all | solution.py:485
  20.0 0.5 broadcast.183
  20.5 0.7 reduce.4
  21.2 0.8 reshape.157.asked_ref
  21.9 4.5 %shard_map.114 = (bf16[256,4608]{1,0:T(8,128)(2,1)}, bf16[256,1024]{1,0:T(8,128)(2,1)}) custom-call(s32[1]{0:T(128)} %bitcast.1.h_ref, s32[256,1]{1,0:T(8,128)} %reshape.157.asked_ref, bf16[128,36864]{1,0:T(8,128)(2,1)} %lat_ref.3, bf16[128,8192]{1,0:T(8,128)(2,1)} %key_ref.3), custom_call_target="tpu_custom_call" | custom-call | tf_op jit(solution)/shard_map/pallas_call | solution.py:134
  26.5 3.9 %all-to-all-start.1 = ((bf16[16,16,4608]{2,1,0:T(8,128)(2,1)}), bf16[16,16,4608]{2,1,0:T(8,128)(2,1)S(1)}, u32[]{:S(2)}, u32[]{:S(2)}) async-start(bf16[16,16,4608]{2,1,0:T(8,128)(2,1)} %bitcast.16), calls=%async_computation.1 | async-start | bytes 4718592 | tf_op jit(solution)/shard_map/all_to_all | solution.py:487
  30.4 0.0 copy-start.11
  30.4 0.0 copy-start.10
  30.4 0.0 copy-done.13
  30.4 0.1 iota_add_fusion
  30.5 0.0 copy-done.12
  30.5 28.1 %all-to-all-done.1 = bf16[16,16,4608]{2,1,0:T(8,128)(2,1)S(1)} async-done(((bf16[16,16,4608]{2,1,0:T(8,128)(2,1)}), bf16[16,16,4608]{2,1,0:T(8,128)(2,1)S(1)}, u32[]{:S(2)}, u32[]{:S(2)}) %all-to-all-start.1) | async-done | bytes 2359328 | tf_op jit(solution)/shard_map/all_to_all | solution.py:487
  58.5 1.4 copy-done
  59.9 2.9 %shard_map.115.refs_0_ = bf16[2,96,1152]{2,1,0:T(8,128)(2,1)} custom-call(s32[48]{0:T(128)} %get-tuple-element.16.idx_ref, bf16[256,4608]{1,0:T(8,128)(2,1)} %bitcast.13), custom_call_target="tpu_custom_call" | custom-call | tf_op jit(solution)/shard_map/pallas_call | solution.py:216
  62.8 1.3 collective-permute-start
  64.1 1.4 collective-permute-start.1
  65.6 1.6 collective-permute-start.2
  67.2 0.0 copy-done.11
  67.2 5.7 %all-to-all-start.2 = ((bf16[16,16,1024]{2,1,0:T(8,128)(2,1)}), bf16[16,16,1024]{2,1,0:T(8,128)(2,1)S(1)}, u32[]{:S(2)}, u32[]{:S(2)}) async-start(bf16[16,16,1024]{2,1,0:T(8,128)(2,1)} %bitcast.7), calls=%async_computation.2 | async-start | bytes 1048576 | tf_op jit(solution)/shard_map/all_to_all | solution.py:488
  73.0 0.1 mul.33
  73.1 0.1 mul.34
  73.2 4.6 %collective-permute-start.3 = (bf16[2,96,1152]{2,1,0:T(8,128)(2,1)}, bf16[2,96,1152]{2,1,0:T(8,128)(2,1)S(1)}, u32[]{:S(2)}, u32[]{:S(2)}) collective-permute-start(bf16[2,96,1152]{2,1,0:T(8,128)(2,1)} %shard_map.115.refs_0_), channel_id=1, source_target_pairs={{0,1},{1,0},{2,3},{3,2},{4,5},{5,4},{6,7},{7,6},{8,9},{9,8},{10,11... | collective-permute-start | bytes 1327112 | tf_op jit(solution)/shard_map/ppermute | solution.py:468
  77.7 0.0 collective-permute-done.refs_1_
  77.7 5.0 %collective-permute-start.4 = (bf16[2,96,1152]{2,1,0:T(8,128)(2,1)S(1)}, bf16[2,96,1152]{2,1,0:T(8,128)(2,1)S(1)}, u32[]{:S(2)}, u32[]{:S(2)}) collective-permute-start(bf16[2,96,1152]{2,1,0:T(8,128)(2,1)S(1)} %collective-permute-done.refs_1_), channel_id=1, source_target_pairs={{0,1},{1,0},{2,3},{3,2},{4,5},{5,4},{6,7},{7,6},{8,9},{9,8},{10,11... | collective-permute-start | bytes 1327112 | tf_op jit(solution)/shard_map/ppermute | solution.py:468
  82.8 0.0 collective-permute-done.1.refs_2_
  82.8 0.1 collective-permute-start.5
  82.9 0.0 collective-permute-done.2.refs_3_
  82.9 4.7 %collective-permute-start.6 = (bf16[2,96,1152]{2,1,0:T(8,128)(2,1)S(1)}, bf16[2,96,1152]{2,1,0:T(8,128)(2,1)}, u32[]{:S(2)}, u32[]{:S(2)}) collective-permute-start(bf16[2,96,1152]{2,1,0:T(8,128)(2,1)S(1)} %collective-permute-done.2.refs_3_), channel_id=1, source_target_pairs={{0,1},{1,0},{2,3},{3,2},{4,5},{5,4},{6,7},{7,6},{8,9},{9,8},{10,11... | collective-permute-start | bytes 1327112 | tf_op jit(solution)/shard_map/ppermute | solution.py:468
  87.6 0.0 copy-done.10
  87.6 8.5 %shard_map.113 = (bf16[2,256,1152]{2,1,0:T(8,128)(2,1)}, bf16[2,2,256,128]{3,2,1,0:T(8,128)(2,1)}) custom-call(s32[16]{0:T(128)} %get-tuple-element.14.idx_ref, bf16[128,36864]{1,0:T(8,128)(2,1)} %lat_ref.3, bf16[128,8192]{1,0:T(8,128)(2,1)} %key_ref.3), custom_call_target="tpu_custom_call" | custom-call | tf_op jit(solution)/shard_map/pallas_call | solution.py:185
  96.2 0.0 copy-done.4
  96.2 0.0 copy-done.6
  96.2 0.1 select_n.56
  96.3 0.7 tile.17.refs_9_.refs_5_
  97.0 0.0 all-to-all-done.2
  97.0 0.8 copy-done.3
  97.8 2.0 %shard_map.117 = bf16[8,192,128]{2,1,0:T(8,128)(2,1)} custom-call(s32[48]{0:T(128)} %get-tuple-element.16.idx_ref, bf16[256,1024]{1,0:T(8,128)(2,1)} %bitcast.17), custom_call_target="tpu_custom_call" | custom-call | tf_op jit(solution)/shard_map/pallas_call | solution.py:239
  99.8 3.5 %all-to-all-start.3 = ((bf16[8,192,128]{2,1,0:T(8,128)(2,1)}), bf16[8,192,128]{2,1,0:T(8,128)(2,1)S(1)}, u32[]{:S(2)}, u32[]{:S(2)}) async-start(bf16[8,192,128]{2,1,0:T(8,128)(2,1)} %shard_map.117), calls=%async_computation.3 | async-start | bytes 786432 | tf_op jit(solution)/shard_map/all_to_all | solution.py:503
  103.3 0.6 and_select_fusion.src_ref
  103.9 0.9 compare_select_fusion.1.refs_8_
  104.8 0.0 collective-permute-done.3.refs_4_
  104.8 0.0 collective-permute-done.4.refs_5_
  104.8 0.0 collective-permute-done.5.refs_6_
  104.8 0.0 copy-start.9
  104.8 0.0 collective-permute-done.6.refs_7_
  104.9 0.7 copy-done.7
  105.6 0.1 copy-done.8
  105.7 0.2 copy-done.9
  105.9 38.6 %shard_map.116 = (bf16[256,8192]{1,0:T(8,128)(2,1)}, bf16[256,2048]{1,0:T(8,128)(2,1)}) custom-call(s32[8]{0:T(128)} %and_select_fusion.src_ref, bf16[256,9216]{1,0:T(8,128)(2,1)} %q_ref.1, bf16[2,256,1152]{2,1,0:T(8,128)(2,1)} %get-tuple-element.15.own_ref, bf16[2,96,1152]{2,1,0:T(8,128)(2,1)} %shard_map.115.refs_0_, bf16[2,96,1152]{2,1,0:T(8,128)(2,1)} %copy-done.4, ...), custom_call_target="tpu_custom_call" | custom-call | tf_op jit(solution)/shard_map/pallas_call | solution.py:310
  144.5 0.0 all-to-all-done.3
  144.5 0.0 copy-start.2
  144.5 4.8 %all-to-all-start.4 = ((bf16[8,32,2048]{2,1,0:T(8,128)(2,1)}), bf16[8,32,2048]{2,1,0:T(8,128)(2,1)S(1)}, u32[]{:S(2)}, u32[]{:S(2)}) async-start(bf16[8,32,2048]{2,1,0:T(8,128)(2,1)} %bitcast.18), calls=%async_computation.4 | async-start | bytes 2097152 | tf_op jit(solution)/shard_map/all_to_all | solution.py:509
  149.4 0.1 add.117
  149.4 0.1 add.118
  149.5 0.1 broadcast_add_fusion
  149.6 0.9 compare_select_fusion.refs_4_
  150.5 0.0 copy-done.2
  150.5 4.5 %shard_map.118.refs_4_ = f32[32,2048]{1,0:T(8,128)} custom-call(s32[1]{0:T(128)} %bitcast.1.h_ref, bf16[32,8192]{1,0:T(8,128)(2,1)} %refs_0_.3, f32[32,64]{1,0:T(8,128)} %refs_1_.3, bf16[2,512,128]{2,1,0:T(8,128)(2,1)} %bitcast.19, bf16[1536,128]{1,0:T(8,128)(2,1)} %bitcast.14, f32[8,32,512]{2,1,0:T(8,128)} %compare_select_fusion.refs_4_, ...), custom_call_target="tpu_custom_call" | custom-call | tf_op jit(solution)/shard_map/pallas_call | solution.py:385
  155.0 9.4 %all-to-all-done.4.refs_5_ = bf16[8,32,2048]{2,1,0:T(8,128)(2,1)S(1)} async-done(((bf16[8,32,2048]{2,1,0:T(8,128)(2,1)}), bf16[8,32,2048]{2,1,0:T(8,128)(2,1)S(1)}, u32[]{:S(2)}, u32[]{:S(2)}) %all-to-all-start.4) | async-done | bytes 1048608 | tf_op jit(solution)/shard_map/all_to_all | solution.py:509
  164.5 1.0 copy-done.1
  165.4 7.4 %shard_map.119 = (f32[32,1]{1,0:T(8,128)}, f32[32,8192]{1,0:T(8,128)}) custom-call(s32[1]{0:T(128)} %bitcast.1.h_ref, bf16[32,8192]{1,0:T(8,128)(2,1)} %refs_0_.3, f32[32,64]{1,0:T(8,128)} %refs_1_.3, bf16[2,512,128]{2,1,0:T(8,128)(2,1)} %bitcast.20, bf16[1536,128]{1,0:T(8,128)(2,1)} %bitcast.15, f32[32,2048]{1,0:T(8,128)} %shard_map.118.refs_4_, ...), custom_call_target="tpu_custom_call" | custom-call | tf_op jit(solution)/shard_map/pallas_call | solution.py:440
  172.8 1.3 reduce.1
  (22 shorter events, 0.1 us)
Async XLA Ops:
  4.4 15.6 %all-to-all-start = ((s32[16,1,16]{2,1,0:T(1,128)}), s32[16,1,16]{2,1,0:T(1,128)S(1)}, u32[]{:S(2)}, u32[]{:S(2)}) async-start(s32[16,1,16]{2,1,0:T(1,128)} %bitcast.22), calls=%async_computation | async-start | bytes 16384 | tf_op jit(solution)/shard_map/all_to_all | solution.py:485
  26.5 3.9 %copy-start.13 = (s32[2]{0:T(128)S(1)}, s32[2]{0:T(128)}, u32[]{:S(2)}) copy-start(s32[2]{0:T(128)} %param.16) | copy-start | bytes 28
  26.5 4.0 %copy-start.12 = (s32[4]{0:T(128)S(1)}, s32[4]{0:T(128)}, u32[]{:S(2)}) copy-start(s32[4]{0:T(128)} %constant.85) | copy-start | bytes 52
  26.5 32.0 %all-to-all-start.1 = ((bf16[16,16,4608]{2,1,0:T(8,128)(2,1)}), bf16[16,16,4608]{2,1,0:T(8,128)(2,1)S(1)}, u32[]{:S(2)}, u32[]{:S(2)}) async-start(bf16[16,16,4608]{2,1,0:T(8,128)(2,1)} %bitcast.16), calls=%async_computation.1 | async-start | bytes 4718592 | tf_op jit(solution)/shard_map/all_to_all | solution.py:487
  30.4 36.9 %copy-start.11 = (s32[16]{0:T(128)S(1)}, s32[16]{0:T(128)}, u32[]{:S(2)}) copy-start(s32[16]{0:T(128)} %get-tuple-element.14.idx_ref) | copy-start | bytes 196
  30.4 57.2 %copy-start.10 = (s32[48]{0:T(128)S(1)}, s32[48]{0:T(128)}, u32[]{:S(2)}) copy-start(s32[48]{0:T(128)} %get-tuple-element.16.idx_ref) | copy-start | bytes 580
  58.5 1.4 copy-start
  62.8 14.9 %collective-permute-start = (bf16[2,96,1152]{2,1,0:T(8,128)(2,1)}, bf16[2,96,1152]{2,1,0:T(8,128)(2,1)S(1)}, u32[]{:S(2)}, u32[]{:S(2)}) collective-permute-start(bf16[2,96,1152]{2,1,0:T(8,128)(2,1)} %shard_map.115.refs_0_), channel_id=1, source_target_pairs={{0,2},{1,3},{2,4},{3,5},{4,6},{5,7},{6,0},{7,1},{8,10},{9,11},{10,... | collective-permute-start | bytes 1327112 | tf_op jit(solution)/shard_map/ppermute | solution.py:467
  64.1 18.7 %collective-permute-start.1 = (bf16[2,96,1152]{2,1,0:T(8,128)(2,1)}, bf16[2,96,1152]{2,1,0:T(8,128)(2,1)S(1)}, u32[]{:S(2)}, u32[]{:S(2)}) collective-permute-start(bf16[2,96,1152]{2,1,0:T(8,128)(2,1)} %shard_map.115.refs_0_), channel_id=1, source_target_pairs={{0,6},{1,7},{2,0},{3,1},{4,2},{5,3},{6,4},{7,5},{8,14},{9,15},{10,... | collective-permute-start | bytes 1327112 | tf_op jit(solution)/shard_map/ppermute | solution.py:467
  65.6 17.3 %collective-permute-start.2 = (bf16[2,96,1152]{2,1,0:T(8,128)(2,1)}, bf16[2,96,1152]{2,1,0:T(8,128)(2,1)S(1)}, u32[]{:S(2)}, u32[]{:S(2)}) collective-permute-start(bf16[2,96,1152]{2,1,0:T(8,128)(2,1)} %shard_map.115.refs_0_), channel_id=1, source_target_pairs={{0,4},{1,5},{2,6},{3,7},{4,0},{5,1},{6,2},{7,3},{8,12},{9,13},{10,... | collective-permute-start | bytes 1327112 | tf_op jit(solution)/shard_map/ppermute | solution.py:467
  67.2 29.8 %all-to-all-start.2 = ((bf16[16,16,1024]{2,1,0:T(8,128)(2,1)}), bf16[16,16,1024]{2,1,0:T(8,128)(2,1)S(1)}, u32[]{:S(2)}, u32[]{:S(2)}) async-start(bf16[16,16,1024]{2,1,0:T(8,128)(2,1)} %bitcast.7), calls=%async_computation.2 | async-start | bytes 1048576 | tf_op jit(solution)/shard_map/all_to_all | solution.py:488
  73.2 31.6 %collective-permute-start.3 = (bf16[2,96,1152]{2,1,0:T(8,128)(2,1)}, bf16[2,96,1152]{2,1,0:T(8,128)(2,1)S(1)}, u32[]{:S(2)}, u32[]{:S(2)}) collective-permute-start(bf16[2,96,1152]{2,1,0:T(8,128)(2,1)} %shard_map.115.refs_0_), channel_id=1, source_target_pairs={{0,1},{1,0},{2,3},{3,2},{4,5},{5,4},{6,7},{7,6},{8,9},{9,8},{10,11... | collective-permute-start | bytes 1327112 | tf_op jit(solution)/shard_map/ppermute | solution.py:468
  77.7 18.4 %copy-start.4 = (bf16[2,96,1152]{2,1,0:T(8,128)(2,1)}, bf16[2,96,1152]{2,1,0:T(8,128)(2,1)S(1)}, u32[]{:S(2)}) copy-start(bf16[2,96,1152]{2,1,0:T(8,128)(2,1)S(1)} %collective-permute-done.refs_1_) | copy-start | bytes 1327108
  77.7 27.1 %collective-permute-start.4 = (bf16[2,96,1152]{2,1,0:T(8,128)(2,1)S(1)}, bf16[2,96,1152]{2,1,0:T(8,128)(2,1)S(1)}, u32[]{:S(2)}, u32[]{:S(2)}) collective-permute-start(bf16[2,96,1152]{2,1,0:T(8,128)(2,1)S(1)} %collective-permute-done.refs_1_), channel_id=1, source_target_pairs={{0,1},{1,0},{2,3},{3,2},{4,5},{5,4},{6,7},{7,6},{8,9},{9,8},{10,11... | collective-permute-start | bytes 1327112 | tf_op jit(solution)/shard_map/ppermute | solution.py:468
  82.8 13.4 %copy-start.5 = (bf16[2,96,1152]{2,1,0:T(8,128)(2,1)}, bf16[2,96,1152]{2,1,0:T(8,128)(2,1)S(1)}, u32[]{:S(2)}) copy-start(bf16[2,96,1152]{2,1,0:T(8,128)(2,1)S(1)} %collective-permute-done.1.refs_2_) | copy-start | bytes 1327108
  82.8 22.0 %collective-permute-start.5 = (bf16[2,96,1152]{2,1,0:T(8,128)(2,1)S(1)}, bf16[2,96,1152]{2,1,0:T(8,128)(2,1)S(1)}, u32[]{:S(2)}, u32[]{:S(2)}) collective-permute-start(bf16[2,96,1152]{2,1,0:T(8,128)(2,1)S(1)} %collective-permute-done.1.refs_2_), channel_id=1, source_target_pairs={{0,1},{1,0},{2,3},{3,2},{4,5},{5,4},{6,7},{7,6},{8,9},{9,8},{10,11... | collective-permute-start | bytes 1327112 | tf_op jit(solution)/shard_map/ppermute | solution.py:468
  82.9 13.3 %copy-start.6 = (bf16[2,96,1152]{2,1,0:T(8,128)(2,1)}, bf16[2,96,1152]{2,1,0:T(8,128)(2,1)S(1)}, u32[]{:S(2)}) copy-start(bf16[2,96,1152]{2,1,0:T(8,128)(2,1)S(1)} %collective-permute-done.2.refs_3_) | copy-start | bytes 1327108
  82.9 22.0 %collective-permute-start.6 = (bf16[2,96,1152]{2,1,0:T(8,128)(2,1)S(1)}, bf16[2,96,1152]{2,1,0:T(8,128)(2,1)}, u32[]{:S(2)}, u32[]{:S(2)}) collective-permute-start(bf16[2,96,1152]{2,1,0:T(8,128)(2,1)S(1)} %collective-permute-done.2.refs_3_), channel_id=1, source_target_pairs={{0,1},{1,0},{2,3},{3,2},{4,5},{5,4},{6,7},{7,6},{8,9},{9,8},{10,11... | collective-permute-start | bytes 1327112 | tf_op jit(solution)/shard_map/ppermute | solution.py:468
  97.0 0.8 copy-start.3
  99.8 44.7 %all-to-all-start.3 = ((bf16[8,192,128]{2,1,0:T(8,128)(2,1)}), bf16[8,192,128]{2,1,0:T(8,128)(2,1)S(1)}, u32[]{:S(2)}, u32[]{:S(2)}) async-start(bf16[8,192,128]{2,1,0:T(8,128)(2,1)} %shard_map.117), calls=%async_computation.3 | async-start | bytes 786432 | tf_op jit(solution)/shard_map/all_to_all | solution.py:503
  104.8 0.8 copy-start.7
  104.8 0.9 copy-start.8
  104.8 1.1 copy-start.9
  144.5 6.0 %copy-start.2 = (bf16[8,192,128]{2,1,0:T(8,128)(2,1)}, bf16[8,192,128]{2,1,0:T(8,128)(2,1)S(1)}, u32[]{:S(2)}) copy-start(bf16[8,192,128]{2,1,0:T(8,128)(2,1)S(1)} %all-to-all-done.3) | copy-start | bytes 1179652
  144.5 19.9 %all-to-all-start.4 = ((bf16[8,32,2048]{2,1,0:T(8,128)(2,1)}), bf16[8,32,2048]{2,1,0:T(8,128)(2,1)S(1)}, u32[]{:S(2)}, u32[]{:S(2)}) async-start(bf16[8,32,2048]{2,1,0:T(8,128)(2,1)} %bitcast.18), calls=%async_computation.4 | async-start | bytes 2097152 | tf_op jit(solution)/shard_map/all_to_all | solution.py:509
  164.5 1.0 copy-start.1

commit v2 on v1

--- a/solution.py
+++ b/solution.py
@@ -25,6 +25,7 @@
 LOG2E = math.log2(math.e)
 NEG = -1e30
 OWN = CAPC * BLK
+PARTS = 1
 REM = NSEL - CAPC
 VMEM_LIMIT = 56 * 1024 * 1024
 
@@ -47,6 +48,10 @@
     return pl.BlockSpec(memory_space=pltpu.VMEM)
 
 
+def far(x):
+    return pltpu.with_memory_space_constraint(x, pltpu.HBM)
+
+
 def nt(a, b):
     return lax.dot_general(a, b, (((1,), (1,)), ((), ())), preferred_element_type=f32)
 
@@ -58,26 +63,14 @@
 def plan_kernel(seqs, blk_dev, me_ref, list_ref, len_ref, req_ref, place_ref, own_ref, count):
     cap = 2 * CAPC
     me = me_ref[0]
-
-    def clear_row(o, carry):
+    req_ref[...] = jnp.full(req_ref.shape, -1, i32)
+    for o in range(seqs):
         count[o] = 0
-
-        def clear(r, c):
-            req_ref[o, r] = -1
-            return c
-
-        return lax.fori_loop(0, cap, clear, carry)
-
-    lax.fori_loop(0, seqs, clear_row, 0)
+    for n in range(2 * REM):
+        place_ref[n] = -1
+    for n in range(2 * CAPC):
+        own_ref[n] = -1
     for g in range(2):
-
-        def clear_place(r, c):
-            place_ref[g * REM + r] = -1
-            return c
-
-        lax.fori_loop(0, REM, clear_place, 0)
-        for r in range(CAPC):
-            own_ref[g * CAPC + r] = -1
 
         def entry(k, carry):
             own_n, rem_n = carry
@@ -94,8 +87,9 @@
             def _():
                 rank = jnp.minimum(count[owner], cap - 1)
                 count[owner] = rank + 1
-                req_ref[owner, rank] = local
-                place_ref[g * REM + jnp.minimum(rem_n, REM - 1)] = owner * cap + rank
+                at = owner * cap + rank
+                req_ref[pl.ds(at, 1), :] = jnp.full((1, req_ref.shape[1]), local, i32)
+                place_ref[g * REM + jnp.minimum(rem_n, REM - 1)] = at
 
             step = mine.astype(i32)
             return own_n + step, rem_n + 1 - step
@@ -107,51 +101,39 @@
     return pl.pallas_call(
         functools.partial(plan_kernel, seqs, blk_dev),
         out_shape=(
-            jax.ShapeDtypeStruct((seqs, 2 * CAPC), i32),
+            jax.ShapeDtypeStruct((seqs * 2 * CAPC, blk_dev), i32),
             jax.ShapeDtypeStruct((2 * REM,), i32),
             jax.ShapeDtypeStruct((2 * CAPC,), i32),
         ),
         in_specs=[smem()] * 3,
-        out_specs=(smem(),) * 3,
+        out_specs=(vmem(), smem(), smem()),
         scratch_shapes=[pltpu.SMEM((seqs,), i32)],
     )(me, lists, lens)
 
 
-def send_kernel(h_ref, asked_ref, lat_ref, key_ref, lat_out, key_out):
-    rows, blocks = asked_ref.shape[0], lat_ref.shape[0]
-    lane = lax.broadcasted_iota(i32, (rows, blocks), 1)
+def send_kernel(h_ref, asked_ref, x_ref, out_ref):
+    lane = lax.broadcasted_iota(i32, asked_ref.shape, 1)
     pick = (asked_ref[...] == lane).astype(f32).astype(bf16)
-    lat_out[...] = nn(pick, lat_ref[...]).astype(bf16)
-    key_out[...] = nn(pick, key_ref[...]).astype(bf16)
-
-
-def send(h, asked, latent, keys, heads):
-    rows = asked.shape[0]
-    blocks = latent.shape[0]
-    steps = 4
-    lw = latent.shape[1] // heads // steps
-    kw = keys.shape[1] // heads // steps
+    out_ref[...] = nn(pick, x_ref[...]).astype(bf16)
+
+
+def send(h, asked, x, heads, part, parts):
+    rows, blocks = asked.shape
+    width = x.shape[1] // heads // parts
     return pl.pallas_call(
         send_kernel,
-        out_shape=(
-            jax.ShapeDtypeStruct((rows, lw * steps), bf16),
-            jax.ShapeDtypeStruct((rows, kw * steps), bf16),
-        ),
+        out_shape=jax.ShapeDtypeStruct((rows, width), bf16),
         grid_spec=pltpu.PrefetchScalarGridSpec(
             num_scalar_prefetch=1,
-            grid=(steps,),
+            grid=(1,),
             in_specs=[
-                pl.BlockSpec((rows, 1), lambda c, h: (0, 0)),
-                pl.BlockSpec((blocks, lw), lambda c, h: (0, h[0] * steps + c)),
-                pl.BlockSpec((blocks, kw), lambda c, h: (0, h[0] * steps + c)),
+                pl.BlockSpec((rows, blocks), lambda c, h: (0, 0)),
+                pl.BlockSpec((blocks, width), lambda c, h: (0, h[0] * parts + part)),
             ],
-            out_specs=(
-                pl.BlockSpec((rows, lw), lambda c, h: (0, c)),
-                pl.BlockSpec((rows, kw), lambda c, h: (0, c)),
-            ),
+            out_specs=pl.BlockSpec((rows, width), lambda c, h: (0, 0)),
         ),
         compiler_params=params(),
-    )(h, asked, latent, keys)
+    )(h, asked, far(x))
 
 
 def picker(idx_ref, rows, width):
@@ -199,7 +181,7 @@
             pl.BlockSpec((2, 2, rows, ID), lambda c: (0, 0, c, 0)),
         ),
         compiler_params=params(),
-    )(idx, latent, keys)
+    )(idx, far(latent), far(keys))
 
 
 def pack_lat_kernel(idx_ref, lat_ref, lat_out):
@@ -222,13 +204,19 @@
     )(idx, lat)
 
 
+def part_pairs(tokens, c):
+    pairs = tokens // 2 // PARTS
+    return range(c * pairs, (c + 1) * pairs)
+
+
 def pack_key_kernel(idx_ref, key_ref, key_out):
     pick = picker(idx_ref, 2 * REM, key_ref.shape[0])
     heads = key_out.shape[0]
     tokens = key_ref.shape[1] // ID
     got = [nn(pick, key_ref[:, t * ID : (t + 1) * ID]) for t in range(tokens)]
     for g in range(2):
-        part = [x[g * REM : (g + 1) * REM] for x in got[0::2] + got[1::2]]
+        order = [2 * i + par for c in range(PARTS) for par in range(2) for i in part_pairs(tokens, c)]
+        part = [got[t][g * REM : (g + 1) * REM] for t in order]
         rows = jnp.concatenate(part, 0).astype(bf16)
         for d in range(heads // 2):
             key_out[g * (heads // 2) + d] = rows
@@ -257,84 +245,197 @@
     ka[pl.ds(at + rows, rows), :] = pltpu.roll(odd, QK, 1).astype(bf16)
 
 
-def attend_kernel(src_ref, q_ref, own_ref, *refs):
-    pieces, (bias_own, bias_rem, ctx_ref, t_ref, ka, kb, total) = refs[:8], refs[8:]
-    step = pl.program_id(1)
-
-    @pl.when(step == 0)
+def score(q, keys, bias, par):
+    pairs = q.shape[1] // PAIR
+    first = [n * PAIR + par * (PAIR - KW) for n in range(pairs)]
+    rows = jnp.concatenate([q[:, c : c + KW] for c in first], 0)
+    s = nt(rows, keys)
+    if bias.shape[0] > 1:
+        s = (s.reshape(pairs, *bias.shape) + bias).reshape(s.shape)
+    else:
+        s = s + bias
+    top = jnp.max(s, -1, keepdims=True)
+    w = jnp.exp2((s - top) * (SCALE * LOG2E))
+    return w, top, jnp.sum(w, -1, keepdims=True)
+
+
+def lane_rows(x):
+    eye = lax.broadcasted_iota(i32, (GROUP, GROUP), 0) == lax.broadcasted_iota(i32, (GROUP, GROUP), 1)
+    parts = [x[r : r + GROUP] for r in range(0, x.shape[0], GROUP)]
+    return jnp.concatenate(
+        [jnp.sum(jnp.where(eye, part, 0.0), 0, keepdims=True) for part in parts], 0
+    )
+
+
+def column(rows):
+    eye = lax.broadcasted_iota(i32, (GROUP, GROUP), 0) == lax.broadcasted_iota(i32, (GROUP, GROUP), 1)
+    parts = [rows[n : n + 1] for n in range(rows.shape[0])]
+    return jnp.concatenate(
+        [jnp.sum(jnp.where(eye, part, 0.0), 1, keepdims=True) for part in parts], 0
+    )
+
+
+HEAD_ROWS = 16
+
+
+def own_stage_kernel(q_ref, own_ref, bias_ref, p_ref, st_ref, v_ref, ka, kb):
+    place_keys(own_ref[...], ka, kb, 0, own_ref.shape[0])
+    v_ref[...] = ka[:, :LAT]
+    q, bias = q_ref[...], bias_ref[...]
+    n = st_ref.shape[0] // 4
+    for par, keys in ((0, ka), (1, kb)):
+        w, top, sum_ = score(q, keys[...], bias, par)
+        p_ref[par] = w.astype(bf16)
+        st_ref[par * n : (par + 1) * n] = lane_rows(top)
+        st_ref[(par + 2) * n : (par + 3) * n] = lane_rows(sum_)
+
+
+def anywhere():
+    return pl.BlockSpec(memory_space=pl.ANY)
+
+
+def group_spec(*shape):
+    return pl.BlockSpec((None, *shape), lambda g: (g, *[0] * len(shape)))
+
+
+def rows_spec(width):
+    return pl.BlockSpec((GROUP, width), lambda g: (g, 0))
+
+
+def own_stage(q, own, bias):
+    heads = q.shape[1] // QK
+    tall = heads // 2 * GROUP
+    return pl.pallas_call(
+        own_stage_kernel,
+        out_shape=(
+            jax.ShapeDtypeStruct((2, 2, tall, OWN), bf16),
+            jax.ShapeDtypeStruct((2, 2 * heads, GROUP), f32),
+            jax.ShapeDtypeStruct((2, OWN, LAT), bf16),
+        ),
+        grid=(2,),
+        in_specs=[rows_spec(q.shape[1]), group_spec(*own.shape[1:]), group_spec(GROUP, OWN)],
+        out_specs=(
+            group_spec(2, tall, OWN),
+            group_spec(2 * heads, GROUP),
+            group_spec(OWN, LAT),
+        ),
+        scratch_shapes=[pltpu.VMEM((OWN, KW), bf16)] * 2,
+        compiler_params=params(1),
+    )(far(q), own, bias)
+
+
+def rest_kernel(n, *refs):
+    src_ref, q_ref, pieces, refs = refs[0], refs[1], refs[2 : 2 + n], refs[2 + n :]
+    bias_ref, po_ref, st_ref, p_ref, f_ref, v_ref, t_ref = refs[:7]
+    ka, kb, ps, total, factors, sem = refs[7:]
+    g = pl.program_id(0)
+    for k, piece in enumerate(pieces):
+        rows = piece.shape[1]
+        at = pl.multiple_of(src_ref[k] * (2 * rows), 2 * rows)
+        place_keys(piece[g], ka, kb, at, rows)
+    v_ref[...] = ka[:, :LAT]
+    q, bias = q_ref[...], bias_ref[...]
+    n = st_ref.shape[0] // 4
+    tall = n * GROUP
+    c = SCALE * LOG2E
+
+    def out_copy(group, par):
+        return pltpu.make_async_copy(
+            ps.at[group, par], p_ref.at[group, par], sem.at[group * 2 + par]
+        )
+
+    for par, keys in ((0, ka), (1, kb)):
+        w, top, sum_ = score(q, keys[...], bias, par)
+        ps[g, par] = w.astype(bf16)
+        out_copy(g, par).start()
+        top_o = column(st_ref[par * n : (par + 1) * n])
+        sum_o = column(st_ref[(par + 2) * n : (par + 3) * n])
+        most = jnp.maximum(top_o, top)
+        fs = [jnp.exp2((x - most) * c) for x in (top_o, top)]
+        inv = 1.0 / (fs[0] * sum_o + fs[1] * sum_)
+        for k in range(2):
+            f = fs[k] * inv
+            factors[:, k : k + 1] = f
+            f_ref[(2 * k + par) * n : (2 * k + par + 1) * n] = lane_rows(f)
+        for r in range(0, GROUP, HEAD_ROWS):
+            at = 0
+            for k, x in enumerate((po_ref.at[par], ps.at[g, par])):
+                wide = x.shape[1]
+                add = total[r : r + HEAD_ROWS, at : at + wide] if par else 0.0
+                for d in range(r, tall, GROUP):
+                    f = factors[d : d + HEAD_ROWS, k : k + 1]
+                    add = add + x[d : d + HEAD_ROWS, :].astype(f32) * f
+                if par:
+                    t_ref[r : r + HEAD_ROWS, at : at + wide] = add.astype(bf16)
+                else:
+                    total[r : r + HEAD_ROWS, at : at + wide] = add
+                at += wide
+
+    @pl.when(g == 1)
     def _():
-        place_keys(own_ref[...], ka, kb, 0, own_ref.shape[0])
-        for n, piece in enumerate(pieces):
-            rows = piece.shape[0]
-            at = pl.multiple_of(OWN + src_ref[n] * (2 * rows), 2 * rows)
-            place_keys(piece[...], ka, kb, at, rows)
-        total[...] = jnp.zeros_like(total)
-
-    q = q_ref[...]
-    pairs = q.shape[1] // PAIR
-    own_b = jnp.concatenate([bias_own[...]] * pairs, 0)
-    rem_b = bias_rem[...]
-    for par, keys in ((0, ka), (1, kb)):
-        first = [n * PAIR + par * (PAIR - KW) for n in range(pairs)]
-        rows = jnp.concatenate([q[:, c : c + KW] for c in first], 0)
-        s = nt(rows, keys[...])
-        s_own = s[:, :OWN] + own_b
-        s_rem = s[:, OWN:] + rem_b
-        top = jnp.maximum(
-            jnp.max(s_own, -1, keepdims=True), jnp.max(s_rem, -1, keepdims=True)
-        )
-        s = jnp.concatenate([s_own, s_rem], 1)
-        w = jnp.exp2((s - top) * (SCALE * LOG2E))
-        probs = w * (1.0 / jnp.sum(w, -1, keepdims=True))
-        add = probs[:GROUP]
-        for n in range(1, pairs):
-            add = add + probs[n * GROUP : (n + 1) * GROUP]
-        total[...] += add
-        out = nn(probs.astype(bf16), ka[:, :LAT]).astype(bf16)
-        for n in range(pairs):
-            c = (2 * n + par) * LAT
-            ctx_ref[:, c : c + LAT] = out[n * GROUP : (n + 1) * GROUP]
-
-    @pl.when(step == pl.num_programs(1) - 1)
-    def _():
-        t_ref[...] = total[...].astype(bf16)
-
-
-def attend(src, q, own, pieces, bias_own, bias_rem):
-    rows, width = q.shape
-    step_heads = 4
-    steps = width // (step_heads * QK)
-    keys = NSEL * BLK
-    piece_rows = pieces[0].shape[1]
-    whole = lambda g, j: (g, 0, 0)
-    return pl.pallas_call(
-        attend_kernel,
+        for group in range(2):
+            for par in range(2):
+                out_copy(group, par).wait()
+
+
+def rest_stage(q, src, pieces, bias, own):
+    heads = q.shape[1] // QK
+    tall = heads // 2 * GROUP
+    keys = bias.shape[2]
+    every = NSEL * BLK
+    return pl.pallas_call(
+        functools.partial(rest_kernel, len(pieces)),
         out_shape=(
-            jax.ShapeDtypeStruct((rows, width // QK * LAT), bf16),
-            jax.ShapeDtypeStruct((rows, keys), bf16),
-        ),
-        grid=(2, steps),
-        in_specs=[
-            smem(),
-            pl.BlockSpec((GROUP, step_heads * QK), lambda g, j: (g, j)),
-            pl.BlockSpec((None, OWN // 2, PAIR), whole),
-        ]
-        + [pl.BlockSpec((None, piece_rows, PAIR), whole)] * 8
-        + [
-            pl.BlockSpec((None, GROUP, OWN), whole),
-            pl.BlockSpec((None, 1, keys - OWN), whole),
-        ],
+            jax.ShapeDtypeStruct((2, 2, tall, keys), bf16),
+            jax.ShapeDtypeStruct((2, 2 * heads, GROUP), f32),
+            jax.ShapeDtypeStruct((2, keys, LAT), bf16),
+            jax.ShapeDtypeStruct((q.shape[0], every), bf16),
+        ),
+        grid=(2,),
+        in_specs=[smem(), rows_spec(q.shape[1])]
+        + [vmem() for x in pieces]
+        + [group_spec(1, keys), group_spec(2, tall, OWN), group_spec(2 * heads, GROUP)],
         out_specs=(
-            pl.BlockSpec((GROUP, step_heads * LAT), lambda g, j: (g, j)),
-            pl.BlockSpec((GROUP, keys), lambda g, j: (g, 0)),
+            anywhere(),
+            group_spec(2 * heads, GROUP),
+            group_spec(keys, LAT),
+            rows_spec(every),
         ),
         scratch_shapes=[
             pltpu.VMEM((keys, KW), bf16),
             pltpu.VMEM((keys, KW), bf16),
-            pltpu.VMEM((GROUP, keys), f32),
+            pltpu.VMEM((2, 2, tall, keys), bf16),
+            pltpu.VMEM((GROUP, every), f32),
+            pltpu.VMEM((tall, GROUP), f32),
+            pltpu.SemaphoreType.DMA((4,)),
         ],
+        compiler_params=params(1),
+    )(src, far(q), *pieces, bias, far(own[0]), own[1])
+
+
+def context_kernel(f_ref, po_ref, pr_ref, vo_ref, vr_ref, ctx_ref):
+    par = pl.program_id(1)
+    n = f_ref.shape[0] // 4
+    fs = [column(f_ref[pl.ds(pl.multiple_of((2 * k + par) * n, n), n), :]) for k in range(2)]
+    out = nn(po_ref[...], vo_ref[...]) * fs[0] + nn(pr_ref[...], vr_ref[...]) * fs[1]
+    out = out.astype(bf16)
+    for k in range(n):
+        at = pl.multiple_of((2 * k + par) * LAT, LAT)
+        ctx_ref[:, pl.ds(at, LAT)] = out[k * GROUP : (k + 1) * GROUP]
+
+
+def contexts(f, po, pr, vo, vr):
+    heads = f.shape[1] // 2
+    part = lambda x: pl.BlockSpec((None, None, *x.shape[2:]), lambda g, par: (g, par, 0, 0))
+    group = lambda x: pl.BlockSpec((None, *x.shape[1:]), lambda g, par: (g, 0, 0))
+    return pl.pallas_call(
+        context_kernel,
+        out_shape=jax.ShapeDtypeStruct((2 * GROUP, heads * LAT), bf16),
+        grid=(2, 2),
+        in_specs=[group(f), part(po), part(pr), group(vo), group(vr)],
+        out_specs=pl.BlockSpec((GROUP, heads * LAT), lambda g, par: (g, 0)),
         compiler_params=params(2),
-    )(src, q, own, *pieces, bias_own, bias_rem)
+    )(f, far(po), far(pr), vo, vr)
 
 
 JB = 8
@@ -345,9 +446,17 @@
     return nt(jnp.concatenate(cols, 0), keys)
 
 
+def fill_index_keys(own_ref, rem_ref, keys):
+    keys[:OWN] = own_ref[...]
+    heads, parts, rows = rem_ref.shape[:3]
+    for c in range(parts):
+        for d in range(heads):
+            at = OWN + (c * heads + d) * rows
+            keys[at : at + rows] = rem_ref[d, c]
+
+
 def logits_kernel(iq_ref, w_ref, own_ref, rem_ref, bias_own, bias_rem, out_ref, keys):
-    keys[:OWN] = own_ref[...]
-    keys[OWN:] = rem_ref[...]
+    fill_index_keys(own_ref, rem_ref, keys)
     rows = iq_ref.shape[0]
     sum_ = jnp.zeros(out_ref.shape, f32)
     for b in range(IH // JB):
@@ -356,27 +465,26 @@
             j = b * JB + n
             sum_ = sum_ + jnp.maximum(act[n * rows : (n + 1) * rows], 0.0) * w_ref[:, j : j + 1]
     logits = sum_ * INDEX_SCALE
-    logits = jnp.concatenate(
-        [logits[:, :OWN] + bias_own[...], logits[:, OWN:] + bias_rem[...]], 1
-    )
+    rem = jnp.concatenate([bias_rem[...]] * PARTS, 1)
+    logits = jnp.concatenate([logits[:, :OWN] + bias_own[...], logits[:, OWN:] + rem], 1)
     top = jnp.max(logits, -1, keepdims=True)
     shifted = logits - top
     out_ref[...] = shifted - jnp.log(jnp.sum(jnp.exp(shifted), -1, keepdims=True))
 
 
-def index_specs(rows, heads):
+def index_specs(rows, heads, rem):
     group = lambda c, h: (h[0] // (heads // 2), 0, 0)
     return group, [
         pl.BlockSpec((rows, IH * ID), lambda c, h: (0, 0)),
         pl.BlockSpec((rows, IH), lambda c, h: (0, 0)),
         pl.BlockSpec((None, OWN, ID), group),
-        pl.BlockSpec((NSEL * BLK - OWN, ID), lambda c, h: (0, 0)),
+        pl.BlockSpec(rem.shape, lambda c, h: (0, 0, 0, 0)),
     ]
 
 
 def index_logits(h, iq, w, own, rem, bias_own, bias_rem, heads):
     rows = iq.shape[0]
-    group, specs = index_specs(rows, heads)
+    group, specs = index_specs(rows, heads, rem)
     keys = NSEL * BLK
 
     def kernel(h_ref, *refs):
@@ -391,7 +499,7 @@
             in_specs=specs
             + [
                 pl.BlockSpec((None, rows, OWN), lambda c, h: (h[0], 0, 0)),
-                pl.BlockSpec((None, 1, keys - OWN), group),
+                pl.BlockSpec((None, 1, bias_rem.shape[2]), group),
             ],
             out_specs=pl.BlockSpec((rows, keys), lambda c, h: (0, 0)),
             scratch_shapes=[pltpu.VMEM((keys, ID), bf16)],
@@ -401,8 +509,7 @@
 
 
 def grad_kernel(iq_ref, w_ref, own_ref, rem_ref, logq_ref, part_ref, loss_ref, grad_ref, keys):
-    keys[:OWN] = own_ref[...]
-    keys[OWN:] = rem_ref[...]
+    fill_index_keys(own_ref, rem_ref, keys)
     rows = iq_ref.shape[0]
     target = part_ref[0].astype(f32)
     for n in range(1, part_ref.shape[0]):
@@ -431,7 +538,7 @@
 
 def index_grads(h, iq, w, own, rem, log_q, parts, heads):
     rows = iq.shape[0]
-    group, specs = index_specs(rows, heads)
+    group, specs = index_specs(rows, heads, rem)
     keys = NSEL * BLK
 
     def kernel(h_ref, *refs):
@@ -472,6 +579,14 @@
     return ring + other, at
 
 
+def after(x, *first):
+    return lax.optimization_barrier((x, *first))[0]
+
+
+def swap(x, axis):
+    return lax.all_to_all(x, axis, split_axis=0, concat_axis=0, tiled=True)
+
+
 def body(query, latent, index_keys, index_query, index_weight, block_list, list_len, start):
     seqs = lax.axis_size("seq")
     heads = lax.axis_size("head")
@@ -482,12 +597,11 @@
     request, place, own_idx = plan(
         me.astype(i32).reshape(1), block_list, list_len, seqs, blk_dev
     )
-    asked = lax.all_to_all(request, "seq", split_axis=0, concat_axis=0, tiled=True)
-    lat_out, key_out = send(h1, asked.reshape(-1, 1), latent, index_keys, heads)
-    lat_in = lax.all_to_all(lat_out, "seq", split_axis=0, concat_axis=0, tiled=True)
-    key_in = lax.all_to_all(key_out, "seq", split_axis=0, concat_axis=0, tiled=True)
-
-    own_lat, own_key = own_rows(own_idx, latent, index_keys)
+    asked = swap(request, "seq")
+    out_l = send(h1, asked, latent, heads, 0, 1)
+    in_l = swap(out_l, "seq")
+    out_k = send(h1, after(asked, out_l), index_keys, heads, 0, 1)
+    own_lat, own_key = own_rows(after(own_idx, out_k), latent, index_keys)
     own_key = own_key.reshape(2, OWN, ID)
 
     col = jnp.arange(OWN, dtype=i32)
@@ -497,22 +611,24 @@
     row_pos = start[:, None] + jnp.arange(GROUP, dtype=i32)[None, :]
     bias_own = jnp.where(key_pos[:, None, :] <= row_pos[:, :, None], 0.0, NEG).astype(f32)
     used = jnp.where(place.reshape(2, REM) >= 0, 0.0, NEG).astype(f32)
-    bias_rem = jnp.tile(used, (1, BLK))[:, None, :]
-
-    pieces, src = gather_head(pack_lat(place, lat_in), heads)
-    rem_key = lax.all_to_all(
-        pack_key(place, key_in, heads), "head", split_axis=0, concat_axis=0, tiled=True
-    ).reshape(-1, ID)
-
-    context, partial = attend(src, query, own_lat, pieces, bias_own, bias_rem)
+    bias_rem = jnp.tile(used, (1, BLK // PARTS))[:, None, :]
+
+    own = own_stage(query, own_lat, bias_own)
+    in_l = after(in_l, own[0], bias_rem)
+    packed = pack_lat(place, in_l)
+    pieces, src = gather_head(packed, heads)
+    in_k = swap(after(out_k, packed), "seq")
+    packed_k = pack_key(place, in_k, heads)
+    rem_key = swap(packed_k, "head").reshape(heads, PARTS, -1, ID)
+    p_r, factors, v_r, partial = rest_stage(after(query, packed_k), src, pieces, bias_rem, own)
     share = index_query.shape[0]
-    parts = lax.all_to_all(
-        partial.reshape(heads, share, -1), "head", split_axis=0, concat_axis=0, tiled=True
-    )
+    parts = swap(partial.reshape(heads, share, -1), "head")
+    context = contexts(after(factors, partial), own[0], p_r, own[2], v_r)
     log_q = index_logits(
         h1, index_query, index_weight, own_key, rem_key,
         bias_own.reshape(heads, share, OWN), bias_rem, heads,
     )
+    parts = after(parts, context, log_q)
     loss, grad = index_grads(
         h1, index_query, index_weight, own_key, rem_key, log_q, parts, heads
     )

time: 175 us -> 154 us (0.88)
  waiting for transfers between devices: 43.8 us -> 14.9 us
  Pallas kernels: 72.2 us -> 81 us
    all_to_all x5, waiting for transfers between devices: 43.8 us -> 14.8 us  [swap(): return lax.all_to_all(x, axis, split_axis=0, concat_axis=0, tiled=True)]
    pallas_call x2 -> x5, Pallas kernels: 43.1 us -> 54 us  [the longest x1 25.7 us: rest_stage(): pl.pallas_call(functools.partial(rest_kernel, len(pieces)), out_shape=(ja...]
    pallas_call x1, Pallas kernels: 3.79 us -> 1.75 us  [plan(): pl.pallas_call(functools.partial(plan_kernel, seqs, blk_dev), out_shape=(...]
    unnamed x28 -> x30, local copies, waits for them, and re-layouts: 4.27 us -> 4.83 us
  transfers between devices with their start and end apart: 12 -> 12, of which waited for: 3 -> 2; matrix products, arithmetic and copies ran while one was open for 2% -> 2% of each run, Pallas kernels for 31% -> 43%
where the time goes in v2:
time: 154 us; the launch traced here: 153 us
  Pallas kernels  81 us (53%)
  starting transfers between devices  46.3 us (30%)
  waiting for transfers between devices  14.9 us (10%)
  local copies, waits for them, and re-layouts  6 us (4%)
  other arithmetic  3.88 us (3%)
    all_to_all x5, starting transfers between devices, swap(): return lax.all_to_all(x, axis, split_axis=0, concat_axis=0, tiled=True)  27.3 us
    pallas_call x1, Pallas kernels, rest_stage(): pl.pallas_call(functools.partial(rest_kernel, len(pieces)), out_shape=(ja...  25.7 us
    all_to_all x5, waiting for transfers between devices, swap(): return lax.all_to_all(x, axis, split_axis=0, concat_axis=0, tiled=True)  14.8 us
    ppermute x4, starting transfers between devices, gather_head(): lax.ppermute(r, 'head', [(i, i ^ 1) for i in range(heads)])  14.6 us
    pallas_call x1, Pallas kernels, contexts(): pl.pallas_call(context_kernel, out_shape=jax.ShapeDtypeStruct((2 * GROUP,...  14.5 us
    pallas_call x1, Pallas kernels, own_rows(): pl.pallas_call(own_kernel, out_shape=(jax.ShapeDtypeStruct((2, OWN // 2,...  8.5 us
    pallas_call x1, Pallas kernels, own_stage(): pl.pallas_call(own_stage_kernel, out_shape=(jax.ShapeDtypeStruct((2, 2, t...  8.15 us
    pallas_call x1, Pallas kernels, index_grads(): pl.pallas_call(kernel, out_shape=(jax.ShapeDtypeStruct((rows, 1), f32), j...  7.37 us
  transfers between devices with their start and end apart: 12, of which 2 were waited for; matrix products, arithmetic and copies ran while one was open for 2% of the time, Pallas kernels for 43%

profile of v2, /device:TPU:1, one launch (start us, length us, event | category | flops | bytes accessed | tf_op | source)
XLA Modules:
  0.0 152.9 jit_solution(11501527626283953141)
XLA Ops:
  0.6 1.7 %shard_map.112 = (s32[256,128]{1,0:T(8,128)}, s32[48]{0:T(128)}, s32[16]{0:T(128)}) custom-call(s32[1]{0:T(128)} %bitcast.me_ref, s32[2,32]{1,0:T(2,128)} %list_ref.1, s32[2]{0:T(128)} %len_ref.1), custom_call_target="tpu_custom_call" | custom-call | tf_op jit(solution)/shard_map/pallas_call | solution.py:101
  2.4 9.4 %all-to-all-start = ((s32[16,16,128]{2,1,0:T(8,128)}), s32[16,16,128]{2,1,0:T(8,128)S(1)}, u32[]{:S(2)}, u32[]{:S(2)}) async-start(s32[16,16,128]{2,1,0:T(8,128)} %bitcast.22), calls=%async_computation | async-start | bytes 262144 | tf_op jit(solution)/shard_map/all_to_all | solution.py:587
  11.8 6.9 %all-to-all-done = s32[16,16,128]{2,1,0:T(8,128)S(1)} async-done(((s32[16,16,128]{2,1,0:T(8,128)}), s32[16,16,128]{2,1,0:T(8,128)S(1)}, u32[]{:S(2)}, u32[]{:S(2)}) %all-to-all-start) | async-done | bytes 131104 | tf_op jit(solution)/shard_map/all_to_all | solution.py:587
  18.6 0.7 copy-done.4
  19.3 3.5 %shard_map.113 = bf16[256,4608]{1,0:T(8,128)(2,1)} custom-call(s32[1]{0:T(128)} %bitcast.1.h_ref, s32[256,128]{1,0:T(8,128)} %bitcast.17, bf16[128,36864]{1,0:T(8,128)(2,1)} %lat_ref.1), custom_call_target="tpu_custom_call" | custom-call | tf_op jit(solution)/shard_map/pallas_call | solution.py:123
  22.8 3.9 %all-to-all-start.1 = ((bf16[16,16,4608]{2,1,0:T(8,128)(2,1)}), bf16[16,16,4608]{2,1,0:T(8,128)(2,1)S(1)}, u32[]{:S(2)}, u32[]{:S(2)}) async-start(bf16[16,16,4608]{2,1,0:T(8,128)(2,1)} %bitcast.13), calls=%async_computation.1 | async-start | bytes 4718592 | tf_op jit(solution)/shard_map/all_to_all | solution.py:587
  26.7 0.0 copy-done.12
  26.7 0.1 mul.33
  26.8 0.1 mul.34
  26.9 0.0 copy-done.11
  26.9 0.1 select_n.56
  27.0 0.1 tile.16
  27.1 0.0 copy-done.14
  27.1 0.1 iota_add_fusion
  27.2 0.9 compare_select_fusion.1.bias_ref
  28.1 2.1 %shard_map.114 = bf16[256,1024]{1,0:T(8,128)(2,1)} custom-call(s32[1]{0:T(128)} %bitcast.1.h_ref, s32[256,128]{1,0:T(8,128)} %bitcast.18, bf16[128,8192]{1,0:T(8,128)(2,1)} %key_ref.1), custom_call_target="tpu_custom_call" | custom-call | tf_op jit(solution)/shard_map/pallas_call | solution.py:123
  30.2 8.5 %shard_map.115 = (bf16[2,256,1152]{2,1,0:T(8,128)(2,1)}, bf16[2,2,256,128]{3,2,1,0:T(8,128)(2,1)}) custom-call(s32[16]{0:T(128)} %get-tuple-element.28.idx_ref, bf16[128,36864]{1,0:T(8,128)(2,1)} %lat_ref.1, bf16[128,8192]{1,0:T(8,128)(2,1)} %key_ref.1), custom_call_target="tpu_custom_call" | custom-call | tf_op jit(solution)/shard_map/pallas_call | solution.py:167
  38.7 8.2 %shard_map.116 = (bf16[2,2,1024,512]{3,2,1,0:T(8,128)(2,1)}, f32[2,32,128]{2,1,0:T(8,128)}, bf16[2,512,512]{2,1,0:T(8,128)(2,1)}) custom-call(bf16[256,9216]{1,0:T(8,128)(2,1)} %refs_1_.2, bf16[2,256,1152]{2,1,0:T(8,128)(2,1)} %get-tuple-element.29.own_ref, f32[2,128,512]{2,1,0:T(8,128)} %compare_select_fusion.1.bias_ref), custom_call_target="tpu_custom_call" | custom-call | tf_op jit(solution)/shard_map/pallas_call | solution.py:308
  46.8 8.0 %all-to-all-done.1 = bf16[16,16,4608]{2,1,0:T(8,128)(2,1)S(1)} async-done(((bf16[16,16,4608]{2,1,0:T(8,128)(2,1)}), bf16[16,16,4608]{2,1,0:T(8,128)(2,1)S(1)}, u32[]{:S(2)}, u32[]{:S(2)}) %all-to-all-start.1) | async-done | bytes 2359328 | tf_op jit(solution)/shard_map/all_to_all | solution.py:587
  54.8 1.4 copy-done
  56.2 2.9 %shard_map.117.refs_2_ = bf16[2,96,1152]{2,1,0:T(8,128)(2,1)} custom-call(s32[48]{0:T(128)} %get-tuple-element.24.idx_ref, bf16[256,4608]{1,0:T(8,128)(2,1)} %bitcast.12), custom_call_target="tpu_custom_call" | custom-call | tf_op jit(solution)/shard_map/pallas_call | solution.py:198
  59.2 1.3 collective-permute-start
  60.5 1.4 collective-permute-start.1
  61.9 1.6 %collective-permute-start.2 = (bf16[2,96,1152]{2,1,0:T(8,128)(2,1)}, bf16[2,96,1152]{2,1,0:T(8,128)(2,1)S(1)}, u32[]{:S(2)}, u32[]{:S(2)}) collective-permute-start(bf16[2,96,1152]{2,1,0:T(8,128)(2,1)} %shard_map.117.refs_2_), channel_id=1, source_target_pairs={{0,4},{1,5},{2,6},{3,7},{4,0},{5,1},{6,2},{7,3},{8,12},{9,13},{10,... | collective-permute-start | bytes 1327112 | tf_op jit(solution)/shard_map/ppermute | solution.py:574
  63.6 5.7 %all-to-all-start.2 = ((bf16[16,16,1024]{2,1,0:T(8,128)(2,1)}), bf16[16,16,1024]{2,1,0:T(8,128)(2,1)S(1)}, u32[]{:S(2)}, u32[]{:S(2)}) async-start(bf16[16,16,1024]{2,1,0:T(8,128)(2,1)} %bitcast.6), calls=%async_computation.2 | async-start | bytes 1048576 | tf_op jit(solution)/shard_map/all_to_all | solution.py:587
  69.3 4.6 %collective-permute-start.3 = (bf16[2,96,1152]{2,1,0:T(8,128)(2,1)}, bf16[2,96,1152]{2,1,0:T(8,128)(2,1)S(1)}, u32[]{:S(2)}, u32[]{:S(2)}) collective-permute-start(bf16[2,96,1152]{2,1,0:T(8,128)(2,1)} %shard_map.117.refs_2_), channel_id=1, source_target_pairs={{0,1},{1,0},{2,3},{3,2},{4,5},{5,4},{6,7},{7,6},{8,9},{9,8},{10,11... | collective-permute-start | bytes 1327112 | tf_op jit(solution)/shard_map/ppermute | solution.py:575
  73.9 0.0 collective-permute-done.refs_3_
  74.0 5.2 %collective-permute-start.4 = (bf16[2,96,1152]{2,1,0:T(8,128)(2,1)S(1)}, bf16[2,96,1152]{2,1,0:T(8,128)(2,1)S(1)}, u32[]{:S(2)}, u32[]{:S(2)}) collective-permute-start(bf16[2,96,1152]{2,1,0:T(8,128)(2,1)S(1)} %collective-permute-done.refs_3_), channel_id=1, source_target_pairs={{0,1},{1,0},{2,3},{3,2},{4,5},{5,4},{6,7},{7,6},{8,9},{9,8},{10,11... | collective-permute-start | bytes 1327112 | tf_op jit(solution)/shard_map/ppermute | solution.py:575
  79.1 0.0 collective-permute-done.1.refs_4_
  79.1 0.1 collective-permute-start.5
  79.2 0.0 collective-permute-done.2.refs_5_
  79.2 4.7 %collective-permute-start.6 = (bf16[2,96,1152]{2,1,0:T(8,128)(2,1)S(1)}, bf16[2,96,1152]{2,1,0:T(8,128)(2,1)}, u32[]{:S(2)}, u32[]{:S(2)}) collective-permute-start(bf16[2,96,1152]{2,1,0:T(8,128)(2,1)S(1)} %collective-permute-done.2.refs_5_), channel_id=1, source_target_pairs={{0,1},{1,0},{2,3},{3,2},{4,5},{5,4},{6,7},{7,6},{8,9},{9,8},{10,11... | collective-permute-start | bytes 1327112 | tf_op jit(solution)/shard_map/ppermute | solution.py:575
  83.9 0.0 all-to-all-done.2
  84.0 0.8 copy-done.3
  84.7 2.0 %shard_map.118 = bf16[8,192,128]{2,1,0:T(8,128)(2,1)} custom-call(s32[48]{0:T(128)} %get-tuple-element.24.idx_ref, bf16[256,1024]{1,0:T(8,128)(2,1)} %bitcast.16), custom_call_target="tpu_custom_call" | custom-call | tf_op jit(solution)/shard_map/pallas_call | solution.py:227
  86.8 3.6 %all-to-all-start.3 = ((bf16[8,192,128]{2,1,0:T(8,128)(2,1)}), bf16[8,192,128]{2,1,0:T(8,128)(2,1)S(1)}, u32[]{:S(2)}, u32[]{:S(2)}) async-start(bf16[8,192,128]{2,1,0:T(8,128)(2,1)} %shard_map.118), calls=%async_computation.3 | async-start | bytes 786432 | tf_op jit(solution)/shard_map/all_to_all | solution.py:587
  90.4 0.6 copy.12.refs_10_.refs_5_
  91.0 0.0 copy-done.13
  91.0 0.6 and_select_fusion.refs_0_
  91.5 0.0 collective-permute-done.3.refs_6_
  91.5 0.0 collective-permute-done.4.refs_7_
  91.6 0.0 copy-start.9
  91.6 0.0 collective-permute-done.5.refs_8_
  91.6 0.0 collective-permute-done.6.refs_9_
  91.6 0.0 copy-done.5
  91.6 0.0 copy-done.6
  91.6 0.0 copy-done.7
  91.6 0.7 copy-done.8
  92.3 0.2 copy-done.9
  92.5 0.1 copy-done.10
  92.6 25.7 %shard_map.119 = (bf16[2,2,1024,1536]{3,2,1,0:T(8,128)(2,1)}, f32[2,32,128]{2,1,0:T(8,128)}, bf16[2,1536,512]{2,1,0:T(8,128)(2,1)}, bf16[256,2048]{1,0:T(8,128)(2,1)}) custom-call(s32[8]{0:T(128)} %and_select_fusion.refs_0_, bf16[256,9216]{1,0:T(8,128)(2,1)} %refs_1_.2, bf16[2,96,1152]{2,1,0:T(8,128)(2,1)} %shard_map.117.refs_2_, ...), custom_call_target="tpu_custom_call" | custom-call | tf_op jit(solution)/shard_map/pallas_call | solution.py:386
  118.3 0.0 all-to-all-done.3
  118.3 4.7 %all-to-all-start.4 = ((bf16[8,32,2048]{2,1,0:T(8,128)(2,1)}), bf16[8,32,2048]{2,1,0:T(8,128)(2,1)S(1)}, u32[]{:S(2)}, u32[]{:S(2)}) async-start(bf16[8,32,2048]{2,1,0:T(8,128)(2,1)} %bitcast.19), calls=%async_computation.4 | async-start | bytes 2097152 | tf_op jit(solution)/shard_map/all_to_all | solution.py:587
  123.0 0.1 add.117
  123.1 0.1 add.118
  123.2 0.1 broadcast_add_fusion
  123.3 0.9 compare_select_fusion.refs_4_
  124.2 0.0 copy-done.2
  124.2 4.5 %shard_map.121.refs_4_ = f32[32,2048]{1,0:T(8,128)} custom-call(s32[1]{0:T(128)} %bitcast.1.h_ref, bf16[32,8192]{1,0:T(8,128)(2,1)} %refs_0_.3, f32[32,64]{1,0:T(8,128)} %refs_1_.4, bf16[2,512,128]{2,1,0:T(8,128)(2,1)} %bitcast.20, bf16[8,1,192,128]{3,2,1,0:T(8,128)(2,1)} %bitcast.14, f32[8,32,512]{2,1,0:T(8,128)} %compare_select_fusion.refs_4_, ...), custom_call_target="tpu_custom_call" | custom-call | tf_op jit(solution)/shard_map/pallas_call | solution.py:493
  128.7 14.5 %shard_map.120 = bf16[256,8192]{1,0:T(8,128)(2,1)} custom-call(f32[2,32,128]{2,1,0:T(8,128)} %get-tuple-element.37.f_ref, bf16[2,2,1024,512]{3,2,1,0:T(8,128)(2,1)} %get-tuple-element.30.refs_11_.po_ref, bf16[2,2,1024,1536]{3,2,1,0:T(8,128)(2,1)} %get-tuple-element.38.pr_ref, bf16[2,512,512]{2,1,0:T(8,128)(2,1)} %get-tuple-element.39.vo_ref, ...), custom_call_target="tpu_custom_call" | custom-call | tf_op jit(solution)/shard_map/pallas_call | solution.py:431
  143.2 0.0 all-to-all-done.4.refs_5_
  143.2 1.0 copy-done.1
  144.2 7.4 %shard_map.122 = (f32[32,1]{1,0:T(8,128)}, f32[32,8192]{1,0:T(8,128)}) custom-call(s32[1]{0:T(128)} %bitcast.1.h_ref, bf16[32,8192]{1,0:T(8,128)(2,1)} %refs_0_.3, f32[32,64]{1,0:T(8,128)} %refs_1_.4, bf16[2,512,128]{2,1,0:T(8,128)(2,1)} %bitcast.21, bf16[8,1,192,128]{3,2,1,0:T(8,128)(2,1)} %bitcast.15, f32[32,2048]{1,0:T(8,128)} %shard_map.121.refs_4_, ...), custom_call_target="tpu_custom_call" | custom-call | tf_op jit(solution)/shard_map/pallas_call | solution.py:547
  151.6 1.3 reduce
  (25 shorter events, 0.1 us)
Async XLA Ops:
  2.4 16.2 %all-to-all-start = ((s32[16,16,128]{2,1,0:T(8,128)}), s32[16,16,128]{2,1,0:T(8,128)S(1)}, u32[]{:S(2)}, u32[]{:S(2)}) async-start(s32[16,16,128]{2,1,0:T(8,128)} %bitcast.22), calls=%async_computation | async-start | bytes 262144 | tf_op jit(solution)/shard_map/all_to_all | solution.py:587
  18.6 0.7 copy-start.4
  22.8 3.9 %copy-start.12 = (s32[16]{0:T(128)S(1)}, s32[16]{0:T(128)}, u32[]{:S(2)}) copy-start(s32[16]{0:T(128)} %get-tuple-element.28.idx_ref) | copy-start | bytes 196
  22.8 4.1 %copy-start.11 = (s32[48]{0:T(128)S(1)}, s32[48]{0:T(128)}, u32[]{:S(2)}) copy-start(s32[48]{0:T(128)} %get-tuple-element.24.idx_ref) | copy-start | bytes 580
  22.8 4.3 %copy-start.14 = (s32[2]{0:T(128)S(1)}, s32[2]{0:T(128)}, u32[]{:S(2)}) copy-start(s32[2]{0:T(128)} %param.16) | copy-start | bytes 28
  22.8 32.0 %all-to-all-start.1 = ((bf16[16,16,4608]{2,1,0:T(8,128)(2,1)}), bf16[16,16,4608]{2,1,0:T(8,128)(2,1)S(1)}, u32[]{:S(2)}, u32[]{:S(2)}) async-start(bf16[16,16,4608]{2,1,0:T(8,128)(2,1)} %bitcast.13), calls=%async_computation.1 | async-start | bytes 4718592 | tf_op jit(solution)/shard_map/all_to_all | solution.py:587
  46.8 44.1 %copy-start.13 = (s32[4]{0:T(128)S(1)}, s32[4]{0:T(128)}, u32[]{:S(2)}) copy-start(s32[4]{0:T(128)} %constant.85) | copy-start | bytes 52
  54.8 1.4 copy-start
  59.2 14.8 %collective-permute-start = (bf16[2,96,1152]{2,1,0:T(8,128)(2,1)}, bf16[2,96,1152]{2,1,0:T(8,128)(2,1)S(1)}, u32[]{:S(2)}, u32[]{:S(2)}) collective-permute-start(bf16[2,96,1152]{2,1,0:T(8,128)(2,1)} %shard_map.117.refs_2_), channel_id=1, source_target_pairs={{0,2},{1,3},{2,4},{3,5},{4,6},{5,7},{6,0},{7,1},{8,10},{9,11},{10,... | collective-permute-start | bytes 1327112 | tf_op jit(solution)/shard_map/ppermute | solution.py:574
  60.5 18.7 %collective-permute-start.1 = (bf16[2,96,1152]{2,1,0:T(8,128)(2,1)}, bf16[2,96,1152]{2,1,0:T(8,128)(2,1)S(1)}, u32[]{:S(2)}, u32[]{:S(2)}) collective-permute-start(bf16[2,96,1152]{2,1,0:T(8,128)(2,1)} %shard_map.117.refs_2_), channel_id=1, source_target_pairs={{0,6},{1,7},{2,0},{3,1},{4,2},{5,3},{6,4},{7,5},{8,14},{9,15},{10,... | collective-permute-start | bytes 1327112 | tf_op jit(solution)/shard_map/ppermute | solution.py:574
  61.9 17.3 %collective-permute-start.2 = (bf16[2,96,1152]{2,1,0:T(8,128)(2,1)}, bf16[2,96,1152]{2,1,0:T(8,128)(2,1)S(1)}, u32[]{:S(2)}, u32[]{:S(2)}) collective-permute-start(bf16[2,96,1152]{2,1,0:T(8,128)(2,1)} %shard_map.117.refs_2_), channel_id=1, source_target_pairs={{0,4},{1,5},{2,6},{3,7},{4,0},{5,1},{6,2},{7,3},{8,12},{9,13},{10,... | collective-permute-start | bytes 1327112 | tf_op jit(solution)/shard_map/ppermute | solution.py:574
  63.6 20.4 %all-to-all-start.2 = ((bf16[16,16,1024]{2,1,0:T(8,128)(2,1)}), bf16[16,16,1024]{2,1,0:T(8,128)(2,1)S(1)}, u32[]{:S(2)}, u32[]{:S(2)}) async-start(bf16[16,16,1024]{2,1,0:T(8,128)(2,1)} %bitcast.6), calls=%async_computation.2 | async-start | bytes 1048576 | tf_op jit(solution)/shard_map/all_to_all | solution.py:587
  69.3 22.3 %collective-permute-start.3 = (bf16[2,96,1152]{2,1,0:T(8,128)(2,1)}, bf16[2,96,1152]{2,1,0:T(8,128)(2,1)S(1)}, u32[]{:S(2)}, u32[]{:S(2)}) collective-permute-start(bf16[2,96,1152]{2,1,0:T(8,128)(2,1)} %shard_map.117.refs_2_), channel_id=1, source_target_pairs={{0,1},{1,0},{2,3},{3,2},{4,5},{5,4},{6,7},{7,6},{8,9},{9,8},{10,11... | collective-permute-start | bytes 1327112 | tf_op jit(solution)/shard_map/ppermute | solution.py:575
  73.9 17.6 %copy-start.5 = (bf16[2,96,1152]{2,1,0:T(8,128)(2,1)}, bf16[2,96,1152]{2,1,0:T(8,128)(2,1)S(1)}, u32[]{:S(2)}) copy-start(bf16[2,96,1152]{2,1,0:T(8,128)(2,1)S(1)} %collective-permute-done.refs_3_) | copy-start | bytes 1327108
  74.0 17.6 %collective-permute-start.4 = (bf16[2,96,1152]{2,1,0:T(8,128)(2,1)S(1)}, bf16[2,96,1152]{2,1,0:T(8,128)(2,1)S(1)}, u32[]{:S(2)}, u32[]{:S(2)}) collective-permute-start(bf16[2,96,1152]{2,1,0:T(8,128)(2,1)S(1)} %collective-permute-done.refs_3_), channel_id=1, source_target_pairs={{0,1},{1,0},{2,3},{3,2},{4,5},{5,4},{6,7},{7,6},{8,9},{9,8},{10,11... | collective-permute-start | bytes 1327112 | tf_op jit(solution)/shard_map/ppermute | solution.py:575
  79.1 12.5 %copy-start.6 = (bf16[2,96,1152]{2,1,0:T(8,128)(2,1)}, bf16[2,96,1152]{2,1,0:T(8,128)(2,1)S(1)}, u32[]{:S(2)}) copy-start(bf16[2,96,1152]{2,1,0:T(8,128)(2,1)S(1)} %collective-permute-done.1.refs_4_) | copy-start | bytes 1327108
  79.1 12.4 %collective-permute-start.5 = (bf16[2,96,1152]{2,1,0:T(8,128)(2,1)S(1)}, bf16[2,96,1152]{2,1,0:T(8,128)(2,1)S(1)}, u32[]{:S(2)}, u32[]{:S(2)}) collective-permute-start(bf16[2,96,1152]{2,1,0:T(8,128)(2,1)S(1)} %collective-permute-done.1.refs_4_), channel_id=1, source_target_pairs={{0,1},{1,0},{2,3},{3,2},{4,5},{5,4},{6,7},{7,6},{8,9},{9,8},{10,11... | collective-permute-start | bytes 1327112 | tf_op jit(solution)/shard_map/ppermute | solution.py:575
  79.2 12.4 %copy-start.7 = (bf16[2,96,1152]{2,1,0:T(8,128)(2,1)}, bf16[2,96,1152]{2,1,0:T(8,128)(2,1)S(1)}, u32[]{:S(2)}) copy-start(bf16[2,96,1152]{2,1,0:T(8,128)(2,1)S(1)} %collective-permute-done.2.refs_5_) | copy-start | bytes 1327108
  79.2 12.3 %collective-permute-start.6 = (bf16[2,96,1152]{2,1,0:T(8,128)(2,1)S(1)}, bf16[2,96,1152]{2,1,0:T(8,128)(2,1)}, u32[]{:S(2)}, u32[]{:S(2)}) collective-permute-start(bf16[2,96,1152]{2,1,0:T(8,128)(2,1)S(1)} %collective-permute-done.2.refs_5_), channel_id=1, source_target_pairs={{0,1},{1,0},{2,3},{3,2},{4,5},{5,4},{6,7},{7,6},{8,9},{9,8},{10,11... | collective-permute-start | bytes 1327112 | tf_op jit(solution)/shard_map/ppermute | solution.py:575
  83.9 0.8 copy-start.3
  86.8 31.5 %all-to-all-start.3 = ((bf16[8,192,128]{2,1,0:T(8,128)(2,1)}), bf16[8,192,128]{2,1,0:T(8,128)(2,1)S(1)}, u32[]{:S(2)}, u32[]{:S(2)}) async-start(bf16[8,192,128]{2,1,0:T(8,128)(2,1)} %shard_map.118), calls=%async_computation.3 | async-start | bytes 786432 | tf_op jit(solution)/shard_map/all_to_all | solution.py:587
  91.5 0.8 copy-start.8
  91.6 0.9 copy-start.9
  91.6 1.0 copy-start.10
  118.3 5.9 %copy-start.2 = (bf16[8,192,128]{2,1,0:T(8,128)(2,1)}, bf16[8,192,128]{2,1,0:T(8,128)(2,1)S(1)}, u32[]{:S(2)}) copy-start(bf16[8,192,128]{2,1,0:T(8,128)(2,1)S(1)} %all-to-all-done.3) | copy-start | bytes 1179652
  118.3 24.9 %all-to-all-start.4 = ((bf16[8,32,2048]{2,1,0:T(8,128)(2,1)}), bf16[8,32,2048]{2,1,0:T(8,128)(2,1)S(1)}, u32[]{:S(2)}, u32[]{:S(2)}) async-start(bf16[8,32,2048]{2,1,0:T(8,128)(2,1)} %bitcast.19), calls=%async_computation.4 | async-start | bytes 2097152 | tf_op jit(solution)/shard_map/all_to_all | solution.py:587
  143.2 1.0 copy-start.1

commit v3 on v2

--- a/solution.py
+++ b/solution.py
@@ -50,6 +50,10 @@
 
 def far(x):
     return pltpu.with_memory_space_constraint(x, pltpu.HBM)
+
+
+def near(x):
+    return pltpu.with_memory_space_constraint(x, pltpu.VMEM)
 
 
 def nt(a, b):
@@ -133,7 +137,7 @@
             out_specs=pl.BlockSpec((rows, width), lambda c, h: (0, 0)),
         ),
         compiler_params=params(),
-    )(h, asked, far(x))
+    )(h, near(asked), far(x))
 
 
 def picker(idx_ref, rows, width):
@@ -201,7 +205,7 @@
         in_specs=[smem(), vmem()],
         out_specs=vmem(),
         compiler_params=params(0),
-    )(idx, lat)
+    )(idx, near(lat))
 
 
 def part_pairs(tokens, c):
@@ -211,26 +215,24 @@
 
 def pack_key_kernel(idx_ref, key_ref, key_out):
     pick = picker(idx_ref, 2 * REM, key_ref.shape[0])
-    heads = key_out.shape[0]
     tokens = key_ref.shape[1] // ID
     got = [nn(pick, key_ref[:, t * ID : (t + 1) * ID]) for t in range(tokens)]
     for g in range(2):
         order = [2 * i + par for c in range(PARTS) for par in range(2) for i in part_pairs(tokens, c)]
         part = [got[t][g * REM : (g + 1) * REM] for t in order]
         rows = jnp.concatenate(part, 0).astype(bf16)
-        for d in range(heads // 2):
-            key_out[g * (heads // 2) + d] = rows
-
-
-def pack_key(idx, keys, heads):
+        key_out[g] = rows
+
+
+def pack_key(idx, keys):
     tokens = keys.shape[1] // ID
     return pl.pallas_call(
         pack_key_kernel,
-        out_shape=jax.ShapeDtypeStruct((heads, tokens * REM, ID), bf16),
+        out_shape=jax.ShapeDtypeStruct((2, tokens * REM, ID), bf16),
         in_specs=[smem(), vmem()],
         out_specs=vmem(),
         compiler_params=params(0),
-    )(idx, keys)
+    )(idx, near(keys))
 
 
 def place_keys(x, ka, kb, at, rows):
@@ -326,8 +328,8 @@
 
 def rest_kernel(n, *refs):
     src_ref, q_ref, pieces, refs = refs[0], refs[1], refs[2 : 2 + n], refs[2 + n :]
-    bias_ref, po_ref, st_ref, p_ref, f_ref, v_ref, t_ref = refs[:7]
-    ka, kb, ps, total, factors, sem = refs[7:]
+    bias_ref, po_ref, st_ref, key_ref, p_ref, f_ref, v_ref, t_ref = refs[:8]
+    ka, kb, ps, total, factors, sem = refs[8:]
     g = pl.program_id(0)
     for k, piece in enumerate(pieces):
         rows = piece.shape[1]
@@ -366,10 +368,17 @@
                     f = factors[d : d + HEAD_ROWS, k : k + 1]
                     add = add + x[d : d + HEAD_ROWS, :].astype(f32) * f
                 if par:
-                    t_ref[r : r + HEAD_ROWS, at : at + wide] = add.astype(bf16)
+                    to, row = r // t_ref.shape[1], r % t_ref.shape[1]
+                    t_ref[to, row : row + HEAD_ROWS, at : at + wide] = add.astype(bf16)
                 else:
                     total[r : r + HEAD_ROWS, at : at + wide] = add
                 at += wide
+
+    share = t_ref.shape[1]
+    for to in range(t_ref.shape[0]):
+        for n in range(key_ref.shape[0] // share):
+            at = NSEL * BLK + n * ID
+            t_ref[to, :, at : at + ID] = key_ref[n * share : (n + 1) * share]
 
     @pl.when(g == 1)
     def _():
@@ -378,28 +387,31 @@
                 out_copy(group, par).wait()
 
 
-def rest_stage(q, src, pieces, bias, own):
+def rest_stage(q, src, pieces, bias, own, rem_key, positions):
     heads = q.shape[1] // QK
     tall = heads // 2 * GROUP
     keys = bias.shape[2]
     every = NSEL * BLK
+    share = q.shape[0] // positions
+    wide = every + rem_key.shape[1] // share * ID
     return pl.pallas_call(
         functools.partial(rest_kernel, len(pieces)),
         out_shape=(
             jax.ShapeDtypeStruct((2, 2, tall, keys), bf16),
             jax.ShapeDtypeStruct((2, 2 * heads, GROUP), f32),
             jax.ShapeDtypeStruct((2, keys, LAT), bf16),
-            jax.ShapeDtypeStruct((q.shape[0], every), bf16),
+            jax.ShapeDtypeStruct((positions, share, wide), bf16),
         ),
         grid=(2,),
         in_specs=[smem(), rows_spec(q.shape[1])]
         + [vmem() for x in pieces]
-        + [group_spec(1, keys), group_spec(2, tall, OWN), group_spec(2 * heads, GROUP)],
+        + [group_spec(1, keys), group_spec(2, tall, OWN), group_spec(2 * heads, GROUP)]
+        + [group_spec(*rem_key.shape[1:])],
         out_specs=(
             anywhere(),
             group_spec(2 * heads, GROUP),
             group_spec(keys, LAT),
-            rows_spec(every),
+            pl.BlockSpec((positions // 2, share, wide), lambda g: (g, 0, 0)),
         ),
         scratch_shapes=[
             pltpu.VMEM((keys, KW), bf16),
@@ -410,7 +422,7 @@
             pltpu.SemaphoreType.DMA((4,)),
         ],
         compiler_params=params(1),
-    )(src, far(q), *pieces, bias, far(own[0]), own[1])
+    )(src, far(q), *pieces, bias, far(own[0]), own[1], rem_key)
 
 
 def context_kernel(f_ref, po_ref, pr_ref, vo_ref, vr_ref, ctx_ref):
@@ -446,126 +458,87 @@
     return nt(jnp.concatenate(cols, 0), keys)
 
 
-def fill_index_keys(own_ref, rem_ref, keys):
+def index_kernel(h_ref, iq_ref, w_ref, own_ref, part_ref, bias_own, bias_rem, loss_ref, grad_ref, keys, acts):
+    rows = iq_ref.shape[0]
+    every = keys.shape[0]
     keys[:OWN] = own_ref[...]
-    heads, parts, rows = rem_ref.shape[:3]
-    for c in range(parts):
-        for d in range(heads):
-            at = OWN + (c * heads + d) * rows
-            keys[at : at + rows] = rem_ref[d, c]
-
-
-def logits_kernel(iq_ref, w_ref, own_ref, rem_ref, bias_own, bias_rem, out_ref, keys):
-    fill_index_keys(own_ref, rem_ref, keys)
-    rows = iq_ref.shape[0]
-    sum_ = jnp.zeros(out_ref.shape, f32)
+    places = part_ref.shape[0]
+    each = (every - OWN) // places
+    for d in range(places):
+        for n in range(each // rows):
+            at = OWN + d * each + n * rows
+            keys[at : at + rows] = part_ref[d, :, every + n * ID : every + (n + 1) * ID]
+    sum_ = jnp.zeros((rows, every), f32)
     for b in range(IH // JB):
         act = index_part(iq_ref, keys[...], b)
+        acts[b] = act.astype(bf16)
         for n in range(JB):
             j = b * JB + n
             sum_ = sum_ + jnp.maximum(act[n * rows : (n + 1) * rows], 0.0) * w_ref[:, j : j + 1]
     logits = sum_ * INDEX_SCALE
-    rem = jnp.concatenate([bias_rem[...]] * PARTS, 1)
-    logits = jnp.concatenate([logits[:, :OWN] + bias_own[...], logits[:, OWN:] + rem], 1)
+    logits = jnp.concatenate(
+        [logits[:, :OWN] + bias_own[...], logits[:, OWN:] + bias_rem[...]], 1
+    )
     top = jnp.max(logits, -1, keepdims=True)
     shifted = logits - top
-    out_ref[...] = shifted - jnp.log(jnp.sum(jnp.exp(shifted), -1, keepdims=True))
-
-
-def index_specs(rows, heads, rem):
-    group = lambda c, h: (h[0] // (heads // 2), 0, 0)
-    return group, [
-        pl.BlockSpec((rows, IH * ID), lambda c, h: (0, 0)),
-        pl.BlockSpec((rows, IH), lambda c, h: (0, 0)),
-        pl.BlockSpec((None, OWN, ID), group),
-        pl.BlockSpec(rem.shape, lambda c, h: (0, 0, 0, 0)),
-    ]
-
-
-def index_logits(h, iq, w, own, rem, bias_own, bias_rem, heads):
-    rows = iq.shape[0]
-    group, specs = index_specs(rows, heads, rem)
-    keys = NSEL * BLK
-
-    def kernel(h_ref, *refs):
-        logits_kernel(*refs)
-
-    return pl.pallas_call(
-        kernel,
-        out_shape=jax.ShapeDtypeStruct((rows, keys), f32),
-        grid_spec=pltpu.PrefetchScalarGridSpec(
-            num_scalar_prefetch=1,
-            grid=(1,),
-            in_specs=specs
-            + [
-                pl.BlockSpec((None, rows, OWN), lambda c, h: (h[0], 0, 0)),
-                pl.BlockSpec((None, 1, bias_rem.shape[2]), group),
-            ],
-            out_specs=pl.BlockSpec((rows, keys), lambda c, h: (0, 0)),
-            scratch_shapes=[pltpu.VMEM((keys, ID), bf16)],
-        ),
-        compiler_params=params(),
-    )(h, iq, w, own, rem, bias_own, bias_rem)
-
-
-def grad_kernel(iq_ref, w_ref, own_ref, rem_ref, logq_ref, part_ref, loss_ref, grad_ref, keys):
-    fill_index_keys(own_ref, rem_ref, keys)
-    rows = iq_ref.shape[0]
-    target = part_ref[0].astype(f32)
-    for n in range(1, part_ref.shape[0]):
-        target = target + part_ref[n].astype(f32)
+    log_q = shifted - jnp.log(jnp.sum(jnp.exp(shifted), -1, keepdims=True))
+    target = part_ref[0, :, :every].astype(f32)
+    for n in range(1, places):
+        target = target + part_ref[n, :, :every].astype(f32)
     target = target / H
-    log_q = logq_ref[...]
     shown = log_q > 0.5 * NEG
     prob_q = jnp.where(shown, jnp.exp(log_q), 0.0)
     live = shown & (target > 0)
     safe = jnp.where(live, target, 1.0)
     terms = jnp.where(live, target * (jnp.log(safe) - log_q), 0.0)
-    loss_ref[...] = jnp.sum(terms, -1, keepdims=True)
+    loss = jnp.sum(terms, -1, keepdims=True)
+    eye = lax.broadcasted_iota(i32, (rows, rows), 0) == lax.broadcasted_iota(i32, (rows, rows), 1)
+    loss_ref[...] = jnp.sum(jnp.where(eye, loss, 0.0), 0, keepdims=True)
     diff = prob_q - target
     for b in range(IH // JB):
-        act = index_part(iq_ref, keys[...], b)
         coef = []
         for n in range(JB):
             j = b * JB + n
             value = diff * (w_ref[:, j : j + 1] * INDEX_SCALE)
-            coef.append(jnp.where(act[n * rows : (n + 1) * rows] > 0, value, 0.0))
-        got = nn(jnp.concatenate(coef, 0).astype(bf16), keys[...])
+            seen = acts[b, n * rows : (n + 1) * rows].astype(f32) > 0
+            coef.append(jnp.where(seen, value, 0.0).astype(bf16))
+        got = nn(jnp.concatenate(coef, 0), keys[...])
         for n in range(JB):
             j = b * JB + n
             grad_ref[:, j * ID : (j + 1) * ID] = got[n * rows : (n + 1) * rows]
 
 
-def index_grads(h, iq, w, own, rem, log_q, parts, heads):
+def index(h, iq, w, own, parts, bias_own, bias_rem):
     rows = iq.shape[0]
-    group, specs = index_specs(rows, heads, rem)
+    heads = parts.shape[0]
     keys = NSEL * BLK
-
-    def kernel(h_ref, *refs):
-        grad_kernel(*refs)
-
-    return pl.pallas_call(
-        kernel,
+    group = lambda c, h: (h[0] // (heads // 2), 0, 0)
+    flat = lambda c, h: (0, 0)
+    return pl.pallas_call(
+        index_kernel,
         out_shape=(
-            jax.ShapeDtypeStruct((rows, 1), f32),
+            jax.ShapeDtypeStruct((1, rows), f32),
             jax.ShapeDtypeStruct((rows, IH * ID), f32),
         ),
         grid_spec=pltpu.PrefetchScalarGridSpec(
             num_scalar_prefetch=1,
             grid=(1,),
-            in_specs=specs
-            + [
-                pl.BlockSpec((rows, keys), lambda c, h: (0, 0)),
-                pl.BlockSpec((heads, rows, keys), lambda c, h: (0, 0, 0)),
+            in_specs=[
+                pl.BlockSpec((rows, IH * ID), flat),
+                pl.BlockSpec((rows, IH), flat),
+                pl.BlockSpec((None, OWN, ID), group),
+                pl.BlockSpec(parts.shape, lambda c, h: (0, 0, 0)),
+                pl.BlockSpec((None, rows, OWN), lambda c, h: (h[0], 0, 0)),
+                pl.BlockSpec((None, 1, keys - OWN), group),
             ],
-            out_specs=(
-                pl.BlockSpec((rows, 1), lambda c, h: (0, 0)),
-                pl.BlockSpec((rows, IH * ID), lambda c, h: (0, 0)),
-            ),
-            scratch_shapes=[pltpu.VMEM((keys, ID), bf16)],
+            out_specs=(pl.BlockSpec((1, rows), flat), pl.BlockSpec((rows, IH * ID), flat)),
+            scratch_shapes=[
+                pltpu.VMEM((keys, ID), bf16),
+                pltpu.VMEM((IH // JB, JB * rows, keys), bf16),
+            ],
         ),
         compiler_params=params(),
-    )(h, iq, w, own, rem, log_q, parts)
+    )(h, iq, w, own, near(parts), bias_own, bias_rem)
 
 
 def gather_head(x, heads):
@@ -573,10 +546,7 @@
     for d in (2, heads - 2, 4):
         ring.append(lax.ppermute(x, "head", [(i, (i + d) % heads) for i in range(heads)]))
     other = [lax.ppermute(r, "head", [(i, i ^ 1) for i in range(heads)]) for r in ring]
-    h = lax.axis_index("head")
-    back = jnp.array([0, 2, heads - 2, 4], i32)
-    at = jnp.concatenate([h - back + heads, (h ^ 1) - back + heads]) % heads
-    return ring + other, at
+    return ring + other
 
 
 def after(x, *first):
@@ -614,23 +584,22 @@
     bias_rem = jnp.tile(used, (1, BLK // PARTS))[:, None, :]
 
     own = own_stage(query, own_lat, bias_own)
-    in_l = after(in_l, own[0], bias_rem)
+    back = jnp.array([0, 2, heads - 2, 4], i32)
+    src = jnp.concatenate([h - back + heads, (h ^ 1) - back + heads]) % heads
+    in_l, bias_rem, src, _ = lax.optimization_barrier((in_l, bias_rem, src, own[0]))
     packed = pack_lat(place, in_l)
-    pieces, src = gather_head(packed, heads)
+    pieces = gather_head(packed, heads)
     in_k = swap(after(out_k, packed), "seq")
-    packed_k = pack_key(place, in_k, heads)
-    rem_key = swap(packed_k, "head").reshape(heads, PARTS, -1, ID)
-    p_r, factors, v_r, partial = rest_stage(after(query, packed_k), src, pieces, bias_rem, own)
+    packed_k = pack_key(place, in_k)
+    p_r, factors, v_r, partial = rest_stage(
+        query, src, pieces, bias_rem, own, packed_k, heads
+    )
+    parts = swap(partial, "head")
+    context = contexts(after(factors, partial), own[0], p_r, own[2], v_r)
     share = index_query.shape[0]
-    parts = swap(partial.reshape(heads, share, -1), "head")
-    context = contexts(after(factors, partial), own[0], p_r, own[2], v_r)
-    log_q = index_logits(
-        h1, index_query, index_weight, own_key, rem_key,
-        bias_own.reshape(heads, share, OWN), bias_rem, heads,
-    )
-    parts = after(parts, context, log_q)
-    loss, grad = index_grads(
-        h1, index_query, index_weight, own_key, rem_key, log_q, parts, heads
+    loss, grad = index(
+        h1, index_query, index_weight, own_key, after(parts, context),
+        bias_own.reshape(heads, share, OWN), bias_rem,
     )
     return context, loss.reshape(-1), grad
 

time: 154 us -> 142 us (0.922)
  starting transfers between devices: 46.3 us -> 41.7 us
  Pallas kernels: 81 us -> 76.5 us
  local copies, waits for them, and re-layouts: 6 us -> 2.2 us
  waiting for transfers between devices: 14.9 us -> 17.7 us
    all_to_all x5 -> x4, starting transfers between devices: 27.3 us -> 22.7 us  [swap(): return lax.all_to_all(x, axis, split_axis=0, concat_axis=0, tiled=True)]
    unnamed x30 -> x20, local copies, waits for them, and re-layouts: 4.83 us -> 1.03 us
    pallas_call x3 -> x2, Pallas kernels: 13.9 us -> 10.5 us  [the longest x1 8.98 us: index(): pl.pallas_call(index_kernel, out_shape=(jax.ShapeDtypeStruct((1, rows), f...]
    all_to_all x5 -> x4, waiting for transfers between devices: 14.8 us -> 17.7 us  [swap(): return lax.all_to_all(x, axis, split_axis=0, concat_axis=0, tiled=True)]
  transfers between devices with their start and end apart: 12 -> 11, of which waited for: 2 -> 3; matrix products, arithmetic and copies ran while one was open for 2% -> 3% of each run, Pallas kernels for 43% -> 25%
where the time goes in v3:
time: 142 us
  Pallas kernels  76.5 us (54%)
  starting transfers between devices  41.7 us (29%)
  waiting for transfers between devices  17.7 us (12%)
  other arithmetic  2.57 us (2%)
  local copies, waits for them, and re-layouts  2.2 us (2%)
    pallas_call x1, Pallas kernels, rest_stage(): pl.pallas_call(functools.partial(rest_kernel, len(pieces)), out_shape=(ja...  25.7 us
    all_to_all x4, starting transfers between devices, swap(): return lax.all_to_all(x, axis, split_axis=0, concat_axis=0, tiled=True)  22.7 us
    all_to_all x4, waiting for transfers between devices, swap(): return lax.all_to_all(x, axis, split_axis=0, concat_axis=0, tiled=True)  17.7 us
    ppermute x4, starting transfers between devices, gather_head(): lax.ppermute(r, 'head', [(i, i ^ 1) for i in range(heads)])  14.6 us
    pallas_call x1, Pallas kernels, contexts(): pl.pallas_call(context_kernel, out_shape=jax.ShapeDtypeStruct((2 * GROUP,...  14.5 us
    pallas_call x1, Pallas kernels, index(): pl.pallas_call(index_kernel, out_shape=(jax.ShapeDtypeStruct((1, rows), f...  8.98 us
    pallas_call x1, Pallas kernels, own_rows(): pl.pallas_call(own_kernel, out_shape=(jax.ShapeDtypeStruct((2, OWN // 2,...  8.53 us
    pallas_call x1, Pallas kernels, own_stage(): pl.pallas_call(own_stage_kernel, out_shape=(jax.ShapeDtypeStruct((2, 2, t...  8.15 us
  transfers between devices with their start and end apart: 11, of which 3 were waited for; matrix products, arithmetic and copies ran while one was open for 3% of the time, Pallas kernels for 25%

profile of v3, /device:TPU:1, one launch (start us, length us, event | category | flops | bytes accessed | tf_op | source)
XLA Modules:
  0.0 141.6 jit_solution(9666372956849396149)
XLA Ops:
  0.6 1.7 %shard_map.112 = (s32[256,128]{1,0:T(8,128)}, s32[48]{0:T(128)}, s32[16]{0:T(128)}) custom-call(s32[1]{0:T(128)} %bitcast.1.me_ref, s32[2,32]{1,0:T(2,128)} %list_ref.1, s32[2]{0:T(128)} %len_ref.1), custom_call_target="tpu_custom_call" | custom-call | tf_op jit(solution)/shard_map/pallas_call | solution.py:105
  2.4 9.4 %all-to-all-start = ((s32[16,16,128]{2,1,0:T(8,128)}), s32[16,16,128]{2,1,0:T(8,128)S(1)}, u32[]{:S(2)}, u32[]{:S(2)}) async-start(s32[16,16,128]{2,1,0:T(8,128)} %bitcast.17), calls=%async_computation | async-start | bytes 262144 | tf_op jit(solution)/shard_map/all_to_all | solution.py:557
  11.8 6.9 %all-to-all-done = s32[16,16,128]{2,1,0:T(8,128)S(1)} async-done(((s32[16,16,128]{2,1,0:T(8,128)}), s32[16,16,128]{2,1,0:T(8,128)S(1)}, u32[]{:S(2)}, u32[]{:S(2)}) %all-to-all-start) | async-done | bytes 131104 | tf_op jit(solution)/shard_map/all_to_all | solution.py:557
  18.6 3.4 %shard_map.113 = bf16[256,4608]{1,0:T(8,128)(2,1)} custom-call(s32[1]{0:T(128)} %bitcast.h_ref, s32[256,128]{1,0:T(8,128)S(1)} %bitcast.13, bf16[128,36864]{1,0:T(8,128)(2,1)} %lat_ref.1), custom_call_target="tpu_custom_call" | custom-call | tf_op jit(solution)/shard_map/pallas_call | solution.py:127
  22.1 0.0 copy-start.7
  22.1 0.0 copy-start.6
  22.1 0.0 copy-start.8
  22.1 0.0 copy-start.9
  22.1 3.9 %all-to-all-start.1 = ((bf16[16,16,4608]{2,1,0:T(8,128)(2,1)}), bf16[16,16,4608]{2,1,0:T(8,128)(2,1)S(1)}, u32[]{:S(2)}, u32[]{:S(2)}) async-start(bf16[16,16,4608]{2,1,0:T(8,128)(2,1)} %bitcast.15), calls=%async_computation.1 | async-start | bytes 4718592 | tf_op jit(solution)/shard_map/all_to_all | solution.py:557
  25.9 0.0 copy-done.7
  26.0 0.1 mul.33
  26.1 0.1 mul.34
  26.2 0.0 copy-done.6
  26.2 0.1 select_n.51
  26.3 0.1 tile.7
  26.4 0.0 copy-done.8
  26.4 0.6 and_select_fusion.refs_0_
  27.0 0.0 copy-done.9
  27.0 0.1 iota_add_fusion
  27.1 0.9 compare_select_fusion.1.bias_ref
  28.0 2.0 %shard_map.114 = bf16[256,1024]{1,0:T(8,128)(2,1)} custom-call(s32[1]{0:T(128)} %bitcast.h_ref, s32[256,128]{1,0:T(8,128)S(1)} %bitcast.14, bf16[128,8192]{1,0:T(8,128)(2,1)} %key_ref.1), custom_call_target="tpu_custom_call" | custom-call | tf_op jit(solution)/shard_map/pallas_call | solution.py:127
  30.0 8.5 %shard_map.115 = (bf16[2,256,1152]{2,1,0:T(8,128)(2,1)}, bf16[2,2,256,128]{3,2,1,0:T(8,128)(2,1)}) custom-call(s32[16]{0:T(128)} %get-tuple-element.29.idx_ref, bf16[128,36864]{1,0:T(8,128)(2,1)} %lat_ref.1, bf16[128,8192]{1,0:T(8,128)(2,1)} %key_ref.1), custom_call_target="tpu_custom_call" | custom-call | tf_op jit(solution)/shard_map/pallas_call | solution.py:171
  38.6 8.1 %shard_map.116 = (bf16[2,2,1024,512]{3,2,1,0:T(8,128)(2,1)}, f32[2,32,128]{2,1,0:T(8,128)}, bf16[2,512,512]{2,1,0:T(8,128)(2,1)}) custom-call(bf16[256,9216]{1,0:T(8,128)(2,1)} %refs_1_.1, bf16[2,256,1152]{2,1,0:T(8,128)(2,1)} %get-tuple-element.30.own_ref, f32[2,128,512]{2,1,0:T(8,128)} %compare_select_fusion.1.bias_ref), custom_call_target="tpu_custom_call" | custom-call | tf_op jit(solution)/shard_map/pallas_call | solution.py:310
  46.7 7.4 %all-to-all-done.1 = bf16[16,16,4608]{2,1,0:T(8,128)(2,1)S(1)} async-done(((bf16[16,16,4608]{2,1,0:T(8,128)(2,1)}), bf16[16,16,4608]{2,1,0:T(8,128)(2,1)S(1)}, u32[]{:S(2)}, u32[]{:S(2)}) %all-to-all-start.1) | async-done | bytes 2359328 | tf_op jit(solution)/shard_map/all_to_all | solution.py:557
  54.1 1.9 %shard_map.117.refs_2_ = bf16[2,96,1152]{2,1,0:T(8,128)(2,1)} custom-call(s32[48]{0:T(128)} %get-tuple-element.26.idx_ref, bf16[256,4608]{1,0:T(8,128)(2,1)S(1)} %bitcast.11), custom_call_target="tpu_custom_call" | custom-call | tf_op jit(solution)/shard_map/pallas_call | solution.py:202
  56.0 1.3 collective-permute-start
  57.3 1.4 %collective-permute-start.1 = (bf16[2,96,1152]{2,1,0:T(8,128)(2,1)}, bf16[2,96,1152]{2,1,0:T(8,128)(2,1)S(1)}, u32[]{:S(2)}, u32[]{:S(2)}) collective-permute-start(bf16[2,96,1152]{2,1,0:T(8,128)(2,1)} %shard_map.117.refs_2_), channel_id=1, source_target_pairs={{0,6},{1,7},{2,0},{3,1},{4,2},{5,3},{6,4},{7,5},{8,14},{9,15},{10,... | collective-permute-start | bytes 1327112 | tf_op jit(solution)/shard_map/ppermute | solution.py:547
  58.7 1.6 %collective-permute-start.2 = (bf16[2,96,1152]{2,1,0:T(8,128)(2,1)}, bf16[2,96,1152]{2,1,0:T(8,128)(2,1)S(1)}, u32[]{:S(2)}, u32[]{:S(2)}) collective-permute-start(bf16[2,96,1152]{2,1,0:T(8,128)(2,1)} %shard_map.117.refs_2_), channel_id=1, source_target_pairs={{0,4},{1,5},{2,6},{3,7},{4,0},{5,1},{6,2},{7,3},{8,12},{9,13},{10,... | collective-permute-start | bytes 1327112 | tf_op jit(solution)/shard_map/ppermute | solution.py:547
  60.4 5.7 %all-to-all-start.2 = ((bf16[16,16,1024]{2,1,0:T(8,128)(2,1)}), bf16[16,16,1024]{2,1,0:T(8,128)(2,1)S(1)}, u32[]{:S(2)}, u32[]{:S(2)}) async-start(bf16[16,16,1024]{2,1,0:T(8,128)(2,1)} %bitcast.6), calls=%async_computation.2 | async-start | bytes 1048576 | tf_op jit(solution)/shard_map/all_to_all | solution.py:557
  66.1 4.6 %collective-permute-start.3 = (bf16[2,96,1152]{2,1,0:T(8,128)(2,1)}, bf16[2,96,1152]{2,1,0:T(8,128)(2,1)S(1)}, u32[]{:S(2)}, u32[]{:S(2)}) collective-permute-start(bf16[2,96,1152]{2,1,0:T(8,128)(2,1)} %shard_map.117.refs_2_), channel_id=1, source_target_pairs={{0,1},{1,0},{2,3},{3,2},{4,5},{5,4},{6,7},{7,6},{8,9},{9,8},{10,11... | collective-permute-start | bytes 1327112 | tf_op jit(solution)/shard_map/ppermute | solution.py:548
  70.8 0.0 collective-permute-done.refs_3_
  70.8 0.0 copy-start
  70.8 5.2 %collective-permute-start.4 = (bf16[2,96,1152]{2,1,0:T(8,128)(2,1)S(1)}, bf16[2,96,1152]{2,1,0:T(8,128)(2,1)S(1)}, u32[]{:S(2)}, u32[]{:S(2)}) collective-permute-start(bf16[2,96,1152]{2,1,0:T(8,128)(2,1)S(1)} %collective-permute-done.refs_3_), channel_id=1, source_target_pairs={{0,1},{1,0},{2,3},{3,2},{4,5},{5,4},{6,7},{7,6},{8,9},{9,8},{10,11... | collective-permute-start | bytes 1327112 | tf_op jit(solution)/shard_map/ppermute | solution.py:548
  76.0 0.0 collective-permute-done.1.refs_4_
  76.0 0.0 copy-start.1
  76.0 0.1 collective-permute-start.5
  76.1 0.0 collective-permute-done.2.refs_5_
  76.1 0.0 copy-start.2
  76.1 4.7 %collective-permute-start.6 = (bf16[2,96,1152]{2,1,0:T(8,128)(2,1)S(1)}, bf16[2,96,1152]{2,1,0:T(8,128)(2,1)}, u32[]{:S(2)}, u32[]{:S(2)}) collective-permute-start(bf16[2,96,1152]{2,1,0:T(8,128)(2,1)S(1)} %collective-permute-done.2.refs_5_), channel_id=1, source_target_pairs={{0,1},{1,0},{2,3},{3,2},{4,5},{5,4},{6,7},{7,6},{8,9},{9,8},{10,11... | collective-permute-start | bytes 1327112 | tf_op jit(solution)/shard_map/ppermute | solution.py:548
  80.8 0.6 copy.12.refs_10_.bias_rem
  81.4 0.0 all-to-all-done.2
  81.4 1.5 %shard_map.118.refs_13_ = bf16[2,192,128]{2,1,0:T(8,128)(2,1)} custom-call(s32[48]{0:T(128)} %get-tuple-element.26.idx_ref, bf16[256,1024]{1,0:T(8,128)(2,1)S(1)} %bitcast.12), custom_call_target="tpu_custom_call" | custom-call | tf_op jit(solution)/shard_map/pallas_call | solution.py:229
  82.9 0.0 collective-permute-done.3.refs_6_
  82.9 0.0 copy-start.3
  82.9 0.0 collective-permute-done.4.refs_7_
  82.9 0.0 copy-start.4
  82.9 0.0 collective-permute-done.5.refs_8_
  82.9 0.0 copy-start.5
  83.0 0.0 collective-permute-done.6.refs_9_
  83.0 0.0 copy-done
  83.0 0.0 copy-done.1
  83.0 0.0 copy-done.2
  83.0 0.7 copy-done.3
  83.7 0.1 copy-done.4
  83.8 0.2 copy-done.5
  84.0 25.7 %shard_map.119 = (bf16[2,2,1024,1536]{3,2,1,0:T(8,128)(2,1)}, f32[2,32,128]{2,1,0:T(8,128)}, bf16[2,1536,512]{2,1,0:T(8,128)(2,1)}, bf16[8,32,2816]{2,1,0:T(8,128)(2,1)}) custom-call(s32[8]{0:T(128)} %and_select_fusion.refs_0_, bf16[256,9216]{1,0:T(8,128)(2,1)} %refs_1_.1, bf16[2,96,1152]{2,1,0:T(8,128)(2,1)} %shard_map.117.refs_2_, ...), custom_call_target="tpu_custom_call" | custom-call | tf_op jit(solution)/shard_map/pallas_call | solution.py:397
  109.7 3.8 %all-to-all-start.3 = ((bf16[8,32,2816]{2,1,0:T(8,128)(2,1)}), bf16[8,32,2816]{2,1,0:T(8,128)(2,1)S(1)}, u32[]{:S(2)}, u32[]{:S(2)}) async-start(bf16[8,32,2816]{2,1,0:T(8,128)(2,1)} %get-tuple-element.38), calls=%async_computation.3 | async-start | bytes 2883584 | tf_op jit(solution)/shard_map/all_to_all | solution.py:557
  113.5 0.1 add.117
  113.6 0.1 add.118
  113.7 0.1 broadcast_add_fusion
  113.8 0.9 compare_select_fusion.bias_own
  114.7 14.5 %shard_map.120 = bf16[256,8192]{1,0:T(8,128)(2,1)} custom-call(f32[2,32,128]{2,1,0:T(8,128)} %get-tuple-element.39.f_ref, bf16[2,2,1024,512]{3,2,1,0:T(8,128)(2,1)} %get-tuple-element.31.refs_11_.po_ref, bf16[2,2,1024,1536]{3,2,1,0:T(8,128)(2,1)} %get-tuple-element.40.pr_ref, bf16[2,512,512]{2,1,0:T(8,128)(2,1)} %get-tuple-element.41.vo_ref, ...), custom_call_target="tpu_custom_call" | custom-call | tf_op jit(solution)/shard_map/pallas_call | solution.py:443
  129.2 3.4 %all-to-all-done.3.part_ref = bf16[8,32,2816]{2,1,0:T(8,128)(2,1)S(1)} async-done(((bf16[8,32,2816]{2,1,0:T(8,128)(2,1)}), bf16[8,32,2816]{2,1,0:T(8,128)(2,1)S(1)}, u32[]{:S(2)}, u32[]{:S(2)}) %all-to-all-start.3) | async-done | bytes 1441824 | tf_op jit(solution)/shard_map/all_to_all | solution.py:557
  132.6 9.0 %shard_map.121 = (f32[1,32]{1,0:T(1,128)}, f32[32,8192]{1,0:T(8,128)}) custom-call(s32[1]{0:T(128)} %bitcast.h_ref, bf16[32,8192]{1,0:T(8,128)(2,1)} %iq_ref.1, f32[32,64]{1,0:T(8,128)} %w_ref.1, bf16[2,512,128]{2,1,0:T(8,128)(2,1)} %bitcast.16, bf16[8,32,2816]{2,1,0:T(8,128)(2,1)S(1)} %all-to-all-done.3.part_ref, ...), custom_call_target="tpu_custom_call" | custom-call | tf_op jit(solution)/shard_map/pallas_call | solution.py:517
  (11 shorter events, 0.1 us)
Async XLA Ops:
  2.4 16.2 %all-to-all-start = ((s32[16,16,128]{2,1,0:T(8,128)}), s32[16,16,128]{2,1,0:T(8,128)S(1)}, u32[]{:S(2)}, u32[]{:S(2)}) async-start(s32[16,16,128]{2,1,0:T(8,128)} %bitcast.17), calls=%async_computation | async-start | bytes 262144 | tf_op jit(solution)/shard_map/all_to_all | solution.py:557
  22.1 3.9 %copy-start.7 = (s32[16]{0:T(128)S(1)}, s32[16]{0:T(128)}, u32[]{:S(2)}) copy-start(s32[16]{0:T(128)} %get-tuple-element.29.idx_ref) | copy-start | bytes 196
  22.1 4.1 %copy-start.6 = (s32[48]{0:T(128)S(1)}, s32[48]{0:T(128)}, u32[]{:S(2)}) copy-start(s32[48]{0:T(128)} %get-tuple-element.26.idx_ref) | copy-start | bytes 580
  22.1 4.3 %copy-start.8 = (s32[4]{0:T(128)S(1)}, s32[4]{0:T(128)}, u32[]{:S(2)}) copy-start(s32[4]{0:T(128)} %constant.85) | copy-start | bytes 52
  22.1 4.9 %copy-start.9 = (s32[2]{0:T(128)S(1)}, s32[2]{0:T(128)}, u32[]{:S(2)}) copy-start(s32[2]{0:T(128)} %param.16) | copy-start | bytes 28
  22.1 32.0 %all-to-all-start.1 = ((bf16[16,16,4608]{2,1,0:T(8,128)(2,1)}), bf16[16,16,4608]{2,1,0:T(8,128)(2,1)S(1)}, u32[]{:S(2)}, u32[]{:S(2)}) async-start(bf16[16,16,4608]{2,1,0:T(8,128)(2,1)} %bitcast.15), calls=%async_computation.1 | async-start | bytes 4718592 | tf_op jit(solution)/shard_map/all_to_all | solution.py:557
  56.0 14.8 %collective-permute-start = (bf16[2,96,1152]{2,1,0:T(8,128)(2,1)}, bf16[2,96,1152]{2,1,0:T(8,128)(2,1)S(1)}, u32[]{:S(2)}, u32[]{:S(2)}) collective-permute-start(bf16[2,96,1152]{2,1,0:T(8,128)(2,1)} %shard_map.117.refs_2_), channel_id=1, source_target_pairs={{0,2},{1,3},{2,4},{3,5},{4,6},{5,7},{6,0},{7,1},{8,10},{9,11},{10,... | collective-permute-start | bytes 1327112 | tf_op jit(solution)/shard_map/ppermute | solution.py:547
  57.3 18.7 %collective-permute-start.1 = (bf16[2,96,1152]{2,1,0:T(8,128)(2,1)}, bf16[2,96,1152]{2,1,0:T(8,128)(2,1)S(1)}, u32[]{:S(2)}, u32[]{:S(2)}) collective-permute-start(bf16[2,96,1152]{2,1,0:T(8,128)(2,1)} %shard_map.117.refs_2_), channel_id=1, source_target_pairs={{0,6},{1,7},{2,0},{3,1},{4,2},{5,3},{6,4},{7,5},{8,14},{9,15},{10,... | collective-permute-start | bytes 1327112 | tf_op jit(solution)/shard_map/ppermute | solution.py:547
  58.7 17.3 %collective-permute-start.2 = (bf16[2,96,1152]{2,1,0:T(8,128)(2,1)}, bf16[2,96,1152]{2,1,0:T(8,128)(2,1)S(1)}, u32[]{:S(2)}, u32[]{:S(2)}) collective-permute-start(bf16[2,96,1152]{2,1,0:T(8,128)(2,1)} %shard_map.117.refs_2_), channel_id=1, source_target_pairs={{0,4},{1,5},{2,6},{3,7},{4,0},{5,1},{6,2},{7,3},{8,12},{9,13},{10,... | collective-permute-start | bytes 1327112 | tf_op jit(solution)/shard_map/ppermute | solution.py:547
  60.4 21.0 %all-to-all-start.2 = ((bf16[16,16,1024]{2,1,0:T(8,128)(2,1)}), bf16[16,16,1024]{2,1,0:T(8,128)(2,1)S(1)}, u32[]{:S(2)}, u32[]{:S(2)}) async-start(bf16[16,16,1024]{2,1,0:T(8,128)(2,1)} %bitcast.6), calls=%async_computation.2 | async-start | bytes 1048576 | tf_op jit(solution)/shard_map/all_to_all | solution.py:557
  66.1 16.8 %collective-permute-start.3 = (bf16[2,96,1152]{2,1,0:T(8,128)(2,1)}, bf16[2,96,1152]{2,1,0:T(8,128)(2,1)S(1)}, u32[]{:S(2)}, u32[]{:S(2)}) collective-permute-start(bf16[2,96,1152]{2,1,0:T(8,128)(2,1)} %shard_map.117.refs_2_), channel_id=1, source_target_pairs={{0,1},{1,0},{2,3},{3,2},{4,5},{5,4},{6,7},{7,6},{8,9},{9,8},{10,11... | collective-permute-start | bytes 1327112 | tf_op jit(solution)/shard_map/ppermute | solution.py:548
  70.8 12.2 %copy-start = (bf16[2,96,1152]{2,1,0:T(8,128)(2,1)}, bf16[2,96,1152]{2,1,0:T(8,128)(2,1)S(1)}, u32[]{:S(2)}) copy-start(bf16[2,96,1152]{2,1,0:T(8,128)(2,1)S(1)} %collective-permute-done.refs_3_) | copy-start | bytes 1327108
  70.8 12.1 %collective-permute-start.4 = (bf16[2,96,1152]{2,1,0:T(8,128)(2,1)S(1)}, bf16[2,96,1152]{2,1,0:T(8,128)(2,1)S(1)}, u32[]{:S(2)}, u32[]{:S(2)}) collective-permute-start(bf16[2,96,1152]{2,1,0:T(8,128)(2,1)S(1)} %collective-permute-done.refs_3_), channel_id=1, source_target_pairs={{0,1},{1,0},{2,3},{3,2},{4,5},{5,4},{6,7},{7,6},{8,9},{9,8},{10,11... | collective-permute-start | bytes 1327112 | tf_op jit(solution)/shard_map/ppermute | solution.py:548
  76.0 7.0 %copy-start.1 = (bf16[2,96,1152]{2,1,0:T(8,128)(2,1)}, bf16[2,96,1152]{2,1,0:T(8,128)(2,1)S(1)}, u32[]{:S(2)}) copy-start(bf16[2,96,1152]{2,1,0:T(8,128)(2,1)S(1)} %collective-permute-done.1.refs_4_) | copy-start | bytes 1327108
  76.0 7.0 %collective-permute-start.5 = (bf16[2,96,1152]{2,1,0:T(8,128)(2,1)S(1)}, bf16[2,96,1152]{2,1,0:T(8,128)(2,1)S(1)}, u32[]{:S(2)}, u32[]{:S(2)}) collective-permute-start(bf16[2,96,1152]{2,1,0:T(8,128)(2,1)S(1)} %collective-permute-done.1.refs_4_), channel_id=1, source_target_pairs={{0,1},{1,0},{2,3},{3,2},{4,5},{5,4},{6,7},{7,6},{8,9},{9,8},{10,11... | collective-permute-start | bytes 1327112 | tf_op jit(solution)/shard_map/ppermute | solution.py:548
  76.1 6.9 %copy-start.2 = (bf16[2,96,1152]{2,1,0:T(8,128)(2,1)}, bf16[2,96,1152]{2,1,0:T(8,128)(2,1)S(1)}, u32[]{:S(2)}) copy-start(bf16[2,96,1152]{2,1,0:T(8,128)(2,1)S(1)} %collective-permute-done.2.refs_5_) | copy-start | bytes 1327108
  76.1 6.9 %collective-permute-start.6 = (bf16[2,96,1152]{2,1,0:T(8,128)(2,1)S(1)}, bf16[2,96,1152]{2,1,0:T(8,128)(2,1)}, u32[]{:S(2)}, u32[]{:S(2)}) collective-permute-start(bf16[2,96,1152]{2,1,0:T(8,128)(2,1)S(1)} %collective-permute-done.2.refs_5_), channel_id=1, source_target_pairs={{0,1},{1,0},{2,3},{3,2},{4,5},{5,4},{6,7},{7,6},{8,9},{9,8},{10,11... | collective-permute-start | bytes 1327112 | tf_op jit(solution)/shard_map/ppermute | solution.py:548
  82.9 0.8 copy-start.3
  82.9 0.9 copy-start.4
  82.9 1.1 copy-start.5
  109.7 22.9 %all-to-all-start.3 = ((bf16[8,32,2816]{2,1,0:T(8,128)(2,1)}), bf16[8,32,2816]{2,1,0:T(8,128)(2,1)S(1)}, u32[]{:S(2)}, u32[]{:S(2)}) async-start(bf16[8,32,2816]{2,1,0:T(8,128)(2,1)} %get-tuple-element.38), calls=%async_computation.3 | async-start | bytes 2883584 | tf_op jit(solution)/shard_map/all_to_all | solution.py:557

commit v4 on v3

--- a/solution.py
+++ b/solution.py
@@ -247,13 +247,15 @@
     ka[pl.ds(at + rows, rows), :] = pltpu.roll(odd, QK, 1).astype(bf16)
 
 
-def score(q, keys, bias, par):
-    pairs = q.shape[1] // PAIR
-    first = [n * PAIR + par * (PAIR - KW) for n in range(pairs)]
-    rows = jnp.concatenate([q[:, c : c + KW] for c in first], 0)
+def head_rows(q, par):
+    first = range(par * (PAIR - KW), q.shape[1], PAIR)
+    return jnp.concatenate([q[:, c : c + KW] for c in first], 0)
+
+
+def score(rows, keys, bias):
     s = nt(rows, keys)
     if bias.shape[0] > 1:
-        s = (s.reshape(pairs, *bias.shape) + bias).reshape(s.shape)
+        s = (s.reshape(-1, *bias.shape) + bias).reshape(s.shape)
     else:
         s = s + bias
     top = jnp.max(s, -1, keepdims=True)
@@ -277,6 +279,7 @@
     )
 
 
+SOME = 2
 HEAD_ROWS = 16
 
 
@@ -286,7 +289,7 @@
     q, bias = q_ref[...], bias_ref[...]
     n = st_ref.shape[0] // 4
     for par, keys in ((0, ka), (1, kb)):
-        w, top, sum_ = score(q, keys[...], bias, par)
+        w, top, sum_ = score(head_rows(q, par), keys[...], bias)
         p_ref[par] = w.astype(bf16)
         st_ref[par * n : (par + 1) * n] = lane_rows(top)
         st_ref[(par + 2) * n : (par + 3) * n] = lane_rows(sum_)
@@ -346,33 +349,41 @@
             ps.at[group, par], p_ref.at[group, par], sem.at[group * 2 + par]
         )
 
-    for par, keys in ((0, ka), (1, kb)):
-        w, top, sum_ = score(q, keys[...], bias, par)
-        ps[g, par] = w.astype(bf16)
-        out_copy(g, par).start()
-        top_o = column(st_ref[par * n : (par + 1) * n])
-        sum_o = column(st_ref[(par + 2) * n : (par + 3) * n])
-        most = jnp.maximum(top_o, top)
-        fs = [jnp.exp2((x - most) * c) for x in (top_o, top)]
-        inv = 1.0 / (fs[0] * sum_o + fs[1] * sum_)
-        for k in range(2):
-            f = fs[k] * inv
-            factors[:, k : k + 1] = f
-            f_ref[(2 * k + par) * n : (2 * k + par + 1) * n] = lane_rows(f)
+    some = SOME * GROUP
+    def head_sums(par):
         for r in range(0, GROUP, HEAD_ROWS):
+            to, row = r // t_ref.shape[1], r % t_ref.shape[1]
             at = 0
             for k, x in enumerate((po_ref.at[par], ps.at[g, par])):
                 wide = x.shape[1]
                 add = total[r : r + HEAD_ROWS, at : at + wide] if par else 0.0
                 for d in range(r, tall, GROUP):
-                    f = factors[d : d + HEAD_ROWS, k : k + 1]
+                    f = factors[par, d : d + HEAD_ROWS, k : k + 1]
                     add = add + x[d : d + HEAD_ROWS, :].astype(f32) * f
                 if par:
-                    to, row = r // t_ref.shape[1], r % t_ref.shape[1]
                     t_ref[to, row : row + HEAD_ROWS, at : at + wide] = add.astype(bf16)
                 else:
                     total[r : r + HEAD_ROWS, at : at + wide] = add
                 at += wide
+
+    for par, keys in ((0, ka), (1, kb)):
+        rows = head_rows(q, par)
+        for i in range(0, n, SOME):
+            here = slice(i * GROUP, i * GROUP + some)
+            w, top, sum_ = score(rows[here], keys[...], bias)
+            ps[g, par, here] = w.astype(bf16)
+            top_o = column(st_ref[par * n + i : par * n + i + SOME])
+            sum_o = column(st_ref[(par + 2) * n + i : (par + 2) * n + i + SOME])
+            most = jnp.maximum(top_o, top)
+            fs = [jnp.exp2((x - most) * c) for x in (top_o, top)]
+            inv = 1.0 / (fs[0] * sum_o + fs[1] * sum_)
+            for k in range(2):
+                f = fs[k] * inv
+                factors[par, here, k : k + 1] = f
+                at = (2 * k + par) * n + i
+                f_ref[at : at + SOME] = lane_rows(f)
+        out_copy(g, par).start()
+        head_sums(par)
 
     share = t_ref.shape[1]
     for to in range(t_ref.shape[0]):
@@ -418,7 +429,7 @@
             pltpu.VMEM((keys, KW), bf16),
             pltpu.VMEM((2, 2, tall, keys), bf16),
             pltpu.VMEM((GROUP, every), f32),
-            pltpu.VMEM((tall, GROUP), f32),
+            pltpu.VMEM((2, tall, GROUP), f32),
             pltpu.SemaphoreType.DMA((4,)),
         ],
         compiler_params=params(1),

time: 142 us -> 140 us (0.986)
  Pallas kernels: 76.5 us -> 74.5 us
    pallas_call x1, Pallas kernels: 25.7 us -> 23.7 us  [rest_stage(): pl.pallas_call(functools.partial(rest_kernel, len(pieces)), out_shape=(ja...]
where the time goes in v4:
time: 140 us
  Pallas kernels  74.5 us (53%)
  starting transfers between devices  41.9 us (30%)
  waiting for transfers between devices  17.6 us (13%)
  other arithmetic  2.57 us (2%)
  local copies, waits for them, and re-layouts  2.2 us (2%)
    pallas_call x1, Pallas kernels, rest_stage(): pl.pallas_call(functools.partial(rest_kernel, len(pieces)), out_shape=(ja...  23.7 us
    all_to_all x4, starting transfers between devices, swap(): return lax.all_to_all(x, axis, split_axis=0, concat_axis=0, tiled=True)  22.9 us
    all_to_all x4, waiting for transfers between devices, swap(): return lax.all_to_all(x, axis, split_axis=0, concat_axis=0, tiled=True)  17.6 us
    ppermute x4, starting transfers between devices, gather_head(): lax.ppermute(r, 'head', [(i, i ^ 1) for i in range(heads)])  14.6 us
    pallas_call x1, Pallas kernels, contexts(): pl.pallas_call(context_kernel, out_shape=jax.ShapeDtypeStruct((2 * GROUP,...  14.5 us
    pallas_call x1, Pallas kernels, index(): pl.pallas_call(index_kernel, out_shape=(jax.ShapeDtypeStruct((1, rows), f...  8.99 us
    pallas_call x1, Pallas kernels, own_rows(): pl.pallas_call(own_kernel, out_shape=(jax.ShapeDtypeStruct((2, OWN // 2,...  8.53 us
    pallas_call x1, Pallas kernels, own_stage(): pl.pallas_call(own_stage_kernel, out_shape=(jax.ShapeDtypeStruct((2, 2, t...  8.15 us
  transfers between devices with their start and end apart: 11, of which 3 were waited for; matrix products, arithmetic and copies ran while one was open for 3% of the time, Pallas kernels for 25%

profile of v4, /device:TPU:1, one launch (start us, length us, event | category | flops | bytes accessed | tf_op | source)
XLA Modules:
  0.0 139.7 jit_solution(6732294223075985371)
XLA Ops:
  0.6 1.7 %shard_map.112 = (s32[256,128]{1,0:T(8,128)}, s32[48]{0:T(128)}, s32[16]{0:T(128)}) custom-call(s32[1]{0:T(128)} %bitcast.1.me_ref, s32[2,32]{1,0:T(2,128)} %list_ref.1, s32[2]{0:T(128)} %len_ref.1), custom_call_target="tpu_custom_call" | custom-call | tf_op jit(solution)/shard_map/pallas_call | solution.py:105
  2.4 9.5 %all-to-all-start = ((s32[16,16,128]{2,1,0:T(8,128)}), s32[16,16,128]{2,1,0:T(8,128)S(1)}, u32[]{:S(2)}, u32[]{:S(2)}) async-start(s32[16,16,128]{2,1,0:T(8,128)} %bitcast.17), calls=%async_computation | async-start | bytes 262144 | tf_op jit(solution)/shard_map/all_to_all | solution.py:568
  11.9 6.9 %all-to-all-done = s32[16,16,128]{2,1,0:T(8,128)S(1)} async-done(((s32[16,16,128]{2,1,0:T(8,128)}), s32[16,16,128]{2,1,0:T(8,128)S(1)}, u32[]{:S(2)}, u32[]{:S(2)}) %all-to-all-start) | async-done | bytes 131104 | tf_op jit(solution)/shard_map/all_to_all | solution.py:568
  18.8 3.4 %shard_map.113 = bf16[256,4608]{1,0:T(8,128)(2,1)} custom-call(s32[1]{0:T(128)} %bitcast.h_ref, s32[256,128]{1,0:T(8,128)S(1)} %bitcast.13, bf16[128,36864]{1,0:T(8,128)(2,1)} %lat_ref.1), custom_call_target="tpu_custom_call" | custom-call | tf_op jit(solution)/shard_map/pallas_call | solution.py:127
  22.2 0.0 copy-start.7
  22.2 0.0 copy-start.6
  22.2 0.0 copy-start.8
  22.2 0.0 copy-start.9
  22.2 3.9 %all-to-all-start.1 = ((bf16[16,16,4608]{2,1,0:T(8,128)(2,1)}), bf16[16,16,4608]{2,1,0:T(8,128)(2,1)S(1)}, u32[]{:S(2)}, u32[]{:S(2)}) async-start(bf16[16,16,4608]{2,1,0:T(8,128)(2,1)} %bitcast.15), calls=%async_computation.1 | async-start | bytes 4718592 | tf_op jit(solution)/shard_map/all_to_all | solution.py:568
  26.1 0.0 copy-done.7
  26.1 0.1 mul.33
  26.2 0.1 mul.34
  26.3 0.0 copy-done.6
  26.3 0.1 select_n.51
  26.4 0.1 tile.7
  26.5 0.0 copy-done.8
  26.5 0.6 and_select_fusion.refs_0_
  27.1 0.0 copy-done.9
  27.2 0.1 iota_add_fusion
  27.2 0.9 compare_select_fusion.1.bias_ref
  28.1 2.0 %shard_map.114 = bf16[256,1024]{1,0:T(8,128)(2,1)} custom-call(s32[1]{0:T(128)} %bitcast.h_ref, s32[256,128]{1,0:T(8,128)S(1)} %bitcast.14, bf16[128,8192]{1,0:T(8,128)(2,1)} %key_ref.1), custom_call_target="tpu_custom_call" | custom-call | tf_op jit(solution)/shard_map/pallas_call | solution.py:127
  30.2 8.5 %shard_map.115 = (bf16[2,256,1152]{2,1,0:T(8,128)(2,1)}, bf16[2,2,256,128]{3,2,1,0:T(8,128)(2,1)}) custom-call(s32[16]{0:T(128)} %get-tuple-element.29.idx_ref, bf16[128,36864]{1,0:T(8,128)(2,1)} %lat_ref.1, bf16[128,8192]{1,0:T(8,128)(2,1)} %key_ref.1), custom_call_target="tpu_custom_call" | custom-call | tf_op jit(solution)/shard_map/pallas_call | solution.py:171
  38.7 8.1 %shard_map.116 = (bf16[2,2,1024,512]{3,2,1,0:T(8,128)(2,1)}, f32[2,32,128]{2,1,0:T(8,128)}, bf16[2,512,512]{2,1,0:T(8,128)(2,1)}) custom-call(bf16[256,9216]{1,0:T(8,128)(2,1)} %refs_1_.1, bf16[2,256,1152]{2,1,0:T(8,128)(2,1)} %get-tuple-element.30.own_ref, f32[2,128,512]{2,1,0:T(8,128)} %compare_select_fusion.1.bias_ref), custom_call_target="tpu_custom_call" | custom-call | tf_op jit(solution)/shard_map/pallas_call | solution.py:313
  46.9 7.4 %all-to-all-done.1 = bf16[16,16,4608]{2,1,0:T(8,128)(2,1)S(1)} async-done(((bf16[16,16,4608]{2,1,0:T(8,128)(2,1)}), bf16[16,16,4608]{2,1,0:T(8,128)(2,1)S(1)}, u32[]{:S(2)}, u32[]{:S(2)}) %all-to-all-start.1) | async-done | bytes 2359328 | tf_op jit(solution)/shard_map/all_to_all | solution.py:568
  54.2 1.9 %shard_map.117.refs_2_ = bf16[2,96,1152]{2,1,0:T(8,128)(2,1)} custom-call(s32[48]{0:T(128)} %get-tuple-element.26.idx_ref, bf16[256,4608]{1,0:T(8,128)(2,1)S(1)} %bitcast.11), custom_call_target="tpu_custom_call" | custom-call | tf_op jit(solution)/shard_map/pallas_call | solution.py:202
  56.1 1.3 collective-permute-start
  57.4 1.4 %collective-permute-start.1 = (bf16[2,96,1152]{2,1,0:T(8,128)(2,1)}, bf16[2,96,1152]{2,1,0:T(8,128)(2,1)S(1)}, u32[]{:S(2)}, u32[]{:S(2)}) collective-permute-start(bf16[2,96,1152]{2,1,0:T(8,128)(2,1)} %shard_map.117.refs_2_), channel_id=1, source_target_pairs={{0,6},{1,7},{2,0},{3,1},{4,2},{5,3},{6,4},{7,5},{8,14},{9,15},{10,... | collective-permute-start | bytes 1327112 | tf_op jit(solution)/shard_map/ppermute | solution.py:558
  58.9 1.6 %collective-permute-start.2 = (bf16[2,96,1152]{2,1,0:T(8,128)(2,1)}, bf16[2,96,1152]{2,1,0:T(8,128)(2,1)S(1)}, u32[]{:S(2)}, u32[]{:S(2)}) collective-permute-start(bf16[2,96,1152]{2,1,0:T(8,128)(2,1)} %shard_map.117.refs_2_), channel_id=1, source_target_pairs={{0,4},{1,5},{2,6},{3,7},{4,0},{5,1},{6,2},{7,3},{8,12},{9,13},{10,... | collective-permute-start | bytes 1327112 | tf_op jit(solution)/shard_map/ppermute | solution.py:558
  60.5 5.7 %all-to-all-start.2 = ((bf16[16,16,1024]{2,1,0:T(8,128)(2,1)}), bf16[16,16,1024]{2,1,0:T(8,128)(2,1)S(1)}, u32[]{:S(2)}, u32[]{:S(2)}) async-start(bf16[16,16,1024]{2,1,0:T(8,128)(2,1)} %bitcast.6), calls=%async_computation.2 | async-start | bytes 1048576 | tf_op jit(solution)/shard_map/all_to_all | solution.py:568
  66.3 4.7 %collective-permute-start.3 = (bf16[2,96,1152]{2,1,0:T(8,128)(2,1)}, bf16[2,96,1152]{2,1,0:T(8,128)(2,1)S(1)}, u32[]{:S(2)}, u32[]{:S(2)}) collective-permute-start(bf16[2,96,1152]{2,1,0:T(8,128)(2,1)} %shard_map.117.refs_2_), channel_id=1, source_target_pairs={{0,1},{1,0},{2,3},{3,2},{4,5},{5,4},{6,7},{7,6},{8,9},{9,8},{10,11... | collective-permute-start | bytes 1327112 | tf_op jit(solution)/shard_map/ppermute | solution.py:559
  70.9 0.0 collective-permute-done.refs_3_
  70.9 0.0 copy-start
  70.9 5.2 %collective-permute-start.4 = (bf16[2,96,1152]{2,1,0:T(8,128)(2,1)S(1)}, bf16[2,96,1152]{2,1,0:T(8,128)(2,1)S(1)}, u32[]{:S(2)}, u32[]{:S(2)}) collective-permute-start(bf16[2,96,1152]{2,1,0:T(8,128)(2,1)S(1)} %collective-permute-done.refs_3_), channel_id=1, source_target_pairs={{0,1},{1,0},{2,3},{3,2},{4,5},{5,4},{6,7},{7,6},{8,9},{9,8},{10,11... | collective-permute-start | bytes 1327112 | tf_op jit(solution)/shard_map/ppermute | solution.py:559
  76.1 0.0 collective-permute-done.1.refs_4_
  76.1 0.0 copy-start.1
  76.1 0.1 collective-permute-start.5
  76.2 0.0 collective-permute-done.2.refs_5_
  76.2 0.0 copy-start.2
  76.2 4.7 %collective-permute-start.6 = (bf16[2,96,1152]{2,1,0:T(8,128)(2,1)S(1)}, bf16[2,96,1152]{2,1,0:T(8,128)(2,1)}, u32[]{:S(2)}, u32[]{:S(2)}) collective-permute-start(bf16[2,96,1152]{2,1,0:T(8,128)(2,1)S(1)} %collective-permute-done.2.refs_5_), channel_id=1, source_target_pairs={{0,1},{1,0},{2,3},{3,2},{4,5},{5,4},{6,7},{7,6},{8,9},{9,8},{10,11... | collective-permute-start | bytes 1327112 | tf_op jit(solution)/shard_map/ppermute | solution.py:559
  80.9 0.6 copy.12.refs_10_.bias_rem
  81.5 0.0 all-to-all-done.2
  81.5 1.5 %shard_map.118.refs_13_ = bf16[2,192,128]{2,1,0:T(8,128)(2,1)} custom-call(s32[48]{0:T(128)} %get-tuple-element.26.idx_ref, bf16[256,1024]{1,0:T(8,128)(2,1)S(1)} %bitcast.12), custom_call_target="tpu_custom_call" | custom-call | tf_op jit(solution)/shard_map/pallas_call | solution.py:229
  83.1 0.0 collective-permute-done.3.refs_6_
  83.1 0.0 copy-start.3
  83.1 0.0 collective-permute-done.4.refs_7_
  83.1 0.0 copy-start.4
  83.1 0.0 collective-permute-done.5.refs_8_
  83.1 0.0 copy-start.5
  83.1 0.0 collective-permute-done.6.refs_9_
  83.1 0.0 copy-done
  83.1 0.0 copy-done.1
  83.1 0.0 copy-done.2
  83.1 0.7 copy-done.3
  83.8 0.1 copy-done.4
  84.0 0.2 copy-done.5
  84.1 23.7 %shard_map.119 = (bf16[2,2,1024,1536]{3,2,1,0:T(8,128)(2,1)}, f32[2,32,128]{2,1,0:T(8,128)}, bf16[2,1536,512]{2,1,0:T(8,128)(2,1)}, bf16[8,32,2816]{2,1,0:T(8,128)(2,1)}) custom-call(s32[8]{0:T(128)} %and_select_fusion.refs_0_, bf16[256,9216]{1,0:T(8,128)(2,1)} %refs_1_.1, bf16[2,96,1152]{2,1,0:T(8,128)(2,1)} %shard_map.117.refs_2_, ...), custom_call_target="tpu_custom_call" | custom-call | tf_op jit(solution)/shard_map/pallas_call | solution.py:408
  107.8 3.8 %all-to-all-start.3 = ((bf16[8,32,2816]{2,1,0:T(8,128)(2,1)}), bf16[8,32,2816]{2,1,0:T(8,128)(2,1)S(1)}, u32[]{:S(2)}, u32[]{:S(2)}) async-start(bf16[8,32,2816]{2,1,0:T(8,128)(2,1)} %get-tuple-element.38), calls=%async_computation.3 | async-start | bytes 2883584 | tf_op jit(solution)/shard_map/all_to_all | solution.py:568
  111.6 0.1 add.117
  111.7 0.1 add.118
  111.8 0.1 broadcast_add_fusion
  111.9 0.9 compare_select_fusion.bias_own
  112.8 14.5 %shard_map.120 = bf16[256,8192]{1,0:T(8,128)(2,1)} custom-call(f32[2,32,128]{2,1,0:T(8,128)} %get-tuple-element.39.f_ref, bf16[2,2,1024,512]{3,2,1,0:T(8,128)(2,1)} %get-tuple-element.31.refs_11_.po_ref, bf16[2,2,1024,1536]{3,2,1,0:T(8,128)(2,1)} %get-tuple-element.40.pr_ref, bf16[2,512,512]{2,1,0:T(8,128)(2,1)} %get-tuple-element.41.vo_ref, ...), custom_call_target="tpu_custom_call" | custom-call | tf_op jit(solution)/shard_map/pallas_call | solution.py:454
  127.3 3.4 %all-to-all-done.3.part_ref = bf16[8,32,2816]{2,1,0:T(8,128)(2,1)S(1)} async-done(((bf16[8,32,2816]{2,1,0:T(8,128)(2,1)}), bf16[8,32,2816]{2,1,0:T(8,128)(2,1)S(1)}, u32[]{:S(2)}, u32[]{:S(2)}) %all-to-all-start.3) | async-done | bytes 1441824 | tf_op jit(solution)/shard_map/all_to_all | solution.py:568
  130.7 9.0 %shard_map.121 = (f32[1,32]{1,0:T(1,128)}, f32[32,8192]{1,0:T(8,128)}) custom-call(s32[1]{0:T(128)} %bitcast.h_ref, bf16[32,8192]{1,0:T(8,128)(2,1)} %iq_ref.1, f32[32,64]{1,0:T(8,128)} %w_ref.1, bf16[2,512,128]{2,1,0:T(8,128)(2,1)} %bitcast.16, bf16[8,32,2816]{2,1,0:T(8,128)(2,1)S(1)} %all-to-all-done.3.part_ref, ...), custom_call_target="tpu_custom_call" | custom-call | tf_op jit(solution)/shard_map/pallas_call | solution.py:528
  (11 shorter events, 0.1 us)
Async XLA Ops:
  2.4 16.4 %all-to-all-start = ((s32[16,16,128]{2,1,0:T(8,128)}), s32[16,16,128]{2,1,0:T(8,128)S(1)}, u32[]{:S(2)}, u32[]{:S(2)}) async-start(s32[16,16,128]{2,1,0:T(8,128)} %bitcast.17), calls=%async_computation | async-start | bytes 262144 | tf_op jit(solution)/shard_map/all_to_all | solution.py:568
  22.2 3.9 %copy-start.7 = (s32[16]{0:T(128)S(1)}, s32[16]{0:T(128)}, u32[]{:S(2)}) copy-start(s32[16]{0:T(128)} %get-tuple-element.29.idx_ref) | copy-start | bytes 196
  22.2 4.1 %copy-start.6 = (s32[48]{0:T(128)S(1)}, s32[48]{0:T(128)}, u32[]{:S(2)}) copy-start(s32[48]{0:T(128)} %get-tuple-element.26.idx_ref) | copy-start | bytes 580
  22.2 4.3 %copy-start.8 = (s32[4]{0:T(128)S(1)}, s32[4]{0:T(128)}, u32[]{:S(2)}) copy-start(s32[4]{0:T(128)} %constant.85) | copy-start | bytes 52
  22.2 4.9 %copy-start.9 = (s32[2]{0:T(128)S(1)}, s32[2]{0:T(128)}, u32[]{:S(2)}) copy-start(s32[2]{0:T(128)} %param.16) | copy-start | bytes 28
  22.2 32.0 %all-to-all-start.1 = ((bf16[16,16,4608]{2,1,0:T(8,128)(2,1)}), bf16[16,16,4608]{2,1,0:T(8,128)(2,1)S(1)}, u32[]{:S(2)}, u32[]{:S(2)}) async-start(bf16[16,16,4608]{2,1,0:T(8,128)(2,1)} %bitcast.15), calls=%async_computation.1 | async-start | bytes 4718592 | tf_op jit(solution)/shard_map/all_to_all | solution.py:568
  56.1 14.8 %collective-permute-start = (bf16[2,96,1152]{2,1,0:T(8,128)(2,1)}, bf16[2,96,1152]{2,1,0:T(8,128)(2,1)S(1)}, u32[]{:S(2)}, u32[]{:S(2)}) collective-permute-start(bf16[2,96,1152]{2,1,0:T(8,128)(2,1)} %shard_map.117.refs_2_), channel_id=1, source_target_pairs={{0,2},{1,3},{2,4},{3,5},{4,6},{5,7},{6,0},{7,1},{8,10},{9,11},{10,... | collective-permute-start | bytes 1327112 | tf_op jit(solution)/shard_map/ppermute | solution.py:558
  57.4 18.7 %collective-permute-start.1 = (bf16[2,96,1152]{2,1,0:T(8,128)(2,1)}, bf16[2,96,1152]{2,1,0:T(8,128)(2,1)S(1)}, u32[]{:S(2)}, u32[]{:S(2)}) collective-permute-start(bf16[2,96,1152]{2,1,0:T(8,128)(2,1)} %shard_map.117.refs_2_), channel_id=1, source_target_pairs={{0,6},{1,7},{2,0},{3,1},{4,2},{5,3},{6,4},{7,5},{8,14},{9,15},{10,... | collective-permute-start | bytes 1327112 | tf_op jit(solution)/shard_map/ppermute | solution.py:558
  58.9 17.3 %collective-permute-start.2 = (bf16[2,96,1152]{2,1,0:T(8,128)(2,1)}, bf16[2,96,1152]{2,1,0:T(8,128)(2,1)S(1)}, u32[]{:S(2)}, u32[]{:S(2)}) collective-permute-start(bf16[2,96,1152]{2,1,0:T(8,128)(2,1)} %shard_map.117.refs_2_), channel_id=1, source_target_pairs={{0,4},{1,5},{2,6},{3,7},{4,0},{5,1},{6,2},{7,3},{8,12},{9,13},{10,... | collective-permute-start | bytes 1327112 | tf_op jit(solution)/shard_map/ppermute | solution.py:558
  60.5 21.0 %all-to-all-start.2 = ((bf16[16,16,1024]{2,1,0:T(8,128)(2,1)}), bf16[16,16,1024]{2,1,0:T(8,128)(2,1)S(1)}, u32[]{:S(2)}, u32[]{:S(2)}) async-start(bf16[16,16,1024]{2,1,0:T(8,128)(2,1)} %bitcast.6), calls=%async_computation.2 | async-start | bytes 1048576 | tf_op jit(solution)/shard_map/all_to_all | solution.py:568
  66.3 16.8 %collective-permute-start.3 = (bf16[2,96,1152]{2,1,0:T(8,128)(2,1)}, bf16[2,96,1152]{2,1,0:T(8,128)(2,1)S(1)}, u32[]{:S(2)}, u32[]{:S(2)}) collective-permute-start(bf16[2,96,1152]{2,1,0:T(8,128)(2,1)} %shard_map.117.refs_2_), channel_id=1, source_target_pairs={{0,1},{1,0},{2,3},{3,2},{4,5},{5,4},{6,7},{7,6},{8,9},{9,8},{10,11... | collective-permute-start | bytes 1327112 | tf_op jit(solution)/shard_map/ppermute | solution.py:559
  70.9 12.2 %copy-start = (bf16[2,96,1152]{2,1,0:T(8,128)(2,1)}, bf16[2,96,1152]{2,1,0:T(8,128)(2,1)S(1)}, u32[]{:S(2)}) copy-start(bf16[2,96,1152]{2,1,0:T(8,128)(2,1)S(1)} %collective-permute-done.refs_3_) | copy-start | bytes 1327108
  70.9 12.1 %collective-permute-start.4 = (bf16[2,96,1152]{2,1,0:T(8,128)(2,1)S(1)}, bf16[2,96,1152]{2,1,0:T(8,128)(2,1)S(1)}, u32[]{:S(2)}, u32[]{:S(2)}) collective-permute-start(bf16[2,96,1152]{2,1,0:T(8,128)(2,1)S(1)} %collective-permute-done.refs_3_), channel_id=1, source_target_pairs={{0,1},{1,0},{2,3},{3,2},{4,5},{5,4},{6,7},{7,6},{8,9},{9,8},{10,11... | collective-permute-start | bytes 1327112 | tf_op jit(solution)/shard_map/ppermute | solution.py:559
  76.1 7.0 %copy-start.1 = (bf16[2,96,1152]{2,1,0:T(8,128)(2,1)}, bf16[2,96,1152]{2,1,0:T(8,128)(2,1)S(1)}, u32[]{:S(2)}) copy-start(bf16[2,96,1152]{2,1,0:T(8,128)(2,1)S(1)} %collective-permute-done.1.refs_4_) | copy-start | bytes 1327108
  76.1 7.0 %collective-permute-start.5 = (bf16[2,96,1152]{2,1,0:T(8,128)(2,1)S(1)}, bf16[2,96,1152]{2,1,0:T(8,128)(2,1)S(1)}, u32[]{:S(2)}, u32[]{:S(2)}) collective-permute-start(bf16[2,96,1152]{2,1,0:T(8,128)(2,1)S(1)} %collective-permute-done.1.refs_4_), channel_id=1, source_target_pairs={{0,1},{1,0},{2,3},{3,2},{4,5},{5,4},{6,7},{7,6},{8,9},{9,8},{10,11... | collective-permute-start | bytes 1327112 | tf_op jit(solution)/shard_map/ppermute | solution.py:559
  76.2 6.9 %copy-start.2 = (bf16[2,96,1152]{2,1,0:T(8,128)(2,1)}, bf16[2,96,1152]{2,1,0:T(8,128)(2,1)S(1)}, u32[]{:S(2)}) copy-start(bf16[2,96,1152]{2,1,0:T(8,128)(2,1)S(1)} %collective-permute-done.2.refs_5_) | copy-start | bytes 1327108
  76.2 6.9 %collective-permute-start.6 = (bf16[2,96,1152]{2,1,0:T(8,128)(2,1)S(1)}, bf16[2,96,1152]{2,1,0:T(8,128)(2,1)}, u32[]{:S(2)}, u32[]{:S(2)}) collective-permute-start(bf16[2,96,1152]{2,1,0:T(8,128)(2,1)S(1)} %collective-permute-done.2.refs_5_), channel_id=1, source_target_pairs={{0,1},{1,0},{2,3},{3,2},{4,5},{5,4},{6,7},{7,6},{8,9},{9,8},{10,11... | collective-permute-start | bytes 1327112 | tf_op jit(solution)/shard_map/ppermute | solution.py:559
  83.1 0.8 copy-start.3
  83.1 0.9 copy-start.4
  83.1 1.1 copy-start.5
  107.8 22.8 %all-to-all-start.3 = ((bf16[8,32,2816]{2,1,0:T(8,128)(2,1)}), bf16[8,32,2816]{2,1,0:T(8,128)(2,1)S(1)}, u32[]{:S(2)}, u32[]{:S(2)}) async-start(bf16[8,32,2816]{2,1,0:T(8,128)(2,1)} %get-tuple-element.38), calls=%async_computation.3 | async-start | bytes 2883584 | tf_op jit(solution)/shard_map/all_to_all | solution.py:568

commit v5 on v4

--- a/solution.py
+++ b/solution.py
@@ -123,18 +123,19 @@
 
 def send(h, asked, x, heads, part, parts):
     rows, blocks = asked.shape
-    width = x.shape[1] // heads // parts
+    steps = 2
+    width = x.shape[1] // heads // parts // steps
     return pl.pallas_call(
         send_kernel,
-        out_shape=jax.ShapeDtypeStruct((rows, width), bf16),
+        out_shape=jax.ShapeDtypeStruct((rows, width * steps), bf16),
         grid_spec=pltpu.PrefetchScalarGridSpec(
             num_scalar_prefetch=1,
-            grid=(1,),
+            grid=(steps,),
             in_specs=[
                 pl.BlockSpec((rows, blocks), lambda c, h: (0, 0)),
-                pl.BlockSpec((blocks, width), lambda c, h: (0, h[0] * parts + part)),
+                pl.BlockSpec((blocks, width), lambda c, h: (0, (h[0] * parts + part) * steps + c)),
             ],
-            out_specs=pl.BlockSpec((rows, width), lambda c, h: (0, 0)),
+            out_specs=pl.BlockSpec((rows, width), lambda c, h: (0, c)),
         ),
         compiler_params=params(),
     )(h, near(asked), far(x))
@@ -339,7 +340,7 @@
         at = pl.multiple_of(src_ref[k] * (2 * rows), 2 * rows)
         place_keys(piece[g], ka, kb, at, rows)
     v_ref[...] = ka[:, :LAT]
-    q, bias = q_ref[...], bias_ref[...]
+    q, bias = q_ref[...], bias_ref[0:1]
     n = st_ref.shape[0] // 4
     tall = n * GROUP
     c = SCALE * LOG2E
@@ -416,7 +417,7 @@
         grid=(2,),
         in_specs=[smem(), rows_spec(q.shape[1])]
         + [vmem() for x in pieces]
-        + [group_spec(1, keys), group_spec(2, tall, OWN), group_spec(2 * heads, GROUP)]
+        + [group_spec(8, keys), group_spec(2, tall, OWN), group_spec(2 * heads, GROUP)]
         + [group_spec(*rem_key.shape[1:])],
         out_specs=(
             anywhere(),
@@ -488,7 +489,7 @@
             sum_ = sum_ + jnp.maximum(act[n * rows : (n + 1) * rows], 0.0) * w_ref[:, j : j + 1]
     logits = sum_ * INDEX_SCALE
     logits = jnp.concatenate(
-        [logits[:, :OWN] + bias_own[...], logits[:, OWN:] + bias_rem[...]], 1
+        [logits[:, :OWN] + bias_own[...], logits[:, OWN:] + bias_rem[0:1]], 1
     )
     top = jnp.max(logits, -1, keepdims=True)
     shifted = logits - top
@@ -540,7 +541,7 @@
                 pl.BlockSpec((None, OWN, ID), group),
                 pl.BlockSpec(parts.shape, lambda c, h: (0, 0, 0)),
                 pl.BlockSpec((None, rows, OWN), lambda c, h: (h[0], 0, 0)),
-                pl.BlockSpec((None, 1, keys - OWN), group),
+                pl.BlockSpec((None, 8, keys - OWN), group),
             ],
             out_specs=(pl.BlockSpec((1, rows), flat), pl.BlockSpec((rows, IH * ID), flat)),
             scratch_shapes=[
@@ -592,7 +593,8 @@
     row_pos = start[:, None] + jnp.arange(GROUP, dtype=i32)[None, :]
     bias_own = jnp.where(key_pos[:, None, :] <= row_pos[:, :, None], 0.0, NEG).astype(f32)
     used = jnp.where(place.reshape(2, REM) >= 0, 0.0, NEG).astype(f32)
-    bias_rem = jnp.tile(used, (1, BLK // PARTS))[:, None, :]
+    bias_rem = jnp.tile(used, (1, BLK // PARTS))
+    bias_rem = jnp.broadcast_to(bias_rem[:, None, :], (2, 8, bias_rem.shape[1]))
 
     own = own_stage(query, own_lat, bias_own)
     back = jnp.array([0, 2, heads - 2, 4], i32)

time: 140 us -> 140 us (level)
  transfers between devices with their start and end apart: 11 -> 11, of which waited for: 3 -> 3; matrix products, arithmetic and copies ran while one was open for 3% -> 2% of each run, Pallas kernels for 25% -> 25%
where the time goes in v5:
time: 140 us; the launch traced here: 139 us
  Pallas kernels  74.1 us (53%)
  starting transfers between devices  41.7 us (30%)
  waiting for transfers between devices  17.6 us (13%)
  other arithmetic  2.57 us (2%)
  local copies, waits for them, and re-layouts  2.23 us (2%)
    pallas_call x1, Pallas kernels, rest_stage(): pl.pallas_call(functools.partial(rest_kernel, len(pieces)), out_shape=(ja...  23.7 us
    all_to_all x4, starting transfers between devices, swap(): return lax.all_to_all(x, axis, split_axis=0, concat_axis=0, tiled=True)  22.7 us
    all_to_all x4, waiting for transfers between devices, swap(): return lax.all_to_all(x, axis, split_axis=0, concat_axis=0, tiled=True)  17.6 us
    ppermute x4, starting transfers between devices, gather_head(): lax.ppermute(r, 'head', [(i, i ^ 1) for i in range(heads)])  14.6 us
    pallas_call x1, Pallas kernels, contexts(): pl.pallas_call(context_kernel, out_shape=jax.ShapeDtypeStruct((2 * GROUP,...  14.5 us
    pallas_call x1, Pallas kernels, index(): pl.pallas_call(index_kernel, out_shape=(jax.ShapeDtypeStruct((1, rows), f...  9.01 us
    pallas_call x1, Pallas kernels, own_rows(): pl.pallas_call(own_kernel, out_shape=(jax.ShapeDtypeStruct((2, OWN // 2,...  8.53 us
    pallas_call x1, Pallas kernels, own_stage(): pl.pallas_call(own_stage_kernel, out_shape=(jax.ShapeDtypeStruct((2, 2, t...  8.15 us
  transfers between devices with their start and end apart: 11, of which 3 were waited for; matrix products, arithmetic and copies ran while one was open for 2% of the time, Pallas kernels for 25%

profile of v5, /device:TPU:1, one launch (start us, length us, event | category | flops | bytes accessed | tf_op | source)
XLA Modules:
  0.0 139.1 jit_solution(17136722018602726644)
XLA Ops:
  0.6 1.7 %shard_map.112 = (s32[256,128]{1,0:T(8,128)}, s32[48]{0:T(128)}, s32[16]{0:T(128)}) custom-call(s32[1]{0:T(128)} %bitcast.1.me_ref, s32[2,32]{1,0:T(2,128)} %list_ref.1, s32[2]{0:T(128)} %len_ref.1), custom_call_target="tpu_custom_call" | custom-call | tf_op jit(solution)/shard_map/pallas_call | solution.py:105
  2.4 9.4 %all-to-all-start = ((s32[16,16,128]{2,1,0:T(8,128)}), s32[16,16,128]{2,1,0:T(8,128)S(1)}, u32[]{:S(2)}, u32[]{:S(2)}) async-start(s32[16,16,128]{2,1,0:T(8,128)} %bitcast.17), calls=%async_computation | async-start | bytes 262144 | tf_op jit(solution)/shard_map/all_to_all | solution.py:569
  11.8 6.9 %all-to-all-done = s32[16,16,128]{2,1,0:T(8,128)S(1)} async-done(((s32[16,16,128]{2,1,0:T(8,128)}), s32[16,16,128]{2,1,0:T(8,128)S(1)}, u32[]{:S(2)}, u32[]{:S(2)}) %all-to-all-start) | async-done | bytes 131104 | tf_op jit(solution)/shard_map/all_to_all | solution.py:569
  18.6 3.0 %shard_map.113 = bf16[256,4608]{1,0:T(8,128)(2,1)} custom-call(s32[1]{0:T(128)} %bitcast.h_ref, s32[256,128]{1,0:T(8,128)S(1)} %bitcast.13, bf16[128,36864]{1,0:T(8,128)(2,1)} %lat_ref.1), custom_call_target="tpu_custom_call" | custom-call | tf_op jit(solution)/shard_map/pallas_call | solution.py:128
  21.6 0.0 copy-start.7
  21.6 0.0 copy-start.6
  21.6 0.0 copy-start.8
  21.6 0.0 copy-start.9
  21.6 3.9 %all-to-all-start.1 = ((bf16[16,16,4608]{2,1,0:T(8,128)(2,1)}), bf16[16,16,4608]{2,1,0:T(8,128)(2,1)S(1)}, u32[]{:S(2)}, u32[]{:S(2)}) async-start(bf16[16,16,4608]{2,1,0:T(8,128)(2,1)} %bitcast.15), calls=%async_computation.1 | async-start | bytes 4718592 | tf_op jit(solution)/shard_map/all_to_all | solution.py:569
  25.5 0.0 copy-done.7
  25.5 0.1 mul.33
  25.6 0.1 mul.34
  25.7 0.0 copy-done.6
  25.8 0.1 select_n.51
  25.9 0.1 tile.7
  26.0 0.0 copy-done.8
  26.0 0.6 and_select_fusion.refs_0_
  26.6 0.0 copy-done.9
  26.6 0.1 iota_add_fusion
  26.7 0.9 compare_select_fusion.1.bias_ref
  27.6 2.1 %shard_map.114 = bf16[256,1024]{1,0:T(8,128)(2,1)} custom-call(s32[1]{0:T(128)} %bitcast.h_ref, s32[256,128]{1,0:T(8,128)S(1)} %bitcast.14, bf16[128,8192]{1,0:T(8,128)(2,1)} %key_ref.1), custom_call_target="tpu_custom_call" | custom-call | tf_op jit(solution)/shard_map/pallas_call | solution.py:128
  29.6 8.5 %shard_map.115 = (bf16[2,256,1152]{2,1,0:T(8,128)(2,1)}, bf16[2,2,256,128]{3,2,1,0:T(8,128)(2,1)}) custom-call(s32[16]{0:T(128)} %get-tuple-element.29.idx_ref, bf16[128,36864]{1,0:T(8,128)(2,1)} %lat_ref.1, bf16[128,8192]{1,0:T(8,128)(2,1)} %key_ref.1), custom_call_target="tpu_custom_call" | custom-call | tf_op jit(solution)/shard_map/pallas_call | solution.py:172
  38.2 8.2 %shard_map.116 = (bf16[2,2,1024,512]{3,2,1,0:T(8,128)(2,1)}, f32[2,32,128]{2,1,0:T(8,128)}, bf16[2,512,512]{2,1,0:T(8,128)(2,1)}) custom-call(bf16[256,9216]{1,0:T(8,128)(2,1)} %refs_1_.1, bf16[2,256,1152]{2,1,0:T(8,128)(2,1)} %get-tuple-element.30.own_ref, f32[2,128,512]{2,1,0:T(8,128)} %compare_select_fusion.1.bias_ref), custom_call_target="tpu_custom_call" | custom-call | tf_op jit(solution)/shard_map/pallas_call | solution.py:314
  46.3 7.4 %all-to-all-done.1 = bf16[16,16,4608]{2,1,0:T(8,128)(2,1)S(1)} async-done(((bf16[16,16,4608]{2,1,0:T(8,128)(2,1)}), bf16[16,16,4608]{2,1,0:T(8,128)(2,1)S(1)}, u32[]{:S(2)}, u32[]{:S(2)}) %all-to-all-start.1) | async-done | bytes 2359328 | tf_op jit(solution)/shard_map/all_to_all | solution.py:569
  53.7 0.6 broadcast_in_dim.32.refs_10_.bias_rem
  54.3 1.9 %shard_map.117.refs_2_ = bf16[2,96,1152]{2,1,0:T(8,128)(2,1)} custom-call(s32[48]{0:T(128)} %get-tuple-element.26.idx_ref, bf16[256,4608]{1,0:T(8,128)(2,1)S(1)} %bitcast.11), custom_call_target="tpu_custom_call" | custom-call | tf_op jit(solution)/shard_map/pallas_call | solution.py:203
  56.2 1.3 collective-permute-start
  57.5 1.4 %collective-permute-start.1 = (bf16[2,96,1152]{2,1,0:T(8,128)(2,1)}, bf16[2,96,1152]{2,1,0:T(8,128)(2,1)S(1)}, u32[]{:S(2)}, u32[]{:S(2)}) collective-permute-start(bf16[2,96,1152]{2,1,0:T(8,128)(2,1)} %shard_map.117.refs_2_), channel_id=1, source_target_pairs={{0,6},{1,7},{2,0},{3,1},{4,2},{5,3},{6,4},{7,5},{8,14},{9,15},{10,... | collective-permute-start | bytes 1327112 | tf_op jit(solution)/shard_map/ppermute | solution.py:559
  59.0 1.6 %collective-permute-start.2 = (bf16[2,96,1152]{2,1,0:T(8,128)(2,1)}, bf16[2,96,1152]{2,1,0:T(8,128)(2,1)S(1)}, u32[]{:S(2)}, u32[]{:S(2)}) collective-permute-start(bf16[2,96,1152]{2,1,0:T(8,128)(2,1)} %shard_map.117.refs_2_), channel_id=1, source_target_pairs={{0,4},{1,5},{2,6},{3,7},{4,0},{5,1},{6,2},{7,3},{8,12},{9,13},{10,... | collective-permute-start | bytes 1327112 | tf_op jit(solution)/shard_map/ppermute | solution.py:559
  60.6 5.7 %all-to-all-start.2 = ((bf16[16,16,1024]{2,1,0:T(8,128)(2,1)}), bf16[16,16,1024]{2,1,0:T(8,128)(2,1)S(1)}, u32[]{:S(2)}, u32[]{:S(2)}) async-start(bf16[16,16,1024]{2,1,0:T(8,128)(2,1)} %bitcast.6), calls=%async_computation.2 | async-start | bytes 1048576 | tf_op jit(solution)/shard_map/all_to_all | solution.py:569
  66.3 4.6 %collective-permute-start.3 = (bf16[2,96,1152]{2,1,0:T(8,128)(2,1)}, bf16[2,96,1152]{2,1,0:T(8,128)(2,1)S(1)}, u32[]{:S(2)}, u32[]{:S(2)}) collective-permute-start(bf16[2,96,1152]{2,1,0:T(8,128)(2,1)} %shard_map.117.refs_2_), channel_id=1, source_target_pairs={{0,1},{1,0},{2,3},{3,2},{4,5},{5,4},{6,7},{7,6},{8,9},{9,8},{10,11... | collective-permute-start | bytes 1327112 | tf_op jit(solution)/shard_map/ppermute | solution.py:560
  71.0 0.0 collective-permute-done.refs_3_
  71.0 0.0 copy-start
  71.0 5.2 %collective-permute-start.4 = (bf16[2,96,1152]{2,1,0:T(8,128)(2,1)S(1)}, bf16[2,96,1152]{2,1,0:T(8,128)(2,1)S(1)}, u32[]{:S(2)}, u32[]{:S(2)}) collective-permute-start(bf16[2,96,1152]{2,1,0:T(8,128)(2,1)S(1)} %collective-permute-done.refs_3_), channel_id=1, source_target_pairs={{0,1},{1,0},{2,3},{3,2},{4,5},{5,4},{6,7},{7,6},{8,9},{9,8},{10,11... | collective-permute-start | bytes 1327112 | tf_op jit(solution)/shard_map/ppermute | solution.py:560
  76.2 0.0 collective-permute-done.1.refs_4_
  76.2 0.0 copy-start.1
  76.2 0.1 collective-permute-start.5
  76.3 0.0 collective-permute-done.2.refs_5_
  76.3 0.0 copy-start.2
  76.3 4.7 %collective-permute-start.6 = (bf16[2,96,1152]{2,1,0:T(8,128)(2,1)S(1)}, bf16[2,96,1152]{2,1,0:T(8,128)(2,1)}, u32[]{:S(2)}, u32[]{:S(2)}) collective-permute-start(bf16[2,96,1152]{2,1,0:T(8,128)(2,1)S(1)} %collective-permute-done.2.refs_5_), channel_id=1, source_target_pairs={{0,1},{1,0},{2,3},{3,2},{4,5},{5,4},{6,7},{7,6},{8,9},{9,8},{10,11... | collective-permute-start | bytes 1327112 | tf_op jit(solution)/shard_map/ppermute | solution.py:560
  81.0 0.0 all-to-all-done.2
  81.0 1.5 %shard_map.118.refs_13_ = bf16[2,192,128]{2,1,0:T(8,128)(2,1)} custom-call(s32[48]{0:T(128)} %get-tuple-element.26.idx_ref, bf16[256,1024]{1,0:T(8,128)(2,1)S(1)} %bitcast.12), custom_call_target="tpu_custom_call" | custom-call | tf_op jit(solution)/shard_map/pallas_call | solution.py:230
  82.5 0.0 collective-permute-done.3.refs_6_
  82.5 0.0 copy-start.3
  82.5 0.0 collective-permute-done.4.refs_7_
  82.5 0.0 copy-start.4
  82.5 0.0 collective-permute-done.5.refs_8_
  82.5 0.0 copy-start.5
  82.6 0.0 collective-permute-done.6.refs_9_
  82.6 0.0 copy-done
  82.6 0.0 copy-done.1
  82.6 0.0 copy-done.2
  82.6 0.7 copy-done.3
  83.3 0.1 copy-done.4
  83.4 0.2 copy-done.5
  83.6 23.7 %shard_map.119 = (bf16[2,2,1024,1536]{3,2,1,0:T(8,128)(2,1)}, f32[2,32,128]{2,1,0:T(8,128)}, bf16[2,1536,512]{2,1,0:T(8,128)(2,1)}, bf16[8,32,2816]{2,1,0:T(8,128)(2,1)}) custom-call(s32[8]{0:T(128)} %and_select_fusion.refs_0_, bf16[256,9216]{1,0:T(8,128)(2,1)} %refs_1_.1, bf16[2,96,1152]{2,1,0:T(8,128)(2,1)} %shard_map.117.refs_2_, ...), custom_call_target="tpu_custom_call" | custom-call | tf_op jit(solution)/shard_map/pallas_call | solution.py:409
  107.3 3.8 %all-to-all-start.3 = ((bf16[8,32,2816]{2,1,0:T(8,128)(2,1)}), bf16[8,32,2816]{2,1,0:T(8,128)(2,1)S(1)}, u32[]{:S(2)}, u32[]{:S(2)}) async-start(bf16[8,32,2816]{2,1,0:T(8,128)(2,1)} %get-tuple-element.38), calls=%async_computation.3 | async-start | bytes 2883584 | tf_op jit(solution)/shard_map/all_to_all | solution.py:569
  111.1 0.1 add.117
  111.1 0.1 add.118
  111.2 0.1 broadcast_add_fusion
  111.3 0.9 compare_select_fusion.bias_own
  112.2 14.5 %shard_map.120 = bf16[256,8192]{1,0:T(8,128)(2,1)} custom-call(f32[2,32,128]{2,1,0:T(8,128)} %get-tuple-element.39.f_ref, bf16[2,2,1024,512]{3,2,1,0:T(8,128)(2,1)} %get-tuple-element.31.refs_11_.po_ref, bf16[2,2,1024,1536]{3,2,1,0:T(8,128)(2,1)} %get-tuple-element.40.pr_ref, bf16[2,512,512]{2,1,0:T(8,128)(2,1)} %get-tuple-element.41.vo_ref, ...), custom_call_target="tpu_custom_call" | custom-call | tf_op jit(solution)/shard_map/pallas_call | solution.py:455
  126.7 3.4 %all-to-all-done.3.part_ref = bf16[8,32,2816]{2,1,0:T(8,128)(2,1)S(1)} async-done(((bf16[8,32,2816]{2,1,0:T(8,128)(2,1)}), bf16[8,32,2816]{2,1,0:T(8,128)(2,1)S(1)}, u32[]{:S(2)}, u32[]{:S(2)}) %all-to-all-start.3) | async-done | bytes 1441824 | tf_op jit(solution)/shard_map/all_to_all | solution.py:569
  130.1 9.0 %shard_map.121 = (f32[1,32]{1,0:T(1,128)}, f32[32,8192]{1,0:T(8,128)}) custom-call(s32[1]{0:T(128)} %bitcast.h_ref, bf16[32,8192]{1,0:T(8,128)(2,1)} %iq_ref.1, f32[32,64]{1,0:T(8,128)} %w_ref.1, bf16[2,512,128]{2,1,0:T(8,128)(2,1)} %bitcast.16, bf16[8,32,2816]{2,1,0:T(8,128)(2,1)S(1)} %all-to-all-done.3.part_ref, ...), custom_call_target="tpu_custom_call" | custom-call | tf_op jit(solution)/shard_map/pallas_call | solution.py:529
  (11 shorter events, 0.1 us)
Async XLA Ops:
  2.4 16.2 %all-to-all-start = ((s32[16,16,128]{2,1,0:T(8,128)}), s32[16,16,128]{2,1,0:T(8,128)S(1)}, u32[]{:S(2)}, u32[]{:S(2)}) async-start(s32[16,16,128]{2,1,0:T(8,128)} %bitcast.17), calls=%async_computation | async-start | bytes 262144 | tf_op jit(solution)/shard_map/all_to_all | solution.py:569
  21.6 3.9 %copy-start.7 = (s32[16]{0:T(128)S(1)}, s32[16]{0:T(128)}, u32[]{:S(2)}) copy-start(s32[16]{0:T(128)} %get-tuple-element.29.idx_ref) | copy-start | bytes 196
  21.6 4.1 %copy-start.6 = (s32[48]{0:T(128)S(1)}, s32[48]{0:T(128)}, u32[]{:S(2)}) copy-start(s32[48]{0:T(128)} %get-tuple-element.26.idx_ref) | copy-start | bytes 580
  21.6 4.3 %copy-start.8 = (s32[4]{0:T(128)S(1)}, s32[4]{0:T(128)}, u32[]{:S(2)}) copy-start(s32[4]{0:T(128)} %constant.85) | copy-start | bytes 52
  21.6 4.9 %copy-start.9 = (s32[2]{0:T(128)S(1)}, s32[2]{0:T(128)}, u32[]{:S(2)}) copy-start(s32[2]{0:T(128)} %param.16) | copy-start | bytes 28
  21.6 32.0 %all-to-all-start.1 = ((bf16[16,16,4608]{2,1,0:T(8,128)(2,1)}), bf16[16,16,4608]{2,1,0:T(8,128)(2,1)S(1)}, u32[]{:S(2)}, u32[]{:S(2)}) async-start(bf16[16,16,4608]{2,1,0:T(8,128)(2,1)} %bitcast.15), calls=%async_computation.1 | async-start | bytes 4718592 | tf_op jit(solution)/shard_map/all_to_all | solution.py:569
  56.2 14.8 %collective-permute-start = (bf16[2,96,1152]{2,1,0:T(8,128)(2,1)}, bf16[2,96,1152]{2,1,0:T(8,128)(2,1)S(1)}, u32[]{:S(2)}, u32[]{:S(2)}) collective-permute-start(bf16[2,96,1152]{2,1,0:T(8,128)(2,1)} %shard_map.117.refs_2_), channel_id=1, source_target_pairs={{0,2},{1,3},{2,4},{3,5},{4,6},{5,7},{6,0},{7,1},{8,10},{9,11},{10,... | collective-permute-start | bytes 1327112 | tf_op jit(solution)/shard_map/ppermute | solution.py:559
  57.5 18.7 %collective-permute-start.1 = (bf16[2,96,1152]{2,1,0:T(8,128)(2,1)}, bf16[2,96,1152]{2,1,0:T(8,128)(2,1)S(1)}, u32[]{:S(2)}, u32[]{:S(2)}) collective-permute-start(bf16[2,96,1152]{2,1,0:T(8,128)(2,1)} %shard_map.117.refs_2_), channel_id=1, source_target_pairs={{0,6},{1,7},{2,0},{3,1},{4,2},{5,3},{6,4},{7,5},{8,14},{9,15},{10,... | collective-permute-start | bytes 1327112 | tf_op jit(solution)/shard_map/ppermute | solution.py:559
  59.0 17.3 %collective-permute-start.2 = (bf16[2,96,1152]{2,1,0:T(8,128)(2,1)}, bf16[2,96,1152]{2,1,0:T(8,128)(2,1)S(1)}, u32[]{:S(2)}, u32[]{:S(2)}) collective-permute-start(bf16[2,96,1152]{2,1,0:T(8,128)(2,1)} %shard_map.117.refs_2_), channel_id=1, source_target_pairs={{0,4},{1,5},{2,6},{3,7},{4,0},{5,1},{6,2},{7,3},{8,12},{9,13},{10,... | collective-permute-start | bytes 1327112 | tf_op jit(solution)/shard_map/ppermute | solution.py:559
  60.6 20.4 %all-to-all-start.2 = ((bf16[16,16,1024]{2,1,0:T(8,128)(2,1)}), bf16[16,16,1024]{2,1,0:T(8,128)(2,1)S(1)}, u32[]{:S(2)}, u32[]{:S(2)}) async-start(bf16[16,16,1024]{2,1,0:T(8,128)(2,1)} %bitcast.6), calls=%async_computation.2 | async-start | bytes 1048576 | tf_op jit(solution)/shard_map/all_to_all | solution.py:569
  66.3 16.2 %collective-permute-start.3 = (bf16[2,96,1152]{2,1,0:T(8,128)(2,1)}, bf16[2,96,1152]{2,1,0:T(8,128)(2,1)S(1)}, u32[]{:S(2)}, u32[]{:S(2)}) collective-permute-start(bf16[2,96,1152]{2,1,0:T(8,128)(2,1)} %shard_map.117.refs_2_), channel_id=1, source_target_pairs={{0,1},{1,0},{2,3},{3,2},{4,5},{5,4},{6,7},{7,6},{8,9},{9,8},{10,11... | collective-permute-start | bytes 1327112 | tf_op jit(solution)/shard_map/ppermute | solution.py:560
  71.0 11.6 %copy-start = (bf16[2,96,1152]{2,1,0:T(8,128)(2,1)}, bf16[2,96,1152]{2,1,0:T(8,128)(2,1)S(1)}, u32[]{:S(2)}) copy-start(bf16[2,96,1152]{2,1,0:T(8,128)(2,1)S(1)} %collective-permute-done.refs_3_) | copy-start | bytes 1327108
  71.0 11.5 %collective-permute-start.4 = (bf16[2,96,1152]{2,1,0:T(8,128)(2,1)S(1)}, bf16[2,96,1152]{2,1,0:T(8,128)(2,1)S(1)}, u32[]{:S(2)}, u32[]{:S(2)}) collective-permute-start(bf16[2,96,1152]{2,1,0:T(8,128)(2,1)S(1)} %collective-permute-done.refs_3_), channel_id=1, source_target_pairs={{0,1},{1,0},{2,3},{3,2},{4,5},{5,4},{6,7},{7,6},{8,9},{9,8},{10,11... | collective-permute-start | bytes 1327112 | tf_op jit(solution)/shard_map/ppermute | solution.py:560
  76.2 6.4 %copy-start.1 = (bf16[2,96,1152]{2,1,0:T(8,128)(2,1)}, bf16[2,96,1152]{2,1,0:T(8,128)(2,1)S(1)}, u32[]{:S(2)}) copy-start(bf16[2,96,1152]{2,1,0:T(8,128)(2,1)S(1)} %collective-permute-done.1.refs_4_) | copy-start | bytes 1327108
  76.2 6.4 %collective-permute-start.5 = (bf16[2,96,1152]{2,1,0:T(8,128)(2,1)S(1)}, bf16[2,96,1152]{2,1,0:T(8,128)(2,1)S(1)}, u32[]{:S(2)}, u32[]{:S(2)}) collective-permute-start(bf16[2,96,1152]{2,1,0:T(8,128)(2,1)S(1)} %collective-permute-done.1.refs_4_), channel_id=1, source_target_pairs={{0,1},{1,0},{2,3},{3,2},{4,5},{5,4},{6,7},{7,6},{8,9},{9,8},{10,11... | collective-permute-start | bytes 1327112 | tf_op jit(solution)/shard_map/ppermute | solution.py:560
  76.3 6.3 %copy-start.2 = (bf16[2,96,1152]{2,1,0:T(8,128)(2,1)}, bf16[2,96,1152]{2,1,0:T(8,128)(2,1)S(1)}, u32[]{:S(2)}) copy-start(bf16[2,96,1152]{2,1,0:T(8,128)(2,1)S(1)} %collective-permute-done.2.refs_5_) | copy-start | bytes 1327108
  76.3 6.3 %collective-permute-start.6 = (bf16[2,96,1152]{2,1,0:T(8,128)(2,1)S(1)}, bf16[2,96,1152]{2,1,0:T(8,128)(2,1)}, u32[]{:S(2)}, u32[]{:S(2)}) collective-permute-start(bf16[2,96,1152]{2,1,0:T(8,128)(2,1)S(1)} %collective-permute-done.2.refs_5_), channel_id=1, source_target_pairs={{0,1},{1,0},{2,3},{3,2},{4,5},{5,4},{6,7},{7,6},{8,9},{9,8},{10,11... | collective-permute-start | bytes 1327112 | tf_op jit(solution)/shard_map/ppermute | solution.py:560
  82.5 0.8 copy-start.3
  82.5 0.9 copy-start.4
  82.5 1.1 copy-start.5
  107.3 22.8 %all-to-all-start.3 = ((bf16[8,32,2816]{2,1,0:T(8,128)(2,1)}), bf16[8,32,2816]{2,1,0:T(8,128)(2,1)S(1)}, u32[]{:S(2)}, u32[]{:S(2)}) async-start(bf16[8,32,2816]{2,1,0:T(8,128)(2,1)} %get-tuple-element.38), calls=%async_computation.3 | async-start | bytes 2883584 | tf_op jit(solution)/shard_map/all_to_all | solution.py:569
